TPU v7x, 128 devices: a whole 4x4x4 slice. The times are simulated.
128 devices in a mesh: grp: 8 (over x, core), tp: 16 (over y, z).
Axes of the slice: x: 4, y: 4, z: 4, core: 2. Of those that a mesh axis runs over, the one named last changes fastest.
Arguments:
- tokens: bfloat16 [12288, 8192], P(('grp', 'tp')), may hold values from -6 to 6
- holder: int32 [12288, 1], P(('grp', 'tp')), may hold values from 0 to 127; in each aligned block of 96 rows (0 to 95, 96 to 191, ...) at most 2 rows name the same one
- adapter_choice_index: int32 [12288, 1], P(('grp', 'tp')), may hold values from 0 to 1
- query_base_output: bfloat16 [8192, 8192], P(None, 'tp'), may hold values from -0.0625 to 0.0625
- value_base_output: bfloat16 [8192, 1024], P(None, 'tp'), may hold values from -0.0625 to 0.0625
- adapter_down_weight: bfloat16 [256, 8192, 128], P(('grp', 'tp')), may hold values from -0.0625 to 0.0625
- adapter_query_up: bfloat16 [256, 64, 8192], P(('grp', 'tp')), may hold values from -0.75 to 0.75
- adapter_value_up: bfloat16 [256, 64, 1024], P(('grp', 'tp')), may hold values from -0.75 to 0.75
Outputs:
- queries: bfloat16 [12288, 8192], P(('grp', 'tp'))
- values: bfloat16 [12288, 1024], P(('grp', 'tp'))
Inputs may be any that keep to these rules, and one draw needn't show every extreme that they name: Among the 96 requests of one device no holder appears more than 2 times, and some holder appears exactly 2 times.
All inputs are finite; a program needn't handle non-finite values.
Results may differ from a plain program's by a relative error of at most 0.0057.
Values may be sent and summed in bfloat16 or wider, within the bound.
No kernel may reach another device: no remote copies, remote signals or barrier semaphores. Data moves between devices by JAX's collectives and lax.ppermute only.
A program may use at most 128 MiB of HBM per device.

v0:
```python
import jax
import jax.numpy as jnp
from jax import lax
from jax.experimental import pallas as pl
from jax.experimental.pallas import tpu as pltpu
from jax.sharding import PartitionSpec as P

adapter_scale = 2.0
BF = jnp.bfloat16
F32 = jnp.float32
side = 4


def shift(x, dy, dz):
    pairs = [
        (y * side + z, (y + dy) % side * side + (z + dz) % side)
        for y in range(side)
        for z in range(side)
    ]
    return lax.ppermute(x, "tp", pairs)


def line_gather(x, step):
    back = (-step[0], -step[1])
    half = x.shape[0] // 2
    before = shift(x, *step)
    after = shift(x, *back)
    far_low = shift(before[:half], *step)
    far_high = shift(after[half:], *back)
    return after, (far_low, far_high), before


def to_absolute(blocks, place):
    for bit in (1, 2):
        moved = jnp.roll(blocks, bit, axis=0)
        blocks = jnp.where((place & bit) != 0, moved, blocks)
    return blocks


def apply_lowrank_adapters(rows, choice, adapter_down_weight, adapter_query_up, adapter_value_up):
    rank = adapter_query_up.shape[1]
    count = adapter_down_weight.shape[0]
    query_parts, value_parts = [], []
    for i in range(count):
        reduced = jnp.dot(rows, adapter_down_weight[i], preferred_element_type=F32)
        reduced = jnp.where(choice == i, reduced, 0.0).astype(BF)
        query_parts.append(reduced[:, :rank])
        value_parts.append(reduced[:, rank:])
    query_low = jnp.concatenate(query_parts, axis=1)
    value_low = jnp.concatenate(value_parts, axis=1)
    query_up = adapter_query_up.reshape(count * rank, adapter_query_up.shape[2])
    value_up = adapter_value_up.reshape(count * rank, adapter_value_up.shape[2])
    query = (adapter_scale * jnp.dot(query_low, query_up, preferred_element_type=F32)).astype(BF)
    value = (adapter_scale * jnp.dot(value_low, value_up, preferred_element_type=F32)).astype(BF)
    return query, value


def finish_kernel(slot_ref, plain_ref, query_ref, value_ref, queries_ref, values_ref):
    rows, query_cols = plain_ref.shape[1], queries_ref.shape[1] // 2
    slots = query_ref.shape[0]
    pick = (lax.broadcasted_iota(jnp.int32, (rows, slots), 1) == slot_ref[...]).astype(BF)
    term = jnp.dot(pick, query_ref[...], preferred_element_type=F32)
    for i in range(2):
        cols = pl.ds(i * query_cols, query_cols)
        base = plain_ref[i, :, :query_cols].astype(F32)
        queries_ref[:, cols] = (base + term[:, i * query_cols : (i + 1) * query_cols]).astype(BF)
    term = jnp.dot(pick, value_ref[...], preferred_element_type=F32)
    base = jnp.concatenate([plain_ref[0, :, query_cols:], plain_ref[1, :, query_cols:]], axis=1)
    values_ref[...] = (base.astype(F32) + term).astype(BF)


def finish(slot_index, plain, terms, query_cols, value_cols):
    members, rows, both = plain.shape
    slots = terms.shape[0]
    value_at = members * query_cols // (2 * value_cols)
    return pl.pallas_call(
        finish_kernel,
        grid=(members // 2,),
        in_specs=[
            pl.BlockSpec((rows, 1), lambda i: (0, 0)),
            pl.BlockSpec((2, rows, both), lambda i: (i, 0, 0)),
            pl.BlockSpec((slots, 2 * query_cols), lambda i: (0, i)),
            pl.BlockSpec((slots, 2 * value_cols), lambda i: (0, value_at + i)),
        ],
        out_specs=[
            pl.BlockSpec((rows, 2 * query_cols), lambda i: (0, i)),
            pl.BlockSpec((rows, 2 * value_cols), lambda i: (0, i)),
        ],
        out_shape=[
            jax.ShapeDtypeStruct((rows, members * query_cols), BF),
            jax.ShapeDtypeStruct((rows, members * value_cols), BF),
        ],
        compiler_params=pltpu.CompilerParams(vmem_limit_bytes=24 << 20),
        cost_estimate=pl.CostEstimate(
            flops=2 * rows * slots * members * (query_cols + value_cols),
            bytes_accessed=2 * (slots + 2 * rows) * members * (query_cols + value_cols),
            transcendentals=0,
        ),
    )(slot_index[:, None], plain, terms, terms)


def on_device(
    tokens,
    holder,
    adapter_choice_index,
    query_base_output,
    value_base_output,
    adapter_down_weight,
    adapter_query_up,
    adapter_value_up,
):
    row_count, width = tokens.shape
    query_cols = query_base_output.shape[1]
    value_cols = value_base_output.shape[1]
    both = query_cols + value_cols
    members = lax.axis_size("tp")
    devices = lax.axis_size("grp") * members
    capacity = 2
    slot_total = devices * capacity
    place = lax.axis_index("tp")

    holder_id = holder[:, 0]
    same_holder = holder_id[:, None] == holder_id[None, :]
    index = jnp.arange(row_count, dtype=jnp.int32)
    earlier = index[:, None] > index[None, :]
    position = jnp.sum((same_holder & earlier).astype(jnp.int32), axis=1)
    slot_index = holder_id * capacity + position
    pick_table = (jnp.arange(slot_total, dtype=jnp.int32)[:, None] == slot_index[None, :]).astype(BF)
    marked = jnp.concatenate(
        [tokens, jnp.broadcast_to(adapter_choice_index.astype(BF), (row_count, 128))], axis=1
    )
    send_rows = jnp.dot(pick_table, marked, preferred_element_type=F32).astype(BF)
    send_rows = send_rows.reshape(devices, capacity, width + 128)

    half = width // 2
    along_z, along_y = (0, 1), (1, 0)
    weights = jnp.concatenate([query_base_output, value_base_output], axis=1)
    lines = []
    for part, step in ((0, along_z), (1, along_y)):
        own = tokens[:, part * half : (part + 1) * half]
        after, far, before = line_gather(own, step)
        lines.append(jnp.concatenate([own, after, *far, before], axis=0))
    lines[0], lines[1], send_rows = lax.optimization_barrier((lines[0], lines[1], send_rows))
    got_rows = lax.all_to_all(
        send_rows, ("grp", "tp"), split_axis=0, concat_axis=0, tiled=True
    ).reshape(slot_total, width + 128)
    query_term, value_term = apply_lowrank_adapters(
        got_rows[:, :width],
        got_rows[:, width : width + 1],
        adapter_down_weight,
        adapter_query_up,
        adapter_value_up,
    )
    terms = jnp.concatenate([query_term, value_term], axis=1)
    back = lax.all_to_all(
        terms.reshape(devices, capacity, terms.shape[1]),
        ("grp", "tp"),
        split_axis=0,
        concat_axis=0,
        tiled=True,
    ).reshape(slot_total, terms.shape[1])

    gathered = []
    for line, step in zip(lines, (along_y, along_z)):
        after, far, before = line_gather(line, step)
        gathered.append([line, after, jnp.concatenate(far, axis=0), before])
    gathered[1][3], back = lax.optimization_barrier((gathered[1][3], back))
    partial = []
    for part in range(2):
        w = weights[part * half : (part + 1) * half]
        partial.append(
            jnp.stack(
                [
                    jnp.dot(x, w, preferred_element_type=F32).reshape(side, row_count, both)
                    for x in gathered[part]
                ]
            )
        )
    projected = (partial[0] + jnp.swapaxes(partial[1], 0, 1)).astype(BF)
    projected = to_absolute(projected, place // side)
    projected = jnp.swapaxes(to_absolute(jnp.swapaxes(projected, 0, 1), place % side), 0, 1)
    plain = lax.all_to_all(
        projected.reshape(members, row_count, both), "tp", split_axis=0, concat_axis=0, tiled=True
    )
    queries, values = finish(slot_index, plain, back, query_cols, value_cols)
    return (queries, values)


def solution(mesh):
    return jax.shard_map(
        on_device,
        mesh=mesh,
        in_specs=(
            P(("grp", "tp"), None),
            P(("grp", "tp"), None),
            P(("grp", "tp"), None),
            P(None, "tp"),
            P(None, "tp"),
            P(("grp", "tp"), None, None),
            P(("grp", "tp"), None, None),
            P(("grp", "tp"), None, None),
        ),
        out_specs=(P(("grp", "tp"), None), P(("grp", "tp"), None)),
        check_vma=False,
    )
```

profile of v0, /device:TPU:6, one launch (start us, length us, event | category | flops | bytes accessed | tf_op | source)
XLA Modules:
  0.0 327.7 jit_solution(3707267409718004828)
XLA Ops:
  0.7 3.4 %fusion.59 = (bf16[96,4096]{1,0:T(8,128)(2,1)}, bf16[384,4096]{1,0:T(8,128)(2,1)}, bf16[384,4096]{1,0:T(8,128)(2,1)}, bf16[96,4096]{1,0:T(8,128)(2,1)}) fusion(bf16[96,8192]{1,0:T(8,128)(2,1)} %param.8), kind=kLoop, calls=%fused_computation.74 | loop fusion | bytes 4718592 | tf_op jit(solution)/shard_map/slice | solution.py:140
  4.1 4.0 %collective-permute-start = (bf16[96,4096]{1,0:T(8,128)(2,1)}, bf16[96,4096]{1,0:T(8,128)(2,1)}, u32[]{:S(2)}, u32[]{:S(2)}) collective-permute-start(bf16[96,4096]{1,0:T(8,128)(2,1)} %get-tuple-element.23), channel_id=1, source_target_pairs={{0,3},{1,0},{2,1},{3,2},{4,7},{5,4},{6,5},{7,6},{8,11},{9,8},{10,9... | collective-permute-start | bytes 2359304 | tf_op jit(solution)/shard_map/ppermute | solution.py:20
  8.1 3.0 collective-permute-start.4
  11.4 3.2 convolution_convert_fusion
  14.7 7.2 %reshape.35 = bf16[128,2,8320]{2,1,0:T(2,128)(2,1)} reshape(bf16[256,8320]{1,0:T(8,128)(2,1)} %convolution_convert_fusion) | data formatting | bytes 8519680 | tf_op jit(solution)/shard_map/reshape | solution.py:133
  21.9 6.7 %collective-permute-done.1 = bf16[96,4096]{1,0:T(8,128)(2,1)} collective-permute-done((bf16[96,4096]{1,0:T(8,128)(2,1)}, bf16[96,4096]{1,0:T(8,128)(2,1)}, u32[]{:S(2)}, u32[]{:S(2)}) %collective-permute-start.1) | collective-permute-done | bytes 786464 | tf_op jit(solution)/shard_map/ppermute | solution.py:20
  28.6 1.0 slice.116
  29.8 1.0 slice.117
  30.8 3.3 %collective-permute-start.3 = (bf16[48,4096]{1,0:T(8,128)(2,1)S(1)}, bf16[48,4096]{1,0:T(8,128)(2,1)S(1)}, u32[]{:S(2)}, u32[]{:S(2)}) collective-permute-start(bf16[48,4096]{1,0:T(8,128)(2,1)S(1)} %slice.117), channel_id=1, source_target_pairs={{0,3},{1,0},{2,1},{3,2},{4,7},{5,4},{6,5},{7,6},{8,11},{9,8},{10,9... | collective-permute-start | bytes 1179656 | tf_op jit(solution)/shard_map/ppermute | solution.py:20
  34.1 1.6 collective-permute-start.6
  35.7 1.0 slice.119
  36.8 1.7 collective-permute-start.7
  38.5 2.1 constant_dynamic-update-slice_fusion.3
  40.6 2.1 constant_dynamic-update-slice_fusion.8
  42.7 0.8 constant_dynamic-update-slice_fusion.2
  43.5 0.8 constant_dynamic-update-slice_fusion.1
  44.3 2.1 constant_dynamic-update-slice_fusion
  46.3 0.8 constant_dynamic-update-slice_fusion.7
  47.1 0.8 constant_dynamic-update-slice_fusion.6
  47.9 0.9 constant_dynamic-update-slice_fusion.5
  48.9 8.0 %all-to-all-start = ((bf16[128,2,8320]{2,1,0:T(2,128)(2,1)}), bf16[128,2,8320]{2,1,0:T(2,128)(2,1)}, u32[]{:S(2)}, u32[]{:S(2)}) async-start(bf16[128,2,8320]{2,1,0:T(2,128)(2,1)} %reshape.35), calls=%async_computation | async-start | bytes 8519680 | tf_op jit(solution)/shard_map/all_to_all | solution.py:144
  56.9 1.8 copy.71
  58.7 9.1 %pad_maximum_fusion = (bf16[4096,576]{1,0:T(8,128)(2,1)}, bf16[4096,576]{1,0:T(8,128)(2,1)}) fusion(bf16[8192,64]{1,0:T(8,128)(2,1)} %copy.71, bf16[8192,512]{1,0:T(8,128)(2,1)} %param.11), kind=kLoop, calls=%fused_computation.6 | loop fusion | flops 18874368 | bytes 18874368 | tf_op jit(solution)/shard_map/concatenate | solution.py:137
  67.8 1.5 collective-permute-start.9
  69.3 1.8 collective-permute-start.8
  71.0 1.6 collective-permute-start.13
  72.7 1.8 collective-permute-start.12
  74.4 36.4 %all-to-all-done = bf16[128,2,8320]{2,1,0:T(2,128)(2,1)} async-done(((bf16[128,2,8320]{2,1,0:T(2,128)(2,1)}), bf16[128,2,8320]{2,1,0:T(2,128)(2,1)}, u32[]{:S(2)}, u32[]{:S(2)}) %all-to-all-start) | async-done | bytes 4259872 | tf_op jit(solution)/shard_map/all_to_all | solution.py:144
  110.8 7.2 %reshape.36 = bf16[256,8320]{1,0:T(8,128)(2,1)} reshape(bf16[128,2,8320]{2,1,0:T(2,128)(2,1)} %all-to-all-done) | data formatting | bytes 8519680 | tf_op jit(solution)/shard_map/reshape | solution.py:146
  118.1 1.0 compare_reduce_fusion.1
  119.1 4.5 %fusion.29 = bf16[256,128]{0,1:T(8,128)(2,1)S(1)} fusion(bf16[2,8192,128]{2,1,0:T(8,128)(2,1)} %param.13, bf16[256,8320]{1,0:T(8,128)(2,1)} %reshape.36, pred[256]{0:T(512)(128)(4,1)S(1)} %get-tuple-element.12), kind=kOutput, calls=%fused_computation.38 | convolution fusion | flops 536936448 | bytes 6357248 | tf_op jit(solution)/shard_map/dot_general | solution.py:45
  123.6 3.2 fusion.39
  126.8 0.3 fusion.23
  127.2 1.3 fusion
  128.5 2.5 pad_maximum_fusion.1
  131.0 7.6 %reshape.39 = bf16[128,2,9216]{2,1,0:T(2,128)(2,1)} reshape(bf16[256,9216]{1,0:T(8,128)(2,1)} %pad_maximum_fusion.1) | data formatting | bytes 9437184 | tf_op jit(solution)/shard_map/reshape | solution.py:156
  138.5 5.2 %all-to-all-start.1 = ((bf16[128,2,9216]{2,1,0:T(2,128)(2,1)}), bf16[128,2,9216]{2,1,0:T(2,128)(2,1)}, u32[]{:S(2)}, u32[]{:S(2)}) async-start(bf16[128,2,9216]{2,1,0:T(2,128)(2,1)} %reshape.39), calls=%async_computation.1 | async-start | bytes 9437184 | tf_op jit(solution)/shard_map/all_to_all | solution.py:155
  143.8 7.1 %fusion.62 = f32[384,576]{1,0:T(8,128)} fusion(bf16[384,4096]{1,0:T(8,128)(2,1)} %constant_dynamic-update-slice_fusion, bf16[4096,576]{1,0:T(8,128)(2,1)} %get-tuple-element.15), kind=kOutput, calls=%fused_computation.77 | convolution fusion | flops 1811939328 | bytes 8749056 | tf_op jit(solution)/shard_map/dot_general | solution.py:174
  150.9 5.5 %fusion.65 = f32[384,576]{1,0:T(8,128)} fusion(bf16[384,4096]{1,0:T(8,128)(2,1)} %constant_dynamic-update-slice_fusion.5, bf16[4096,576]{1,0:T(8,128)(2,1)S(1)} %bitcast.68), kind=kOutput, calls=%fused_computation.80 | convolution fusion | flops 1811939328 | bytes 8749056 | tf_op jit(solution)/shard_map/dot_general | solution.py:174
  156.4 55.5 %collective-permute-done.8 = bf16[384,4096]{1,0:T(8,128)(2,1)} collective-permute-done((bf16[384,4096]{1,0:T(8,128)(2,1)}, bf16[384,4096]{1,0:T(8,128)(2,1)}, u32[]{:S(2)}, u32[]{:S(2)}) %collective-permute-start.8) | collective-permute-done | bytes 3145760 | tf_op jit(solution)/shard_map/ppermute | solution.py:20
  212.0 1.5 slice.123
  213.5 1.9 collective-permute-start.11
  215.4 1.5 slice.122
  216.9 0.3 collective-permute-start.10
  217.2 1.5 slice.125
  218.8 3.7 %collective-permute-start.15 = (bf16[192,4096]{1,0:T(8,128)(2,1)S(1)}, bf16[192,4096]{1,0:T(8,128)(2,1)S(1)}, u32[]{:S(2)}, u32[]{:S(2)}) collective-permute-start(bf16[192,4096]{1,0:T(8,128)(2,1)S(1)} %slice.125), channel_id=1, source_target_pairs={{0,3},{1,0},{2,1},{3,2},{4,7},{5,4},{6,5},{7,6},{8,11},{9,8},{10,9... | collective-permute-start | bytes 4718600 | tf_op jit(solution)/shard_map/ppermute | solution.py:20
  222.4 1.5 slice.124
  224.3 5.5 %fusion.64 = f32[384,576]{1,0:T(8,128)} fusion(bf16[384,4096]{1,0:T(8,128)(2,1)} %collective-permute-done.9, bf16[4096,576]{1,0:T(8,128)(2,1)S(1)} %bitcast.70), kind=kOutput, calls=%fused_computation.79 | convolution fusion | flops 1811939328 | bytes 8749056 | tf_op jit(solution)/shard_map/dot_general | solution.py:174
  229.8 5.5 %fusion.63 = f32[384,576]{1,0:T(8,128)} fusion(bf16[384,4096]{1,0:T(8,128)(2,1)} %collective-permute-done.8, bf16[4096,576]{1,0:T(8,128)(2,1)S(1)} %bitcast.70), kind=kOutput, calls=%fused_computation.78 | convolution fusion | flops 1811939328 | bytes 8749056 | tf_op jit(solution)/shard_map/dot_general | solution.py:174
  235.3 5.4 %fusion.66 = f32[384,576]{1,0:T(8,128)} fusion(bf16[384,4096]{1,0:T(8,128)(2,1)} %collective-permute-done.12, bf16[4096,576]{1,0:T(8,128)(2,1)S(1)} %bitcast.68), kind=kOutput, calls=%fused_computation.81 | convolution fusion | flops 1811939328 | bytes 8749056 | tf_op jit(solution)/shard_map/dot_general | solution.py:174
  240.7 17.4 %collective-permute-done.11 = bf16[192,4096]{1,0:T(8,128)(2,1)S(1)} collective-permute-done((bf16[192,4096]{1,0:T(8,128)(2,1)S(1)}, bf16[192,4096]{1,0:T(8,128)(2,1)S(1)}, u32[]{:S(2)}, u32[]{:S(2)}) %collective-permute-start.11) | collective-permute-done | bytes 1572896 | tf_op jit(solution)/shard_map/ppermute | solution.py:20
  258.1 3.7 %fusion.7 = f32[384,576]{1,0:T(8,128)} fusion(bf16[4096,576]{1,0:T(8,128)(2,1)S(1)} %bitcast.70, bf16[192,4096]{1,0:T(8,128)(2,1)S(1)} %collective-permute-done.11, bf16[192,4096]{1,0:T(8,128)(2,1)S(1)} %collective-permute-done.10), kind=kOutput, calls=%fused_computation.15 | convolution fusion | flops 1818230784 | bytes 8749056 | tf_op jit(solution)/shard_map/dot_general | solution.py:174
  261.8 3.7 %fusion.11 = f32[384,576]{1,0:T(8,128)} fusion(bf16[4096,576]{1,0:T(8,128)(2,1)S(1)} %bitcast.68, bf16[192,4096]{1,0:T(8,128)(2,1)S(1)} %collective-permute-done.15, bf16[192,4096]{1,0:T(8,128)(2,1)S(1)} %collective-permute-done.14), kind=kOutput, calls=%fused_computation.19 | convolution fusion | flops 1818230784 | bytes 8749056 | tf_op jit(solution)/shard_map/dot_general | solution.py:174
  265.5 7.6 %reshape.40.query_ref.value_ref = bf16[256,9216]{1,0:T(8,128)(2,1)} reshape(bf16[128,2,9216]{2,1,0:T(2,128)(2,1)} %all-to-all-done.1) | data formatting | bytes 9437184 | tf_op jit(solution)/shard_map/reshape | solution.py:161
  273.1 6.2 %fusion.67 = f32[384,576]{1,0:T(8,128)S(1)} fusion(bf16[384,4096]{1,0:T(8,128)(2,1)} %collective-permute-done.13, bf16[4096,576]{1,0:T(8,128)(2,1)} %get-tuple-element.14), kind=kOutput, calls=%fused_computation.82 | convolution fusion | flops 1811939328 | bytes 8749056 | tf_op jit(solution)/shard_map/dot_general | solution.py:174
  279.3 0.6 fusion.2
  280.1 1.0 maximum_select_fusion
  281.3 0.3 fusion.19
  281.9 0.3 maximum_select_fusion.2
  282.4 1.6 maximum_select_fusion.3
  284.0 6.5 %all-to-all-start.2 = ((bf16[16,96,576]{2,1,0:T(8,128)(2,1)}), bf16[16,96,576]{2,1,0:T(8,128)(2,1)}, u32[]{:S(2)}, u32[]{:S(2)}) async-start(bf16[16,96,576]{2,1,0:T(8,128)(2,1)} %bitcast.66), calls=%async_computation.2 | async-start | bytes 3932160 | tf_op jit(solution)/shard_map/all_to_all | solution.py:182
  290.6 28.2 %all-to-all-done.2.plain_ref = bf16[16,96,576]{2,1,0:T(8,128)(2,1)} async-done(((bf16[16,96,576]{2,1,0:T(8,128)(2,1)}), bf16[16,96,576]{2,1,0:T(8,128)(2,1)}, u32[]{:S(2)}, u32[]{:S(2)}) %all-to-all-start.2) | async-done | bytes 1769504 | tf_op jit(solution)/shard_map/all_to_all | solution.py:182
  318.9 2.3 copy-done.2
  321.2 6.5 %shard_map.95 = (bf16[96,8192]{1,0:T(8,128)(2,1)}, bf16[96,1024]{1,0:T(8,128)(2,1)}) custom-call(s32[96,1]{1,0:T(8,128)S(1)} %copy.84.slot_ref, bf16[16,96,576]{2,1,0:T(8,128)(2,1)} %all-to-all-done.2.plain_ref, bf16[256,9216]{1,0:T(8,128)(2,1)S(1)} %copy-done.2, bf16[256,9216]{1,0:T(8,128)(2,1)S(1)} %copy-done.2), custom_call_target="tpu_custom_call" | custom-call | flops 452984832 | bytes 8257536 | tf_op jit(solution)/shard_map/pallas_call | solution.py:76
  (73 shorter events, 1.6 us)
Async XLA Ops:
  0.6 126.5 %copy-start = (bf16[2,64,8192]{2,1,0:T(8,128)(2,1)S(1)}, bf16[2,64,8192]{2,1,0:T(8,128)(2,1)}, u32[]{:S(2)}) copy-start(bf16[2,64,8192]{2,1,0:T(8,128)(2,1)} %param.14) | copy-start | bytes 6291460
  0.6 10.8 %copy-start.3 = (bf16[96,8192]{1,0:T(8,128)(2,1)S(1)}, bf16[96,8192]{1,0:T(8,128)(2,1)}, u32[]{:S(2)}) copy-start(bf16[96,8192]{1,0:T(8,128)(2,1)} %param.8) | copy-start | bytes 4718596
  0.7 10.5 %copy-start.15 = (s32[96,1]{0,1:T(1,128)S(1)}, s32[96,1]{0,1:T(1,128)}, u32[]{:S(2)}) copy-start(s32[96,1]{0,1:T(1,128)} %param.9) | copy-start | bytes 1156
  0.7 10.6 %copy-start.14 = (s32[96,1]{0,1:T(1,128)S(1)}, s32[96,1]{0,1:T(1,128)}, u32[]{:S(2)}) copy-start(s32[96,1]{0,1:T(1,128)} %param.10) | copy-start | bytes 1156
  4.1 25.7 %collective-permute-start = (bf16[96,4096]{1,0:T(8,128)(2,1)}, bf16[96,4096]{1,0:T(8,128)(2,1)}, u32[]{:S(2)}, u32[]{:S(2)}) collective-permute-start(bf16[96,4096]{1,0:T(8,128)(2,1)} %get-tuple-element.23), channel_id=1, source_target_pairs={{0,3},{1,0},{2,1},{3,2},{4,7},{5,4},{6,5},{7,6},{8,11},{9,8},{10,9... | collective-permute-start | bytes 2359304 | tf_op jit(solution)/shard_map/ppermute | solution.py:20
  8.1 20.5 %collective-permute-start.1 = (bf16[96,4096]{1,0:T(8,128)(2,1)}, bf16[96,4096]{1,0:T(8,128)(2,1)}, u32[]{:S(2)}, u32[]{:S(2)}) collective-permute-start(bf16[96,4096]{1,0:T(8,128)(2,1)} %get-tuple-element.23), channel_id=1, source_target_pairs={{0,1},{1,2},{2,3},{3,0},{4,5},{5,6},{6,7},{7,4},{8,9},{9,10},{10,1... | collective-permute-start | bytes 2359304 | tf_op jit(solution)/shard_map/ppermute | solution.py:20
  8.1 27.6 %collective-permute-start.4 = (bf16[96,4096]{1,0:T(8,128)(2,1)}, bf16[96,4096]{1,0:T(8,128)(2,1)}, u32[]{:S(2)}, u32[]{:S(2)}) collective-permute-start(bf16[96,4096]{1,0:T(8,128)(2,1)} %get-tuple-element.20), channel_id=1, source_target_pairs={{0,12},{1,13},{2,14},{3,15},{4,0},{5,1},{6,2},{7,3},{8,4},{9,5},{1... | collective-permute-start | bytes 2359304 | tf_op jit(solution)/shard_map/ppermute | solution.py:20
  11.1 22.9 %collective-permute-start.5 = (bf16[96,4096]{1,0:T(8,128)(2,1)}, bf16[96,4096]{1,0:T(8,128)(2,1)S(1)}, u32[]{:S(2)}, u32[]{:S(2)}) collective-permute-start(bf16[96,4096]{1,0:T(8,128)(2,1)} %get-tuple-element.20), channel_id=1, source_target_pairs={{0,4},{1,5},{2,6},{3,7},{4,8},{5,9},{6,10},{7,11},{8,12},{9,13},{1... | collective-permute-start | bytes 2359304 | tf_op jit(solution)/shard_map/ppermute | solution.py:20
  29.7 13.0 %collective-permute-start.2 = (bf16[48,4096]{1,0:T(8,128)(2,1)S(1)}, bf16[48,4096]{1,0:T(8,128)(2,1)S(1)}, u32[]{:S(2)}, u32[]{:S(2)}) collective-permute-start(bf16[48,4096]{1,0:T(8,128)(2,1)S(1)} %slice.116), channel_id=1, source_target_pairs={{0,1},{1,2},{2,3},{3,0},{4,5},{5,6},{6,7},{7,4},{8,9},{9,10},{10,1... | collective-permute-start | bytes 1179656 | tf_op jit(solution)/shard_map/ppermute | solution.py:20
  30.8 12.7 %collective-permute-start.3 = (bf16[48,4096]{1,0:T(8,128)(2,1)S(1)}, bf16[48,4096]{1,0:T(8,128)(2,1)S(1)}, u32[]{:S(2)}, u32[]{:S(2)}) collective-permute-start(bf16[48,4096]{1,0:T(8,128)(2,1)S(1)} %slice.117), channel_id=1, source_target_pairs={{0,3},{1,0},{2,1},{3,2},{4,7},{5,4},{6,5},{7,6},{8,11},{9,8},{10,9... | collective-permute-start | bytes 1179656 | tf_op jit(solution)/shard_map/ppermute | solution.py:20
  34.1 12.2 %collective-permute-start.6 = (bf16[48,4096]{1,0:T(8,128)(2,1)S(1)}, bf16[48,4096]{1,0:T(8,128)(2,1)S(1)}, u32[]{:S(2)}, u32[]{:S(2)}) collective-permute-start(bf16[48,4096]{1,0:T(8,128)(2,1)S(1)} %slice.118), channel_id=1, source_target_pairs={{0,4},{1,5},{2,6},{3,7},{4,8},{5,9},{6,10},{7,11},{8,12},{9,13},{1... | collective-permute-start | bytes 1179656 | tf_op jit(solution)/shard_map/ppermute | solution.py:20
  36.8 10.4 %collective-permute-start.7 = (bf16[48,4096]{1,0:T(8,128)(2,1)S(1)}, bf16[48,4096]{1,0:T(8,128)(2,1)S(1)}, u32[]{:S(2)}, u32[]{:S(2)}) collective-permute-start(bf16[48,4096]{1,0:T(8,128)(2,1)S(1)} %slice.119), channel_id=1, source_target_pairs={{0,12},{1,13},{2,14},{3,15},{4,0},{5,1},{6,2},{7,3},{8,4},{9,5},{1... | collective-permute-start | bytes 1179656 | tf_op jit(solution)/shard_map/ppermute | solution.py:20
  48.9 8.0 %copy-start.12 = (bf16[8192,64]{0,1:T(8,128)(2,1)S(1)}, bf16[8192,64]{0,1:T(8,128)(2,1)}, u32[]{:S(2)}) copy-start(bf16[8192,64]{0,1:T(8,128)(2,1)} %param.12) | copy-start | bytes 3145732
  48.9 62.0 %all-to-all-start = ((bf16[128,2,8320]{2,1,0:T(2,128)(2,1)}), bf16[128,2,8320]{2,1,0:T(2,128)(2,1)}, u32[]{:S(2)}, u32[]{:S(2)}) async-start(bf16[128,2,8320]{2,1,0:T(2,128)(2,1)} %reshape.35), calls=%async_computation | async-start | bytes 8519680 | tf_op jit(solution)/shard_map/all_to_all | solution.py:144
  67.8 147.6 %collective-permute-start.9 = (bf16[384,4096]{1,0:T(8,128)(2,1)}, bf16[384,4096]{1,0:T(8,128)(2,1)}, u32[]{:S(2)}, u32[]{:S(2)}) collective-permute-start(bf16[384,4096]{1,0:T(8,128)(2,1)} %constant_dynamic-update-slice_fusion), channel_id=1, source_target_pairs={{0,4},{1,5},{2,6},{3,7},{4,8},{5,9},{6,10},{7,11},{8,12},{9,13},{1... | collective-permute-start | bytes 9437192 | tf_op jit(solution)/shard_map/ppermute | solution.py:20
  69.3 142.7 %collective-permute-start.8 = (bf16[384,4096]{1,0:T(8,128)(2,1)}, bf16[384,4096]{1,0:T(8,128)(2,1)}, u32[]{:S(2)}, u32[]{:S(2)}) collective-permute-start(bf16[384,4096]{1,0:T(8,128)(2,1)} %constant_dynamic-update-slice_fusion), channel_id=1, source_target_pairs={{0,12},{1,13},{2,14},{3,15},{4,0},{5,1},{6,2},{7,3},{8,4},{9,5},{1... | collective-permute-start | bytes 9437192 | tf_op jit(solution)/shard_map/ppermute | solution.py:20
  71.0 151.4 %collective-permute-start.13 = (bf16[384,4096]{1,0:T(8,128)(2,1)}, bf16[384,4096]{1,0:T(8,128)(2,1)}, u32[]{:S(2)}, u32[]{:S(2)}) collective-permute-start(bf16[384,4096]{1,0:T(8,128)(2,1)} %constant_dynamic-update-slice_fusion.5), channel_id=1, source_target_pairs={{0,1},{1,2},{2,3},{3,0},{4,5},{5,6},{6,7},{7,4},{8,9},{9,10},{10,1... | collective-permute-start | bytes 9437192 | tf_op jit(solution)/shard_map/ppermute | solution.py:20
  72.7 144.5 %collective-permute-start.12 = (bf16[384,4096]{1,0:T(8,128)(2,1)}, bf16[384,4096]{1,0:T(8,128)(2,1)}, u32[]{:S(2)}, u32[]{:S(2)}) collective-permute-start(bf16[384,4096]{1,0:T(8,128)(2,1)} %constant_dynamic-update-slice_fusion.5), channel_id=1, source_target_pairs={{0,3},{1,0},{2,1},{3,2},{4,7},{5,4},{6,5},{7,6},{8,11},{9,8},{10,9... | collective-permute-start | bytes 9437192 | tf_op jit(solution)/shard_map/ppermute | solution.py:20
  119.1 4.5 %copy-start.4 = (bf16[256,8320]{1,0:T(8,128)(2,1)S(1)}, bf16[256,8320]{1,0:T(8,128)(2,1)}, u32[]{:S(2)}) copy-start(bf16[256,8320]{1,0:T(8,128)(2,1)} %reshape.36) | copy-start | bytes 12779524
  123.6 3.2 copy-start.13
  138.5 12.4 %slice-start = ((s8[5242880]{0:T(1024)(128)(4,1)}), s8[1048576]{0:T(1024)(128)(4,1)S(1)}, s32[]{:S(2)}) async-start(s8[5242880]{0:T(1024)(128)(4,1)} %bitcast.67), calls=%async_computation.3 | async-start | bytes 2097152
  138.5 126.9 %all-to-all-start.1 = ((bf16[128,2,9216]{2,1,0:T(2,128)(2,1)}), bf16[128,2,9216]{2,1,0:T(2,128)(2,1)}, u32[]{:S(2)}, u32[]{:S(2)}) async-start(bf16[128,2,9216]{2,1,0:T(2,128)(2,1)} %reshape.39), calls=%async_computation.1 | async-start | bytes 9437184 | tf_op jit(solution)/shard_map/all_to_all | solution.py:155
  143.7 7.2 %slice-start.1 = ((s8[5242880]{0:T(1024)(128)(4,1)}), s8[4194304]{0:T(1024)(128)(4,1)S(1)}, s32[]{:S(2)}) async-start(s8[5242880]{0:T(1024)(128)(4,1)} %bitcast.67), calls=%async_computation.4 | async-start | bytes 8388608
  143.8 80.5 %slice-start.2 = ((s8[5242880]{0:T(1024)(128)(4,1)}), s8[4194304]{0:T(1024)(128)(4,1)S(1)}, s32[]{:S(2)}) async-start(s8[5242880]{0:T(1024)(128)(4,1)} %bitcast.69), calls=%async_computation.5 | async-start | bytes 8388608
  150.9 73.4 %slice-start.3 = ((s8[5242880]{0:T(1024)(128)(4,1)}), s8[1048576]{0:T(1024)(128)(4,1)S(1)}, s32[]{:S(2)}) async-start(s8[5242880]{0:T(1024)(128)(4,1)} %bitcast.69), calls=%async_computation.6 | async-start | bytes 2097152
  213.5 44.6 %collective-permute-start.11 = (bf16[192,4096]{1,0:T(8,128)(2,1)S(1)}, bf16[192,4096]{1,0:T(8,128)(2,1)S(1)}, u32[]{:S(2)}, u32[]{:S(2)}) collective-permute-start(bf16[192,4096]{1,0:T(8,128)(2,1)S(1)} %slice.123), channel_id=1, source_target_pairs={{0,12},{1,13},{2,14},{3,15},{4,0},{5,1},{6,2},{7,3},{8,4},{9,5},{1... | collective-permute-start | bytes 4718600 | tf_op jit(solution)/shard_map/ppermute | solution.py:20
  216.9 41.2 %collective-permute-start.10 = (bf16[192,4096]{1,0:T(8,128)(2,1)S(1)}, bf16[192,4096]{1,0:T(8,128)(2,1)S(1)}, u32[]{:S(2)}, u32[]{:S(2)}) collective-permute-start(bf16[192,4096]{1,0:T(8,128)(2,1)S(1)} %slice.122), channel_id=1, source_target_pairs={{0,4},{1,5},{2,6},{3,7},{4,8},{5,9},{6,10},{7,11},{8,12},{9,13},{1... | collective-permute-start | bytes 4718600 | tf_op jit(solution)/shard_map/ppermute | solution.py:20
  218.8 43.0 %collective-permute-start.15 = (bf16[192,4096]{1,0:T(8,128)(2,1)S(1)}, bf16[192,4096]{1,0:T(8,128)(2,1)S(1)}, u32[]{:S(2)}, u32[]{:S(2)}) collective-permute-start(bf16[192,4096]{1,0:T(8,128)(2,1)S(1)} %slice.125), channel_id=1, source_target_pairs={{0,3},{1,0},{2,1},{3,2},{4,7},{5,4},{6,5},{7,6},{8,11},{9,8},{10,9... | collective-permute-start | bytes 4718600 | tf_op jit(solution)/shard_map/ppermute | solution.py:20
  224.0 37.8 %collective-permute-start.14 = (bf16[192,4096]{1,0:T(8,128)(2,1)S(1)}, bf16[192,4096]{1,0:T(8,128)(2,1)S(1)}, u32[]{:S(2)}, u32[]{:S(2)}) collective-permute-start(bf16[192,4096]{1,0:T(8,128)(2,1)S(1)} %slice.124), channel_id=1, source_target_pairs={{0,1},{1,2},{2,3},{3,0},{4,5},{5,6},{6,7},{7,4},{8,9},{9,10},{10,1... | collective-permute-start | bytes 4718600 | tf_op jit(solution)/shard_map/ppermute | solution.py:20
  273.0 6.2 %copy-start.5 = (f32[384,576]{1,0:T(8,128)S(1)}, f32[384,576]{1,0:T(8,128)}, u32[]{:S(2)}) copy-start(f32[384,576]{1,0:T(8,128)} %fusion.62) | copy-start | bytes 2654212
  273.0 6.2 %copy-start.6 = (f32[384,576]{1,0:T(8,128)S(1)}, f32[384,576]{1,0:T(8,128)}, u32[]{:S(2)}) copy-start(f32[384,576]{1,0:T(8,128)} %fusion.65) | copy-start | bytes 2654212
  273.0 6.2 %copy-start.7 = (f32[384,576]{1,0:T(8,128)S(1)}, f32[384,576]{1,0:T(8,128)}, u32[]{:S(2)}) copy-start(f32[384,576]{1,0:T(8,128)} %fusion.64) | copy-start | bytes 2654212
  273.0 6.2 %copy-start.8 = (f32[384,576]{1,0:T(8,128)S(1)}, f32[384,576]{1,0:T(8,128)}, u32[]{:S(2)}) copy-start(f32[384,576]{1,0:T(8,128)} %fusion.63) | copy-start | bytes 2654212
  273.0 6.2 %copy-start.9 = (f32[384,576]{1,0:T(8,128)S(1)}, f32[384,576]{1,0:T(8,128)}, u32[]{:S(2)}) copy-start(f32[384,576]{1,0:T(8,128)} %fusion.66) | copy-start | bytes 2654212
  273.0 6.2 %copy-start.10 = (f32[384,576]{1,0:T(8,128)S(1)}, f32[384,576]{1,0:T(8,128)}, u32[]{:S(2)}) copy-start(f32[384,576]{1,0:T(8,128)} %fusion.7) | copy-start | bytes 2654212
  273.0 6.2 %copy-start.11 = (f32[384,576]{1,0:T(8,128)S(1)}, f32[384,576]{1,0:T(8,128)}, u32[]{:S(2)}) copy-start(f32[384,576]{1,0:T(8,128)} %fusion.11) | copy-start | bytes 2654212
  284.0 34.9 %all-to-all-start.2 = ((bf16[16,96,576]{2,1,0:T(8,128)(2,1)}), bf16[16,96,576]{2,1,0:T(8,128)(2,1)}, u32[]{:S(2)}, u32[]{:S(2)}) async-start(bf16[16,96,576]{2,1,0:T(8,128)(2,1)} %bitcast.66), calls=%async_computation.2 | async-start | bytes 3932160 | tf_op jit(solution)/shard_map/all_to_all | solution.py:182
  290.5 37.1 %copy-start.1 = (bf16[2,64,8192]{2,1,0:T(8,128)(2,1)S(1)}, bf16[2,64,8192]{2,1,0:T(8,128)(2,1)}, u32[]{:S(2)}) copy-start(bf16[2,64,8192]{2,1,0:T(8,128)(2,1)} %param.14) | copy-start | bytes 6291460
  318.9 2.3 copy-start.2
where the time goes:
time: 330 us; the launch traced here: 328 us
  waiting for transfers between devices  144 us (44%)
  local copies, waits for them, and re-layouts  57.7 us (17%)
  matrix products  55.1 us (17%)
  starting transfers between devices  46.3 us (14%)
  other arithmetic  16.7 us (5%)
  Pallas kernels  6.46 us (2%)
    ppermute x16, waiting for transfers between devices, shift(): return lax.ppermute(x, 'tp', pairs)  79.7 us
    dot_general x8, matrix products, on_device(): jnp.dot(x, w, preferred_element_type=F32).reshape(side, row_count, both)  42.5 us
    all_to_all x1, waiting for transfers between devices, on_device(): lax.all_to_all(send_rows, ('grp', 'tp'), split_axis=0, concat_axis=0, til...  36.4 us
    all_to_all x1, waiting for transfers between devices, on_device(): lax.all_to_all(projected.reshape(members, row_count, both), 'tp', split_a...  28.2 us
    ppermute x16, starting transfers between devices, shift(): return lax.ppermute(x, 'tp', pairs)  26.5 us
    unnamed x47, local copies, waits for them, and re-layouts  11.5 us
    concatenate x1, other arithmetic, on_device(): weights = jnp.concatenate([query_base_output, value_base_output], axis=1)  9.12 us
    all_to_all x1, starting transfers between devices, on_device(): lax.all_to_all(send_rows, ('grp', 'tp'), split_axis=0, concat_axis=0, til...  8.01 us
  transfers between devices with their start and end apart: 19, of which 5 were waited for; matrix products, arithmetic and copies ran while one was open for 32% of the time, Pallas kernels for 0%

commit v1 on v0

--- a/solution.py
+++ b/solution.py
@@ -20,14 +20,18 @@
     return lax.ppermute(x, "tp", pairs)
 
 
+def line_sides(x, step):
+    return shift(x, -step[0], -step[1]), shift(x, *step)
+
+
+def line_far(after, before, step):
+    half = before.shape[0] // 2
+    return shift(before[:half], *step), shift(after[half:], -step[0], -step[1])
+
+
 def line_gather(x, step):
-    back = (-step[0], -step[1])
-    half = x.shape[0] // 2
-    before = shift(x, *step)
-    after = shift(x, *back)
-    far_low = shift(before[:half], *step)
-    far_high = shift(after[half:], *back)
-    return after, (far_low, far_high), before
+    after, before = line_sides(x, step)
+    return after, line_far(after, before, step), before
 
 
 def to_absolute(blocks, place):
@@ -55,32 +59,26 @@
     return query, value
 
 
-def finish_kernel(slot_ref, plain_ref, query_ref, value_ref, queries_ref, values_ref):
-    rows, query_cols = plain_ref.shape[1], queries_ref.shape[1] // 2
-    slots = query_ref.shape[0]
-    pick = (lax.broadcasted_iota(jnp.int32, (rows, slots), 1) == slot_ref[...]).astype(BF)
-    term = jnp.dot(pick, query_ref[...], preferred_element_type=F32)
+def finish_kernel(plain_ref, query_term_ref, value_term_ref, queries_ref, values_ref):
+    query_cols = queries_ref.shape[1] // 2
     for i in range(2):
-        cols = pl.ds(i * query_cols, query_cols)
+        cols = slice(i * query_cols, (i + 1) * query_cols)
         base = plain_ref[i, :, :query_cols].astype(F32)
-        queries_ref[:, cols] = (base + term[:, i * query_cols : (i + 1) * query_cols]).astype(BF)
-    term = jnp.dot(pick, value_ref[...], preferred_element_type=F32)
+        queries_ref[:, cols] = (base + query_term_ref[:, cols].astype(F32)).astype(BF)
     base = jnp.concatenate([plain_ref[0, :, query_cols:], plain_ref[1, :, query_cols:]], axis=1)
-    values_ref[...] = (base.astype(F32) + term).astype(BF)
-
-
-def finish(slot_index, plain, terms, query_cols, value_cols):
+    values_ref[...] = (base.astype(F32) + value_term_ref[...].astype(F32)).astype(BF)
+
+
+def finish(plain, terms, query_cols, value_cols):
     members, rows, both = plain.shape
-    slots = terms.shape[0]
     value_at = members * query_cols // (2 * value_cols)
     return pl.pallas_call(
         finish_kernel,
         grid=(members // 2,),
         in_specs=[
-            pl.BlockSpec((rows, 1), lambda i: (0, 0)),
             pl.BlockSpec((2, rows, both), lambda i: (i, 0, 0)),
-            pl.BlockSpec((slots, 2 * query_cols), lambda i: (0, i)),
-            pl.BlockSpec((slots, 2 * value_cols), lambda i: (0, value_at + i)),
+            pl.BlockSpec((rows, 2 * query_cols), lambda i: (0, i)),
+            pl.BlockSpec((rows, 2 * value_cols), lambda i: (0, value_at + i)),
         ],
         out_specs=[
             pl.BlockSpec((rows, 2 * query_cols), lambda i: (0, i)),
@@ -92,11 +90,9 @@
         ],
         compiler_params=pltpu.CompilerParams(vmem_limit_bytes=24 << 20),
         cost_estimate=pl.CostEstimate(
-            flops=2 * rows * slots * members * (query_cols + value_cols),
-            bytes_accessed=2 * (slots + 2 * rows) * members * (query_cols + value_cols),
-            transcendentals=0,
+            flops=rows * members * both, bytes_accessed=6 * rows * members * both, transcendentals=0
         ),
-    )(slot_index[:, None], plain, terms, terms)
+    )(plain, terms, terms)
 
 
 def on_device(
@@ -117,7 +113,6 @@
     devices = lax.axis_size("grp") * members
     capacity = 2
     slot_total = devices * capacity
-    place = lax.axis_index("tp")
 
     holder_id = holder[:, 0]
     same_holder = holder_id[:, None] == holder_id[None, :]
@@ -132,15 +127,6 @@
     send_rows = jnp.dot(pick_table, marked, preferred_element_type=F32).astype(BF)
     send_rows = send_rows.reshape(devices, capacity, width + 128)
 
-    half = width // 2
-    along_z, along_y = (0, 1), (1, 0)
-    weights = jnp.concatenate([query_base_output, value_base_output], axis=1)
-    lines = []
-    for part, step in ((0, along_z), (1, along_y)):
-        own = tokens[:, part * half : (part + 1) * half]
-        after, far, before = line_gather(own, step)
-        lines.append(jnp.concatenate([own, after, *far, before], axis=0))
-    lines[0], lines[1], send_rows = lax.optimization_barrier((lines[0], lines[1], send_rows))
     got_rows = lax.all_to_all(
         send_rows, ("grp", "tp"), split_axis=0, concat_axis=0, tiled=True
     ).reshape(slot_total, width + 128)
@@ -158,13 +144,23 @@
         split_axis=0,
         concat_axis=0,
         tiled=True,
-    ).reshape(slot_total, terms.shape[1])
-
+    )
+
+    half = width // 2
+    along_z, along_y = (0, 1), (1, 0)
     gathered = []
-    for line, step in zip(lines, (along_y, along_z)):
-        after, far, before = line_gather(line, step)
-        gathered.append([line, after, jnp.concatenate(far, axis=0), before])
-    gathered[1][3], back = lax.optimization_barrier((gathered[1][3], back))
+    for part, (one, two) in enumerate(((along_z, along_y), (along_y, along_z))):
+        own = tokens[:, part * half : (part + 1) * half]
+        after, far, before = line_gather(own, one)
+        line = jnp.concatenate([own, after, *far, before], axis=0)
+        after, before = line_sides(line, two)
+        gathered.append([line, after, before])
+    query_base_output, value_base_output, _ = lax.optimization_barrier(
+        (query_base_output, value_base_output, far[0][:16, :128])
+    )
+    weights = jnp.concatenate([query_base_output, value_base_output], axis=1)
+    for blocks, two in zip(gathered, (along_y, along_z)):
+        blocks.insert(2, jnp.concatenate(line_far(blocks[1], blocks[2], two), axis=0))
     partial = []
     for part in range(2):
         w = weights[part * half : (part + 1) * half]
@@ -176,13 +172,17 @@
                 ]
             )
         )
+    place = lax.axis_index("tp")
     projected = (partial[0] + jnp.swapaxes(partial[1], 0, 1)).astype(BF)
     projected = to_absolute(projected, place // side)
     projected = jnp.swapaxes(to_absolute(jnp.swapaxes(projected, 0, 1), place % side), 0, 1)
+    projected, back = lax.optimization_barrier((projected, back))
+    back = back.reshape(slot_total, back.shape[2])
+    row_terms = jnp.dot(pick_table.T, back, preferred_element_type=F32).astype(BF)
     plain = lax.all_to_all(
         projected.reshape(members, row_count, both), "tp", split_axis=0, concat_axis=0, tiled=True
     )
-    queries, values = finish(slot_index, plain, back, query_cols, value_cols)
+    queries, values = finish(plain, row_terms, query_cols, value_cols)
     return (queries, values)
 
 

time: 330 us -> 302 us (0.915)
  waiting for transfers between devices: 144 us -> 121 us
  other arithmetic: 16.7 us -> 12.5 us
  starting transfers between devices: 46.3 us -> 49.9 us
  matrix products: 55.1 us -> 51.6 us
    all_to_all x1, waiting for transfers between devices: 36.4 us -> 0.01 us  [on_device(): lax.all_to_all(send_rows, ('grp', 'tp'), split_axis=0, concat_axis=0, til...]
    ppermute x16, waiting for transfers between devices: 79.7 us -> 107 us  [shift(): return lax.ppermute(x, 'tp', pairs)]
    all_to_all x1, waiting for transfers between devices: 28.2 us -> 13.5 us  [on_device(): lax.all_to_all(projected.reshape(members, row_count, both), 'tp', split_a...]
    dot_general x8, matrix products: 42.5 us -> 34.4 us  [on_device(): jnp.dot(x, w, preferred_element_type=F32).reshape(side, row_count, both)]
    dot_general x0 -> x1, matrix products: none -> 4.67 us  [on_device(): jnp.dot(pick_table.T, back, preferred_element_type=F32).astype(BF)]
    concatenate x1, other arithmetic: 9.12 us -> 4.86 us  [on_device(): weights = jnp.concatenate([query_base_output, value_base_output], axis=1)]
    unnamed x47 -> x38, local copies, waits for them, and re-layouts: 11.5 us -> 8.82 us
  transfers between devices with their start and end apart: 19 -> 19, of which waited for: 5 -> 7; matrix products, arithmetic and copies ran while one was open for 32% -> 39% of each run, Pallas kernels for 0% -> 0%
where the time goes in v1:
time: 302 us; the launch traced here: 300 us
  waiting for transfers between devices  121 us (40%)
  local copies, waits for them, and re-layouts  58.4 us (19%)
  matrix products  51.6 us (17%)
  starting transfers between devices  49.9 us (17%)
  other arithmetic  12.5 us (4%)
  Pallas kernels  5.73 us (2%)
    ppermute x16, waiting for transfers between devices, shift(): return lax.ppermute(x, 'tp', pairs)  107 us
    dot_general x8, matrix products, on_device(): jnp.dot(x, w, preferred_element_type=F32).reshape(side, row_count, both)  34.4 us
    ppermute x16, starting transfers between devices, shift(): return lax.ppermute(x, 'tp', pairs)  28.8 us
    all_to_all x1, waiting for transfers between devices, on_device(): lax.all_to_all(projected.reshape(members, row_count, both), 'tp', split_a...  13.5 us
    all_to_all x1, starting transfers between devices, on_device(): lax.all_to_all(send_rows, ('grp', 'tp'), split_axis=0, concat_axis=0, til...  10.1 us
    unnamed x38, local copies, waits for them, and re-layouts  8.82 us
    dot_general x2, matrix products, apply_lowrank_adapters(): reduced = jnp.dot(rows, adapter_down_weight[i], preferred_element_type=F32)  7.7 us
    reshape x1, local copies, waits for them, and re-layouts, on_device(): back = back.reshape(slot_total, back.shape[2])  7.54 us
  transfers between devices with their start and end apart: 19, of which 7 were waited for; matrix products, arithmetic and copies ran while one was open for 39% of the time, Pallas kernels for 0%

profile of v1, /device:TPU:6, one launch (start us, length us, event | category | flops | bytes accessed | tf_op | source)
XLA Modules:
  0.0 300.2 jit_solution(7596308675151852162)
XLA Ops:
  0.7 3.4 %fusion.61 = (bf16[96,4096]{1,0:T(8,128)(2,1)}, bf16[384,4096]{1,0:T(8,128)(2,1)}, bf16[384,4096]{1,0:T(8,128)(2,1)}, bf16[96,4096]{1,0:T(8,128)(2,1)}) fusion(bf16[96,8192]{1,0:T(8,128)(2,1)} %param.8), kind=kLoop, calls=%fused_computation.76 | loop fusion | bytes 4718592 | tf_op jit(solution)/shard_map/slice | solution.py:153
  4.1 4.0 %collective-permute-start = (bf16[96,4096]{1,0:T(8,128)(2,1)}, bf16[96,4096]{1,0:T(8,128)(2,1)}, u32[]{:S(2)}, u32[]{:S(2)}) collective-permute-start(bf16[96,4096]{1,0:T(8,128)(2,1)} %get-tuple-element.21), channel_id=1, source_target_pairs={{0,3},{1,0},{2,1},{3,2},{4,7},{5,4},{6,5},{7,6},{8,11},{9,8},{10,9... | collective-permute-start | bytes 2359304 | tf_op jit(solution)/shard_map/ppermute | solution.py:20
  8.1 3.0 %collective-permute-start.8 = (bf16[96,4096]{1,0:T(8,128)(2,1)}, bf16[96,4096]{1,0:T(8,128)(2,1)}, u32[]{:S(2)}, u32[]{:S(2)}) collective-permute-start(bf16[96,4096]{1,0:T(8,128)(2,1)} %get-tuple-element.18), channel_id=1, source_target_pairs={{0,12},{1,13},{2,14},{3,15},{4,0},{5,1},{6,2},{7,3},{8,4},{9,5},{1... | collective-permute-start | bytes 2359304 | tf_op jit(solution)/shard_map/ppermute | solution.py:20
  11.4 3.3 %convolution_convert_fusion = bf16[256,8320]{1,0:T(8,128)(2,1)} fusion(bf16[96,128]{1,0:T(8,128)(2,1)S(1)} %broadcast_in_dim.34, bf16[96,8192]{1,0:T(8,128)(2,1)S(1)} %copy-done.3, s32[96]{0:T(128)S(1)} %multiply_add_fusion), kind=kOutput, calls=%fused_computation | convolution fusion | flops 414294016 | bytes 5857664 | tf_op jit(solution)/shard_map/dot_general | solution.py:127
  14.7 7.3 %reshape.34 = bf16[128,2,8320]{2,1,0:T(2,128)(2,1)} reshape(bf16[256,8320]{1,0:T(8,128)(2,1)} %convolution_convert_fusion) | data formatting | bytes 8519680 | tf_op jit(solution)/shard_map/reshape | solution.py:128
  21.9 10.1 %all-to-all-start = ((bf16[128,2,8320]{2,1,0:T(2,128)(2,1)}), bf16[128,2,8320]{2,1,0:T(2,128)(2,1)}, u32[]{:S(2)}, u32[]{:S(2)}) async-start(bf16[128,2,8320]{2,1,0:T(2,128)(2,1)} %reshape.34), calls=%async_computation | async-start | bytes 8519680 | tf_op jit(solution)/shard_map/all_to_all | solution.py:130
  32.1 2.7 copy.46
  34.8 4.9 %pad_maximum_fusion = (bf16[4096,576]{1,0:T(8,128)(2,1)S(1)}, bf16[4096,576]{1,0:T(8,128)(2,1)S(1)}) fusion(bf16[8192,64]{1,0:T(8,128)(2,1)} %copy.46, bf16[8192,512]{1,0:T(8,128)(2,1)} %param.11), kind=kLoop, calls=%fused_computation.7 | loop fusion | flops 18874368 | bytes 18874368 | tf_op jit(solution)/shard_map/concatenate | solution.py:161
  39.7 1.3 slice.117
  41.0 1.7 collective-permute-start.2
  42.7 1.3 slice.118
  44.0 1.9 collective-permute-start.3
  45.9 1.6 collective-permute-start.10
  47.5 1.0 slice.124
  48.5 1.8 collective-permute-start.11
  50.3 2.1 constant_dynamic-update-slice_fusion.3
  52.4 2.1 constant_dynamic-update-slice_fusion.8
  54.5 34.9 %collective-permute-done.2 = bf16[48,4096]{1,0:T(8,128)(2,1)S(1)} collective-permute-done((bf16[48,4096]{1,0:T(8,128)(2,1)S(1)}, bf16[48,4096]{1,0:T(8,128)(2,1)S(1)}, u32[]{:S(2)}, u32[]{:S(2)}) %collective-permute-start.2) | collective-permute-done | bytes 393248 | tf_op jit(solution)/shard_map/ppermute | solution.py:20
  89.4 0.8 constant_dynamic-update-slice_fusion.2
  90.2 0.8 constant_dynamic-update-slice_fusion.1
  90.9 2.1 constant_dynamic-update-slice_fusion
  93.0 1.5 collective-permute-start.5
  94.5 1.7 collective-permute-start.4
  96.2 0.8 constant_dynamic-update-slice_fusion.7
  97.0 0.8 constant_dynamic-update-slice_fusion.6
  97.8 1.0 constant_dynamic-update-slice_fusion.5
  99.0 3.0 collective-permute-start.12
  102.0 5.4 %fusion.64 = f32[384,576]{1,0:T(8,128)} fusion(bf16[384,4096]{1,0:T(8,128)(2,1)} %constant_dynamic-update-slice_fusion, bf16[4096,576]{1,0:T(8,128)(2,1)S(1)} %get-tuple-element.13), kind=kOutput, calls=%fused_computation.79 | convolution fusion | flops 1811939328 | bytes 8749056 | tf_op jit(solution)/shard_map/dot_general | solution.py:170
  107.4 5.5 %fusion.67 = f32[384,576]{1,0:T(8,128)} fusion(bf16[384,4096]{1,0:T(8,128)(2,1)} %constant_dynamic-update-slice_fusion.5, bf16[4096,576]{1,0:T(8,128)(2,1)S(1)} %get-tuple-element.12), kind=kOutput, calls=%fused_computation.82 | convolution fusion | flops 1811939328 | bytes 8749056 | tf_op jit(solution)/shard_map/dot_general | solution.py:170
  112.9 7.3 %reshape.35 = bf16[256,8320]{1,0:T(8,128)(2,1)} reshape(bf16[128,2,8320]{2,1,0:T(2,128)(2,1)} %all-to-all-done) | data formatting | bytes 8519680 | tf_op jit(solution)/shard_map/reshape | solution.py:132
  120.1 1.0 compare_reduce_fusion.1
  121.1 4.5 %fusion.30 = bf16[256,128]{0,1:T(8,128)(2,1)S(1)} fusion(bf16[2,8192,128]{2,1,0:T(8,128)(2,1)} %param.13, bf16[256,8320]{1,0:T(8,128)(2,1)} %reshape.35, pred[256]{0:T(512)(128)(4,1)S(1)} %get-tuple-element.10), kind=kOutput, calls=%fused_computation.40 | convolution fusion | flops 536936448 | bytes 6357248 | tf_op jit(solution)/shard_map/dot_general | solution.py:49
  125.7 3.2 %fusion.40 = bf16[256,128]{0,1:T(8,128)(2,1)S(1)} fusion(bf16[2,8192,128]{2,1,0:T(8,128)(2,1)} %param.13, bf16[256,8320]{1,0:T(8,128)(2,1)S(1)} %copy-done.6, pred[256]{0:T(512)(128)(4,1)S(1)} %get-tuple-element.11), kind=kOutput, calls=%fused_computation.42 | convolution fusion | flops 536936448 | bytes 6357504 | tf_op jit(solution)/shard_map/dot_general | solution.py:49
  129.2 1.3 fusion
  130.5 2.5 pad_maximum_fusion.1
  133.0 7.5 %reshape.38 = bf16[128,2,9216]{2,1,0:T(2,128)(2,1)} reshape(bf16[256,9216]{1,0:T(8,128)(2,1)} %pad_maximum_fusion.1) | data formatting | bytes 9437184 | tf_op jit(solution)/shard_map/reshape | solution.py:142
  140.5 6.3 %all-to-all-start.1 = ((bf16[128,2,9216]{2,1,0:T(2,128)(2,1)}), bf16[128,2,9216]{2,1,0:T(2,128)(2,1)}, u32[]{:S(2)}, u32[]{:S(2)}) async-start(bf16[128,2,9216]{2,1,0:T(2,128)(2,1)} %reshape.38), calls=%async_computation.1 | async-start | bytes 9437184 | tf_op jit(solution)/shard_map/all_to_all | solution.py:141
  146.9 58.3 %collective-permute-done.4 = bf16[384,4096]{1,0:T(8,128)(2,1)} collective-permute-done((bf16[384,4096]{1,0:T(8,128)(2,1)}, bf16[384,4096]{1,0:T(8,128)(2,1)}, u32[]{:S(2)}, u32[]{:S(2)}) %collective-permute-start.4) | collective-permute-done | bytes 3145760 | tf_op jit(solution)/shard_map/ppermute | solution.py:20
  205.2 1.5 slice.122
  206.8 4.1 %collective-permute-start.7 = (bf16[192,4096]{1,0:T(8,128)(2,1)S(1)}, bf16[192,4096]{1,0:T(8,128)(2,1)S(1)}, u32[]{:S(2)}, u32[]{:S(2)}) collective-permute-start(bf16[192,4096]{1,0:T(8,128)(2,1)S(1)} %slice.122), channel_id=1, source_target_pairs={{0,12},{1,13},{2,14},{3,15},{4,0},{5,1},{6,2},{7,3},{8,4},{9,5},{1... | collective-permute-start | bytes 4718600 | tf_op jit(solution)/shard_map/ppermute | solution.py:20
  210.9 1.5 slice.121
  212.5 7.2 %collective-permute-done.12 = bf16[384,4096]{1,0:T(8,128)(2,1)} collective-permute-done((bf16[384,4096]{1,0:T(8,128)(2,1)}, bf16[384,4096]{1,0:T(8,128)(2,1)}, u32[]{:S(2)}, u32[]{:S(2)}) %collective-permute-start.12) | collective-permute-done | bytes 3145760 | tf_op jit(solution)/shard_map/ppermute | solution.py:20
  219.7 1.5 slice.126
  221.2 3.9 %collective-permute-start.15 = (bf16[192,4096]{1,0:T(8,128)(2,1)S(1)}, bf16[192,4096]{1,0:T(8,128)(2,1)S(1)}, u32[]{:S(2)}, u32[]{:S(2)}) collective-permute-start(bf16[192,4096]{1,0:T(8,128)(2,1)S(1)} %slice.126), channel_id=1, source_target_pairs={{0,3},{1,0},{2,1},{3,2},{4,7},{5,4},{6,5},{7,6},{8,11},{9,8},{10,9... | collective-permute-start | bytes 4718600 | tf_op jit(solution)/shard_map/ppermute | solution.py:20
  225.1 1.7 slice.125
  227.2 4.5 %fusion.66 = f32[384,576]{1,0:T(8,128)S(1)} fusion(bf16[384,4096]{1,0:T(8,128)(2,1)} %collective-permute-done.5, bf16[4096,576]{1,0:T(8,128)(2,1)S(1)} %bitcast.69), kind=kOutput, calls=%fused_computation.81 | convolution fusion | flops 1811939328 | bytes 8749056 | tf_op jit(solution)/shard_map/dot_general | solution.py:170
  231.7 4.5 %fusion.65 = f32[384,576]{1,0:T(8,128)S(1)} fusion(bf16[384,4096]{1,0:T(8,128)(2,1)} %collective-permute-done.4, bf16[4096,576]{1,0:T(8,128)(2,1)S(1)} %bitcast.69), kind=kOutput, calls=%fused_computation.80 | convolution fusion | flops 1811939328 | bytes 8749056 | tf_op jit(solution)/shard_map/dot_general | solution.py:170
  236.2 4.5 %fusion.69 = f32[384,576]{1,0:T(8,128)S(1)} fusion(bf16[384,4096]{1,0:T(8,128)(2,1)} %collective-permute-done.13, bf16[4096,576]{1,0:T(8,128)(2,1)S(1)} %bitcast.67), kind=kOutput, calls=%fused_computation.84 | convolution fusion | flops 1811939328 | bytes 8749056 | tf_op jit(solution)/shard_map/dot_general | solution.py:170
  240.7 4.5 %fusion.68 = f32[384,576]{1,0:T(8,128)S(1)} fusion(bf16[384,4096]{1,0:T(8,128)(2,1)} %collective-permute-done.12, bf16[4096,576]{1,0:T(8,128)(2,1)S(1)} %bitcast.67), kind=kOutput, calls=%fused_computation.83 | convolution fusion | flops 1811939328 | bytes 8749056 | tf_op jit(solution)/shard_map/dot_general | solution.py:170
  245.3 3.4 %collective-permute-done.7 = bf16[192,4096]{1,0:T(8,128)(2,1)S(1)} collective-permute-done((bf16[192,4096]{1,0:T(8,128)(2,1)S(1)}, bf16[192,4096]{1,0:T(8,128)(2,1)S(1)}, u32[]{:S(2)}, u32[]{:S(2)}) %collective-permute-start.7) | collective-permute-done | bytes 1572896 | tf_op jit(solution)/shard_map/ppermute | solution.py:20
  248.7 2.7 fusion.7
  251.4 1.7 collective-permute-done.15
  253.1 1.8 collective-permute-done.14
  254.9 2.9 fusion.11
  257.8 0.6 fusion.2
  258.6 1.0 maximum_select_fusion
  259.9 0.3 fusion.19
  260.9 1.7 fusion.20
  262.6 4.7 %all-to-all-start.2 = ((bf16[16,96,576]{2,1,0:T(8,128)(2,1)}), bf16[16,96,576]{2,1,0:T(8,128)(2,1)}, u32[]{:S(2)}, u32[]{:S(2)}) async-start(bf16[16,96,576]{2,1,0:T(8,128)(2,1)} %bitcast.65), calls=%async_computation.2 | async-start | bytes 3932160 | tf_op jit(solution)/shard_map/all_to_all | solution.py:182
  267.3 7.5 %reshape.40 = bf16[256,9216]{1,0:T(8,128)(2,1)} reshape(bf16[128,2,9216]{2,1,0:T(2,128)(2,1)} %all-to-all-done.1) | data formatting | bytes 9437184 | tf_op jit(solution)/shard_map/reshape | solution.py:180
  274.8 4.7 %convolution_convert_fusion.1.query_term_ref.value_term_ref = bf16[96,9216]{1,0:T(8,128)(2,1)} fusion(bf16[256,9216]{1,0:T(8,128)(2,1)} %reshape.40, s32[96]{0:T(128)S(1)} %multiply_add_fusion), kind=kOutput, calls=%fused_computation.2 | convolution fusion | flops 453894144 | bytes 6488448 | tf_op jit(solution)/shard_map/dot_general | solution.py:181
  279.5 13.5 %all-to-all-done.2.plain_ref = bf16[16,96,576]{2,1,0:T(8,128)(2,1)} async-done(((bf16[16,96,576]{2,1,0:T(8,128)(2,1)}), bf16[16,96,576]{2,1,0:T(8,128)(2,1)}, u32[]{:S(2)}, u32[]{:S(2)}) %all-to-all-start.2) | async-done | bytes 1769504 | tf_op jit(solution)/shard_map/all_to_all | solution.py:182
  293.0 1.5 copy-done.2
  294.5 5.7 %shard_map.95 = (bf16[96,8192]{1,0:T(8,128)(2,1)}, bf16[96,1024]{1,0:T(8,128)(2,1)}) custom-call(bf16[16,96,576]{2,1,0:T(8,128)(2,1)} %all-to-all-done.2.plain_ref, bf16[96,9216]{1,0:T(8,128)(2,1)S(1)} %copy-done.2, bf16[96,9216]{1,0:T(8,128)(2,1)S(1)} %copy-done.2), custom_call_target="tpu_custom_call" | custom-call | flops 884736 | bytes 5308416 | tf_op jit(solution)/shard_map/pallas_call | solution.py:75
  (64 shorter events, 2.4 us)
Async XLA Ops:
  0.6 128.6 %copy-start = (bf16[2,64,8192]{2,1,0:T(8,128)(2,1)S(1)}, bf16[2,64,8192]{2,1,0:T(8,128)(2,1)}, u32[]{:S(2)}) copy-start(bf16[2,64,8192]{2,1,0:T(8,128)(2,1)} %param.14) | copy-start | bytes 6291460
  0.6 10.8 %copy-start.3 = (bf16[96,8192]{1,0:T(8,128)(2,1)S(1)}, bf16[96,8192]{1,0:T(8,128)(2,1)}, u32[]{:S(2)}) copy-start(bf16[96,8192]{1,0:T(8,128)(2,1)} %param.8) | copy-start | bytes 4718596
  0.7 10.5 %copy-start.10 = (s32[96,1]{0,1:T(1,128)S(1)}, s32[96,1]{0,1:T(1,128)}, u32[]{:S(2)}) copy-start(s32[96,1]{0,1:T(1,128)} %param.10) | copy-start | bytes 1156
  0.7 10.5 %copy-start.11 = (s32[96,1]{0,1:T(1,128)S(1)}, s32[96,1]{0,1:T(1,128)}, u32[]{:S(2)}) copy-start(s32[96,1]{0,1:T(1,128)} %param.9) | copy-start | bytes 1156
  4.1 38.7 %collective-permute-start = (bf16[96,4096]{1,0:T(8,128)(2,1)}, bf16[96,4096]{1,0:T(8,128)(2,1)}, u32[]{:S(2)}, u32[]{:S(2)}) collective-permute-start(bf16[96,4096]{1,0:T(8,128)(2,1)} %get-tuple-element.21), channel_id=1, source_target_pairs={{0,3},{1,0},{2,1},{3,2},{4,7},{5,4},{6,5},{7,6},{8,11},{9,8},{10,9... | collective-permute-start | bytes 2359304 | tf_op jit(solution)/shard_map/ppermute | solution.py:20
  8.1 31.6 %collective-permute-start.1 = (bf16[96,4096]{1,0:T(8,128)(2,1)}, bf16[96,4096]{1,0:T(8,128)(2,1)}, u32[]{:S(2)}, u32[]{:S(2)}) collective-permute-start(bf16[96,4096]{1,0:T(8,128)(2,1)} %get-tuple-element.21), channel_id=1, source_target_pairs={{0,1},{1,2},{2,3},{3,0},{4,5},{5,6},{6,7},{7,4},{8,9},{9,10},{10,1... | collective-permute-start | bytes 2359304 | tf_op jit(solution)/shard_map/ppermute | solution.py:20
  8.1 39.4 %collective-permute-start.8 = (bf16[96,4096]{1,0:T(8,128)(2,1)}, bf16[96,4096]{1,0:T(8,128)(2,1)}, u32[]{:S(2)}, u32[]{:S(2)}) collective-permute-start(bf16[96,4096]{1,0:T(8,128)(2,1)} %get-tuple-element.18), channel_id=1, source_target_pairs={{0,12},{1,13},{2,14},{3,15},{4,0},{5,1},{6,2},{7,3},{8,4},{9,5},{1... | collective-permute-start | bytes 2359304 | tf_op jit(solution)/shard_map/ppermute | solution.py:20
  11.1 34.8 %collective-permute-start.9 = (bf16[96,4096]{1,0:T(8,128)(2,1)}, bf16[96,4096]{1,0:T(8,128)(2,1)S(1)}, u32[]{:S(2)}, u32[]{:S(2)}) collective-permute-start(bf16[96,4096]{1,0:T(8,128)(2,1)} %get-tuple-element.18), channel_id=1, source_target_pairs={{0,4},{1,5},{2,6},{3,7},{4,8},{5,9},{6,10},{7,11},{8,12},{9,13},{1... | collective-permute-start | bytes 2359304 | tf_op jit(solution)/shard_map/ppermute | solution.py:20
  21.9 90.9 %all-to-all-start = ((bf16[128,2,8320]{2,1,0:T(2,128)(2,1)}), bf16[128,2,8320]{2,1,0:T(2,128)(2,1)}, u32[]{:S(2)}, u32[]{:S(2)}) async-start(bf16[128,2,8320]{2,1,0:T(2,128)(2,1)} %reshape.34), calls=%async_computation | async-start | bytes 8519680 | tf_op jit(solution)/shard_map/all_to_all | solution.py:130
  39.7 62.3 %copy-start.5 = (bf16[4096,576]{1,0:T(8,128)(2,1)}, bf16[4096,576]{1,0:T(8,128)(2,1)S(1)}, u32[]{:S(2)}) copy-start(bf16[4096,576]{1,0:T(8,128)(2,1)S(1)} %get-tuple-element.13) | copy-start | bytes 14155780
  39.7 67.7 %copy-start.4 = (bf16[4096,576]{1,0:T(8,128)(2,1)}, bf16[4096,576]{1,0:T(8,128)(2,1)S(1)}, u32[]{:S(2)}) copy-start(bf16[4096,576]{1,0:T(8,128)(2,1)S(1)} %get-tuple-element.12) | copy-start | bytes 14155780
  41.0 48.4 %collective-permute-start.2 = (bf16[48,4096]{1,0:T(8,128)(2,1)S(1)}, bf16[48,4096]{1,0:T(8,128)(2,1)S(1)}, u32[]{:S(2)}, u32[]{:S(2)}) collective-permute-start(bf16[48,4096]{1,0:T(8,128)(2,1)S(1)} %slice.117), channel_id=1, source_target_pairs={{0,1},{1,2},{2,3},{3,0},{4,5},{5,6},{6,7},{7,4},{8,9},{9,10},{10,1... | collective-permute-start | bytes 1179656 | tf_op jit(solution)/shard_map/ppermute | solution.py:20
  44.0 46.1 %collective-permute-start.3 = (bf16[48,4096]{1,0:T(8,128)(2,1)S(1)}, bf16[48,4096]{1,0:T(8,128)(2,1)S(1)}, u32[]{:S(2)}, u32[]{:S(2)}) collective-permute-start(bf16[48,4096]{1,0:T(8,128)(2,1)S(1)} %slice.118), channel_id=1, source_target_pairs={{0,3},{1,0},{2,1},{3,2},{4,7},{5,4},{6,5},{7,6},{8,11},{9,8},{10,9... | collective-permute-start | bytes 1179656 | tf_op jit(solution)/shard_map/ppermute | solution.py:20
  45.9 50.3 %collective-permute-start.10 = (bf16[48,4096]{1,0:T(8,128)(2,1)S(1)}, bf16[48,4096]{1,0:T(8,128)(2,1)S(1)}, u32[]{:S(2)}, u32[]{:S(2)}) collective-permute-start(bf16[48,4096]{1,0:T(8,128)(2,1)S(1)} %slice.123), channel_id=1, source_target_pairs={{0,4},{1,5},{2,6},{3,7},{4,8},{5,9},{6,10},{7,11},{8,12},{9,13},{1... | collective-permute-start | bytes 1179656 | tf_op jit(solution)/shard_map/ppermute | solution.py:20
  48.5 48.5 %collective-permute-start.11 = (bf16[48,4096]{1,0:T(8,128)(2,1)S(1)}, bf16[48,4096]{1,0:T(8,128)(2,1)S(1)}, u32[]{:S(2)}, u32[]{:S(2)}) collective-permute-start(bf16[48,4096]{1,0:T(8,128)(2,1)S(1)} %slice.124), channel_id=1, source_target_pairs={{0,12},{1,13},{2,14},{3,15},{4,0},{5,1},{6,2},{7,3},{8,4},{9,5},{1... | collective-permute-start | bytes 1179656 | tf_op jit(solution)/shard_map/ppermute | solution.py:20
  93.0 117.9 %collective-permute-start.5 = (bf16[384,4096]{1,0:T(8,128)(2,1)}, bf16[384,4096]{1,0:T(8,128)(2,1)}, u32[]{:S(2)}, u32[]{:S(2)}) collective-permute-start(bf16[384,4096]{1,0:T(8,128)(2,1)} %constant_dynamic-update-slice_fusion), channel_id=1, source_target_pairs={{0,4},{1,5},{2,6},{3,7},{4,8},{5,9},{6,10},{7,11},{8,12},{9,13},{1... | collective-permute-start | bytes 9437192 | tf_op jit(solution)/shard_map/ppermute | solution.py:20
  94.5 110.7 %collective-permute-start.4 = (bf16[384,4096]{1,0:T(8,128)(2,1)}, bf16[384,4096]{1,0:T(8,128)(2,1)}, u32[]{:S(2)}, u32[]{:S(2)}) collective-permute-start(bf16[384,4096]{1,0:T(8,128)(2,1)} %constant_dynamic-update-slice_fusion), channel_id=1, source_target_pairs={{0,12},{1,13},{2,14},{3,15},{4,0},{5,1},{6,2},{7,3},{8,4},{9,5},{1... | collective-permute-start | bytes 9437192 | tf_op jit(solution)/shard_map/ppermute | solution.py:20
  98.7 126.4 %collective-permute-start.13 = (bf16[384,4096]{1,0:T(8,128)(2,1)}, bf16[384,4096]{1,0:T(8,128)(2,1)}, u32[]{:S(2)}, u32[]{:S(2)}) collective-permute-start(bf16[384,4096]{1,0:T(8,128)(2,1)} %constant_dynamic-update-slice_fusion.5), channel_id=1, source_target_pairs={{0,1},{1,2},{2,3},{3,0},{4,5},{5,6},{6,7},{7,4},{8,9},{9,10},{10,1... | collective-permute-start | bytes 9437192 | tf_op jit(solution)/shard_map/ppermute | solution.py:20
  99.0 120.7 %collective-permute-start.12 = (bf16[384,4096]{1,0:T(8,128)(2,1)}, bf16[384,4096]{1,0:T(8,128)(2,1)}, u32[]{:S(2)}, u32[]{:S(2)}) collective-permute-start(bf16[384,4096]{1,0:T(8,128)(2,1)} %constant_dynamic-update-slice_fusion.5), channel_id=1, source_target_pairs={{0,3},{1,0},{2,1},{3,2},{4,7},{5,4},{6,5},{7,6},{8,11},{9,8},{10,9... | collective-permute-start | bytes 9437192 | tf_op jit(solution)/shard_map/ppermute | solution.py:20
  121.1 4.5 %copy-start.6 = (bf16[256,8320]{1,0:T(8,128)(2,1)S(1)}, bf16[256,8320]{1,0:T(8,128)(2,1)}, u32[]{:S(2)}) copy-start(bf16[256,8320]{1,0:T(8,128)(2,1)} %reshape.35) | copy-start | bytes 12779524
  125.7 3.2 %copy-start.9 = (bf16[2,64,1024]{2,1,0:T(8,128)(2,1)S(1)}, bf16[2,64,1024]{2,1,0:T(8,128)(2,1)}, u32[]{:S(2)}) copy-start(bf16[2,64,1024]{2,1,0:T(8,128)(2,1)} %param.15) | copy-start | bytes 786436
  140.5 86.6 %slice-start.2 = ((s8[5242880]{0:T(1024)(128)(4,1)}), s8[1048576]{0:T(1024)(128)(4,1)S(1)}, s32[]{:S(2)}) async-start(s8[5242880]{0:T(1024)(128)(4,1)} %bitcast.68), calls=%async_computation.5 | async-start | bytes 2097152
  140.5 122.1 %all-to-all-start.1 = ((bf16[128,2,9216]{2,1,0:T(2,128)(2,1)}), bf16[128,2,9216]{2,1,0:T(2,128)(2,1)}, u32[]{:S(2)}, u32[]{:S(2)}) async-start(bf16[128,2,9216]{2,1,0:T(2,128)(2,1)} %reshape.38), calls=%async_computation.1 | async-start | bytes 9437184 | tf_op jit(solution)/shard_map/all_to_all | solution.py:141
  146.9 80.3 %slice-start.3 = ((s8[5242880]{0:T(1024)(128)(4,1)}), s8[4194304]{0:T(1024)(128)(4,1)S(1)}, s32[]{:S(2)}) async-start(s8[5242880]{0:T(1024)(128)(4,1)} %bitcast.68), calls=%async_computation.6 | async-start | bytes 8388608
  206.8 41.9 %collective-permute-start.7 = (bf16[192,4096]{1,0:T(8,128)(2,1)S(1)}, bf16[192,4096]{1,0:T(8,128)(2,1)S(1)}, u32[]{:S(2)}, u32[]{:S(2)}) collective-permute-start(bf16[192,4096]{1,0:T(8,128)(2,1)S(1)} %slice.122), channel_id=1, source_target_pairs={{0,12},{1,13},{2,14},{3,15},{4,0},{5,1},{6,2},{7,3},{8,4},{9,5},{1... | collective-permute-start | bytes 4718600 | tf_op jit(solution)/shard_map/ppermute | solution.py:20
  212.4 36.3 %collective-permute-start.6 = (bf16[192,4096]{1,0:T(8,128)(2,1)S(1)}, bf16[192,4096]{1,0:T(8,128)(2,1)S(1)}, u32[]{:S(2)}, u32[]{:S(2)}) collective-permute-start(bf16[192,4096]{1,0:T(8,128)(2,1)S(1)} %slice.121), channel_id=1, source_target_pairs={{0,4},{1,5},{2,6},{3,7},{4,8},{5,9},{6,10},{7,11},{8,12},{9,13},{1... | collective-permute-start | bytes 4718600 | tf_op jit(solution)/shard_map/ppermute | solution.py:20
  221.2 31.9 %collective-permute-start.15 = (bf16[192,4096]{1,0:T(8,128)(2,1)S(1)}, bf16[192,4096]{1,0:T(8,128)(2,1)S(1)}, u32[]{:S(2)}, u32[]{:S(2)}) collective-permute-start(bf16[192,4096]{1,0:T(8,128)(2,1)S(1)} %slice.126), channel_id=1, source_target_pairs={{0,3},{1,0},{2,1},{3,2},{4,7},{5,4},{6,5},{7,6},{8,11},{9,8},{10,9... | collective-permute-start | bytes 4718600 | tf_op jit(solution)/shard_map/ppermute | solution.py:20
  225.1 11.0 %slice-start = ((s8[5242880]{0:T(1024)(128)(4,1)}), s8[4194304]{0:T(1024)(128)(4,1)S(1)}, s32[]{:S(2)}) async-start(s8[5242880]{0:T(1024)(128)(4,1)} %bitcast.66), calls=%async_computation.3 | async-start | bytes 8388608
  226.9 9.3 %slice-start.1 = ((s8[5242880]{0:T(1024)(128)(4,1)}), s8[1048576]{0:T(1024)(128)(4,1)S(1)}, s32[]{:S(2)}) async-start(s8[5242880]{0:T(1024)(128)(4,1)} %bitcast.66), calls=%async_computation.4 | async-start | bytes 2097152
  226.9 28.1 %collective-permute-start.14 = (bf16[192,4096]{1,0:T(8,128)(2,1)S(1)}, bf16[192,4096]{1,0:T(8,128)(2,1)S(1)}, u32[]{:S(2)}, u32[]{:S(2)}) collective-permute-start(bf16[192,4096]{1,0:T(8,128)(2,1)S(1)} %slice.125), channel_id=1, source_target_pairs={{0,1},{1,2},{2,3},{3,0},{4,5},{5,6},{6,7},{7,4},{8,9},{9,10},{10,1... | collective-permute-start | bytes 4718600 | tf_op jit(solution)/shard_map/ppermute | solution.py:20
  251.4 6.4 %copy-start.7 = (f32[384,576]{1,0:T(8,128)S(1)}, f32[384,576]{1,0:T(8,128)}, u32[]{:S(2)}) copy-start(f32[384,576]{1,0:T(8,128)} %fusion.64) | copy-start | bytes 2654212
  251.4 6.4 %copy-start.8 = (f32[384,576]{1,0:T(8,128)S(1)}, f32[384,576]{1,0:T(8,128)}, u32[]{:S(2)}) copy-start(f32[384,576]{1,0:T(8,128)} %fusion.67) | copy-start | bytes 2654212
  262.6 30.4 %all-to-all-start.2 = ((bf16[16,96,576]{2,1,0:T(8,128)(2,1)}), bf16[16,96,576]{2,1,0:T(8,128)(2,1)}, u32[]{:S(2)}, u32[]{:S(2)}) async-start(bf16[16,96,576]{2,1,0:T(8,128)(2,1)} %bitcast.65), calls=%async_computation.2 | async-start | bytes 3932160 | tf_op jit(solution)/shard_map/all_to_all | solution.py:182
  274.8 25.4 %copy-start.1 = (bf16[2,64,8192]{2,1,0:T(8,128)(2,1)S(1)}, bf16[2,64,8192]{2,1,0:T(8,128)(2,1)}, u32[]{:S(2)}) copy-start(bf16[2,64,8192]{2,1,0:T(8,128)(2,1)} %param.14) | copy-start | bytes 6291460
  293.0 1.5 copy-start.2

commit v2 on v1

--- a/solution.py
+++ b/solution.py
@@ -127,6 +127,16 @@
     send_rows = jnp.dot(pick_table, marked, preferred_element_type=F32).astype(BF)
     send_rows = send_rows.reshape(devices, capacity, width + 128)
 
+    half = width // 2
+    along_z, along_y = (0, 1), (1, 0)
+    firsts = []
+    for part, one in enumerate((along_z, along_y)):
+        own = tokens[:, part * half : (part + 1) * half]
+        after, far, before = line_gather(own, one)
+        firsts.append((own, after, far, before))
+    own, after, far, before = firsts[1]
+    far, send_rows = lax.optimization_barrier((far, send_rows))
+    firsts[1] = own, after, far, before
     got_rows = lax.all_to_all(
         send_rows, ("grp", "tp"), split_axis=0, concat_axis=0, tiled=True
     ).reshape(slot_total, width + 128)
@@ -138,29 +148,21 @@
         adapter_value_up,
     )
     terms = jnp.concatenate([query_term, value_term], axis=1)
-    back = lax.all_to_all(
-        terms.reshape(devices, capacity, terms.shape[1]),
-        ("grp", "tp"),
-        split_axis=0,
-        concat_axis=0,
-        tiled=True,
-    )
-
-    half = width // 2
-    along_z, along_y = (0, 1), (1, 0)
-    gathered = []
-    for part, (one, two) in enumerate(((along_z, along_y), (along_y, along_z))):
-        own = tokens[:, part * half : (part + 1) * half]
-        after, far, before = line_gather(own, one)
-        line = jnp.concatenate([own, after, *far, before], axis=0)
-        after, before = line_sides(line, two)
-        gathered.append([line, after, before])
-    query_base_output, value_base_output, _ = lax.optimization_barrier(
-        (query_base_output, value_base_output, far[0][:16, :128])
+    terms = terms.reshape(devices, capacity, terms.shape[1])
+    slot_index, terms = lax.optimization_barrier((slot_index, terms))
+    back = lax.all_to_all(terms, ("grp", "tp"), split_axis=0, concat_axis=0, tiled=True)
+
+    lines = [jnp.concatenate([own, after, *far, before], axis=0) for own, after, far, before in firsts]
+    lines, query_base_output, value_base_output = lax.optimization_barrier(
+        (lines, query_base_output, value_base_output)
     )
     weights = jnp.concatenate([query_base_output, value_base_output], axis=1)
-    for blocks, two in zip(gathered, (along_y, along_z)):
-        blocks.insert(2, jnp.concatenate(line_far(blocks[1], blocks[2], two), axis=0))
+    gathered = [[line, *line_sides(line, two)] for line, two in zip(lines, (along_y, along_z))]
+    sides = [blocks[1:] for blocks in gathered]
+    sides, slot_index = lax.optimization_barrier((sides, slot_index))
+    for blocks, (after, before), two in zip(gathered, sides, (along_y, along_z)):
+        far = jnp.concatenate(line_far(after, before, two), axis=0)
+        blocks[1:] = [after, far, before]
     partial = []
     for part in range(2):
         w = weights[part * half : (part + 1) * half]
@@ -178,7 +180,8 @@
     projected = jnp.swapaxes(to_absolute(jnp.swapaxes(projected, 0, 1), place % side), 0, 1)
     projected, back = lax.optimization_barrier((projected, back))
     back = back.reshape(slot_total, back.shape[2])
-    row_terms = jnp.dot(pick_table.T, back, preferred_element_type=F32).astype(BF)
+    pick_row = (slot_index[:, None] == jnp.arange(slot_total, dtype=jnp.int32)[None, :]).astype(BF)
+    row_terms = jnp.dot(pick_row, back, preferred_element_type=F32).astype(BF)
     plain = lax.all_to_all(
         projected.reshape(members, row_count, both), "tp", split_axis=0, concat_axis=0, tiled=True
     )

time: 302 us -> 323 us (1.070)
  waiting for transfers between devices: 121 us -> 130 us
  local copies, waits for them, and re-layouts: 58.4 us -> 67 us
  matrix products: 51.6 us -> 57.9 us
  starting transfers between devices: 49.9 us -> 46.5 us
    all_to_all x1, waiting for transfers between devices: 0.01 us -> 22.4 us  [on_device(): lax.all_to_all(send_rows, ('grp', 'tp'), split_axis=0, concat_axis=0, til...]
    ppermute x16, waiting for transfers between devices: 107 us -> 94.1 us  [shift(): return lax.ppermute(x, 'tp', pairs)]
    dot_general x8, matrix products: 34.4 us -> 39.3 us  [on_device(): jnp.dot(x, w, preferred_element_type=F32).reshape(side, row_count, both)]
    unnamed x38 -> x48, local copies, waits for them, and re-layouts: 8.82 us -> 13.1 us
    all_to_all x1, starting transfers between devices: 10.1 us -> 6.13 us  [on_device(): lax.all_to_all(send_rows, ('grp', 'tp'), split_axis=0, concat_axis=0, til...]
  transfers between devices with their start and end apart: 19 -> 19, of which waited for: 7 -> 11; matrix products, arithmetic and copies ran while one was open for 39% -> 37% of each run, Pallas kernels for 0% -> 0%
where the time goes in v2:
time: 323 us; the launch traced here: 321 us
  waiting for transfers between devices  130 us (40%)
  local copies, waits for them, and re-layouts  67 us (21%)
  matrix products  57.9 us (18%)
  starting transfers between devices  46.5 us (14%)
  other arithmetic  12.6 us (4%)
  Pallas kernels  5.73 us (2%)
    ppermute x16, waiting for transfers between devices, shift(): return lax.ppermute(x, 'tp', pairs)  94.1 us
    dot_general x8, matrix products, on_device(): jnp.dot(x, w, preferred_element_type=F32).reshape(side, row_count, both)  39.3 us
    ppermute x16, starting transfers between devices, shift(): return lax.ppermute(x, 'tp', pairs)  27 us
    all_to_all x1, waiting for transfers between devices, on_device(): lax.all_to_all(send_rows, ('grp', 'tp'), split_axis=0, concat_axis=0, til...  22.4 us
    all_to_all x1, waiting for transfers between devices, on_device(): lax.all_to_all(projected.reshape(members, row_count, both), 'tp', split_a...  13.8 us
    unnamed x48, local copies, waits for them, and re-layouts  13.1 us
    dot_general x2, matrix products, apply_lowrank_adapters(): reduced = jnp.dot(rows, adapter_down_weight[i], preferred_element_type=F32)  7.71 us
    reshape x1, local copies, waits for them, and re-layouts, on_device(): terms = terms.reshape(devices, capacity, terms.shape[1])  7.62 us
  transfers between devices with their start and end apart: 19, of which 11 were waited for; matrix products, arithmetic and copies ran while one was open for 37% of the time, Pallas kernels for 0%

profile of v2, /device:TPU:6, one launch (start us, length us, event | category | flops | bytes accessed | tf_op | source)
XLA Modules:
  0.0 321.1 jit_solution(5304887195244350024)
XLA Ops:
  0.7 3.4 %fusion.61 = (bf16[96,4096]{1,0:T(8,128)(2,1)}, bf16[384,4096]{1,0:T(8,128)(2,1)}, bf16[384,4096]{1,0:T(8,128)(2,1)}, bf16[96,4096]{1,0:T(8,128)(2,1)}) fusion(bf16[96,8192]{1,0:T(8,128)(2,1)} %param.8), kind=kLoop, calls=%fused_computation.77 | loop fusion | bytes 4718592 | tf_op jit(solution)/shard_map/slice | solution.py:134
  4.0 1.6 collective-permute-start.5
  5.6 1.7 collective-permute-start.4
  7.3 4.0 %collective-permute-start = (bf16[96,4096]{1,0:T(8,128)(2,1)}, bf16[96,4096]{1,0:T(8,128)(2,1)}, u32[]{:S(2)}, u32[]{:S(2)}) collective-permute-start(bf16[96,4096]{1,0:T(8,128)(2,1)} %get-tuple-element.45), channel_id=1, source_target_pairs={{0,3},{1,0},{2,1},{3,2},{4,7},{5,4},{6,5},{7,6},{8,11},{9,8},{10,9... | collective-permute-start | bytes 2359304 | tf_op jit(solution)/shard_map/ppermute | solution.py:20
  11.6 4.6 %convolution_convert_fusion = bf16[256,8320]{1,0:T(8,128)(2,1)} fusion(bf16[96,128]{1,0:T(8,128)(2,1)S(1)} %broadcast_in_dim.36, bf16[96,8192]{1,0:T(8,128)(2,1)} %param.8, s32[96]{0:T(128)S(1)} %multiply_add_fusion), kind=kOutput, calls=%fused_computation | convolution fusion | flops 414294016 | bytes 5857664 | tf_op jit(solution)/shard_map/dot_general | solution.py:127
  16.2 7.2 %reshape.35 = bf16[128,2,8320]{2,1,0:T(2,128)(2,1)} reshape(bf16[256,8320]{1,0:T(8,128)(2,1)} %convolution_convert_fusion) | data formatting | bytes 8519680 | tf_op jit(solution)/shard_map/reshape | solution.py:128
  23.5 1.3 collective-permute-done.5
  25.2 1.0 slice.119
  26.2 3.0 collective-permute-start.7
  29.2 2.1 collective-permute-done.1
  31.3 1.8 slice.116
  33.1 1.8 slice.117
  34.9 3.2 %collective-permute-start.3 = (bf16[48,4096]{1,0:T(8,128)(2,1)}, bf16[48,4096]{1,0:T(8,128)(2,1)}, u32[]{:S(2)}, u32[]{:S(2)}) collective-permute-start(bf16[48,4096]{1,0:T(8,128)(2,1)} %slice.117), channel_id=1, source_target_pairs={{0,3},{1,0},{2,1},{3,2},{4,7},{5,4},{6,5},{7,6},{8,11},{9,8},{10,9... | collective-permute-start | bytes 1179656 | tf_op jit(solution)/shard_map/ppermute | solution.py:20
  38.1 2.1 constant_dynamic-update-slice_fusion.8
  40.2 2.1 constant_dynamic-update-slice_fusion.3
  42.3 6.1 %all-to-all-start = ((bf16[128,2,8320]{2,1,0:T(2,128)(2,1)}), bf16[128,2,8320]{2,1,0:T(2,128)(2,1)}, u32[]{:S(2)}, u32[]{:S(2)}) async-start(bf16[128,2,8320]{2,1,0:T(2,128)(2,1)} %reshape.35), calls=%async_computation | async-start | bytes 8519680 | tf_op jit(solution)/shard_map/all_to_all | solution.py:140
  49.2 1.8 constant_dynamic-update-slice_fusion.6
  51.0 1.8 constant_dynamic-update-slice_fusion.2
  52.8 1.8 constant_dynamic-update-slice_fusion.1
  54.6 0.9 constant_dynamic-update-slice_fusion.5
  55.5 2.1 constant_dynamic-update-slice_fusion
  57.6 3.4 %collective-permute-start.10 = (bf16[384,4096]{1,0:T(8,128)(2,1)}, bf16[384,4096]{1,0:T(8,128)(2,1)}, u32[]{:S(2)}, u32[]{:S(2)}) collective-permute-start(bf16[384,4096]{1,0:T(8,128)(2,1)} %constant_dynamic-update-slice_fusion.5), channel_id=1, source_target_pairs={{0,3},{1,0},{2,1},{3,2},{4,7},{5,4},{6,5},{7,6},{8,11},{9,8},{10,9... | collective-permute-start | bytes 9437192 | tf_op jit(solution)/shard_map/ppermute | solution.py:20
  61.0 2.9 collective-permute-start.8
  63.9 2.7 copy.46
  66.6 5.0 %pad_maximum_fusion = (bf16[4096,576]{1,0:T(8,128)(2,1)S(1)}, bf16[4096,576]{1,0:T(8,128)(2,1)S(1)}) fusion(bf16[8192,64]{1,0:T(8,128)(2,1)} %copy.46, bf16[8192,512]{1,0:T(8,128)(2,1)} %param.11), kind=kLoop, calls=%fused_computation.7 | loop fusion | flops 18874368 | bytes 18874368 | tf_op jit(solution)/shard_map/concatenate | solution.py:159
  71.6 3.5 %fusion.67 = f32[384,576]{1,0:T(8,128)} fusion(bf16[384,4096]{1,0:T(8,128)(2,1)S(1)} %copy-done.12, bf16[4096,576]{1,0:T(8,128)(2,1)S(1)} %get-tuple-element.36), kind=kOutput, calls=%fused_computation.83 | convolution fusion | flops 1811939328 | bytes 8749056 | tf_op jit(solution)/shard_map/dot_general | solution.py:172
  75.2 1.2 copy-done.3
  76.4 3.6 %fusion.64 = f32[384,576]{1,0:T(8,128)} fusion(bf16[384,4096]{1,0:T(8,128)(2,1)S(1)} %copy-done.11, bf16[4096,576]{1,0:T(8,128)(2,1)S(1)} %get-tuple-element.37), kind=kOutput, calls=%fused_computation.80 | convolution fusion | flops 1811939328 | bytes 8749056 | tf_op jit(solution)/shard_map/dot_general | solution.py:172
  80.0 22.4 %all-to-all-done = bf16[128,2,8320]{2,1,0:T(2,128)(2,1)} async-done(((bf16[128,2,8320]{2,1,0:T(2,128)(2,1)}), bf16[128,2,8320]{2,1,0:T(2,128)(2,1)}, u32[]{:S(2)}, u32[]{:S(2)}) %all-to-all-start) | async-done | bytes 4259872 | tf_op jit(solution)/shard_map/all_to_all | solution.py:140
  102.4 7.2 %reshape.36 = bf16[256,8320]{1,0:T(8,128)(2,1)} reshape(bf16[128,2,8320]{2,1,0:T(2,128)(2,1)} %all-to-all-done) | data formatting | bytes 8519680 | tf_op jit(solution)/shard_map/reshape | solution.py:142
  109.6 1.0 compare_reduce_fusion.1
  110.6 4.5 %fusion.30 = bf16[256,128]{0,1:T(8,128)(2,1)S(1)} fusion(bf16[2,8192,128]{2,1,0:T(8,128)(2,1)} %param.13, bf16[256,8320]{1,0:T(8,128)(2,1)} %reshape.36, pred[256]{0:T(512)(128)(4,1)S(1)} %get-tuple-element.34), kind=kOutput, calls=%fused_computation.40 | convolution fusion | flops 536936448 | bytes 6357248 | tf_op jit(solution)/shard_map/dot_general | solution.py:49
  115.2 3.2 fusion.40
  118.7 1.3 fusion
  120.0 2.4 pad_maximum_fusion.1
  122.4 7.6 %reshape.39 = bf16[128,2,9216]{2,1,0:T(2,128)(2,1)} reshape(bf16[256,9216]{1,0:T(8,128)(2,1)} %pad_maximum_fusion.1) | data formatting | bytes 9437184 | tf_op jit(solution)/shard_map/reshape | solution.py:151
  130.1 33.5 %collective-permute-done.10 = bf16[384,4096]{1,0:T(8,128)(2,1)} collective-permute-done((bf16[384,4096]{1,0:T(8,128)(2,1)}, bf16[384,4096]{1,0:T(8,128)(2,1)}, u32[]{:S(2)}, u32[]{:S(2)}) %collective-permute-start.10) | collective-permute-done | bytes 3145760 | tf_op jit(solution)/shard_map/ppermute | solution.py:20
  163.6 1.3 collective-permute-done.11
  165.5 7.0 %fusion.68 = f32[384,576]{1,0:T(8,128)} fusion(bf16[384,4096]{1,0:T(8,128)(2,1)} %collective-permute-done.10, bf16[4096,576]{1,0:T(8,128)(2,1)} %copy-done.4), kind=kOutput, calls=%fused_computation.84 | convolution fusion | flops 1811939328 | bytes 8749056 | tf_op jit(solution)/shard_map/dot_general | solution.py:172
  172.5 1.5 slice.107
  174.1 2.7 slice.106
  176.8 1.2 collective-permute-start.14
  178.0 2.5 collective-permute-start.15
  180.4 5.5 %fusion.69 = f32[384,576]{1,0:T(8,128)} fusion(bf16[384,4096]{1,0:T(8,128)(2,1)} %collective-permute-done.11, bf16[4096,576]{1,0:T(8,128)(2,1)S(1)} %bitcast.69), kind=kOutput, calls=%fused_computation.85 | convolution fusion | flops 1811939328 | bytes 8749056 | tf_op jit(solution)/shard_map/dot_general | solution.py:172
  185.9 2.8 slice.103
  189.2 2.7 slice.104
  191.9 2.8 collective-permute-start.13
  194.6 6.3 %all-to-all-start.1 = ((bf16[128,2,9216]{2,1,0:T(2,128)(2,1)}), bf16[128,2,9216]{2,1,0:T(2,128)(2,1)}, u32[]{:S(2)}, u32[]{:S(2)}) async-start(bf16[128,2,9216]{2,1,0:T(2,128)(2,1)} %reshape.39), calls=%async_computation.1 | async-start | bytes 9437184 | tf_op jit(solution)/shard_map/all_to_all | solution.py:153
  201.0 6.2 %fusion.65 = f32[384,576]{1,0:T(8,128)S(1)} fusion(bf16[384,4096]{1,0:T(8,128)(2,1)} %collective-permute-done.8, bf16[4096,576]{1,0:T(8,128)(2,1)} %copy-done.3), kind=kOutput, calls=%fused_computation.81 | convolution fusion | flops 1811939328 | bytes 8749056 | tf_op jit(solution)/shard_map/dot_general | solution.py:172
  207.2 4.6 %fusion.66 = f32[384,576]{1,0:T(8,128)S(1)} fusion(bf16[384,4096]{1,0:T(8,128)(2,1)} %collective-permute-done.9, bf16[4096,576]{1,0:T(8,128)(2,1)S(1)} %bitcast.67), kind=kOutput, calls=%fused_computation.82 | convolution fusion | flops 1811939328 | bytes 8749056 | tf_op jit(solution)/shard_map/dot_general | solution.py:172
  211.8 35.9 %collective-permute-done.14 = bf16[192,4096]{1,0:T(8,128)(2,1)} collective-permute-done((bf16[192,4096]{1,0:T(8,128)(2,1)}, bf16[192,4096]{1,0:T(8,128)(2,1)}, u32[]{:S(2)}, u32[]{:S(2)}) %collective-permute-start.14) | collective-permute-done | bytes 1572896 | tf_op jit(solution)/shard_map/ppermute | solution.py:20
  247.7 6.1 %collective-permute-done.15 = bf16[192,4096]{1,0:T(8,128)(2,1)} collective-permute-done((bf16[192,4096]{1,0:T(8,128)(2,1)S(1)}, bf16[192,4096]{1,0:T(8,128)(2,1)}, u32[]{:S(2)}, u32[]{:S(2)}) %collective-permute-start.15) | collective-permute-done | bytes 1572896 | tf_op jit(solution)/shard_map/ppermute | solution.py:20
  253.8 4.5 %fusion.11 = f32[384,576]{1,0:T(8,128)S(1)} fusion(bf16[4096,576]{1,0:T(8,128)(2,1)S(1)} %bitcast.71, bf16[192,4096]{1,0:T(8,128)(2,1)} %collective-permute-done.15, bf16[192,4096]{1,0:T(8,128)(2,1)} %collective-permute-done.14), kind=kOutput, calls=%fused_computation.20 | convolution fusion | flops 1818230784 | bytes 8749056 | tf_op jit(solution)/shard_map/dot_general | solution.py:172
  258.4 8.3 %collective-permute-done.12 = bf16[192,4096]{1,0:T(8,128)(2,1)} collective-permute-done((bf16[192,4096]{1,0:T(8,128)(2,1)}, bf16[192,4096]{1,0:T(8,128)(2,1)}, u32[]{:S(2)}, u32[]{:S(2)}) %collective-permute-start.12) | collective-permute-done | bytes 1572896 | tf_op jit(solution)/shard_map/ppermute | solution.py:20
  266.6 5.0 %collective-permute-done.13 = bf16[192,4096]{1,0:T(8,128)(2,1)} collective-permute-done((bf16[192,4096]{1,0:T(8,128)(2,1)}, bf16[192,4096]{1,0:T(8,128)(2,1)}, u32[]{:S(2)}, u32[]{:S(2)}) %collective-permute-start.13) | collective-permute-done | bytes 1572896 | tf_op jit(solution)/shard_map/ppermute | solution.py:20
  271.6 4.5 %fusion.7 = f32[384,576]{1,0:T(8,128)S(1)} fusion(bf16[4096,576]{1,0:T(8,128)(2,1)S(1)} %bitcast.67, bf16[192,4096]{1,0:T(8,128)(2,1)} %collective-permute-done.13, bf16[192,4096]{1,0:T(8,128)(2,1)} %collective-permute-done.12), kind=kOutput, calls=%fused_computation.16 | convolution fusion | flops 1818230784 | bytes 8749056 | tf_op jit(solution)/shard_map/dot_general | solution.py:172
  276.9 1.0 maximum_select_fusion
  279.2 1.7 fusion.20
  280.9 7.0 %all-to-all-start.2 = ((bf16[16,96,576]{2,1,0:T(8,128)(2,1)}), bf16[16,96,576]{2,1,0:T(8,128)(2,1)}, u32[]{:S(2)}, u32[]{:S(2)}) async-start(bf16[16,96,576]{2,1,0:T(8,128)(2,1)} %bitcast.65), calls=%async_computation.2 | async-start | bytes 3932160 | tf_op jit(solution)/shard_map/all_to_all | solution.py:185
  288.0 7.5 %reshape.41 = bf16[256,9216]{1,0:T(8,128)(2,1)} reshape(bf16[128,2,9216]{2,1,0:T(2,128)(2,1)} %all-to-all-done.1) | data formatting | bytes 9437184 | tf_op jit(solution)/shard_map/reshape | solution.py:182
  295.5 4.6 %convolution_convert_fusion.1.query_term_ref.value_term_ref = bf16[96,9216]{1,0:T(8,128)(2,1)} fusion(bf16[256,9216]{1,0:T(8,128)(2,1)} %reshape.41, s32[96]{0:T(128)S(1)} %multiply_add_fusion), kind=kOutput, calls=%fused_computation.2 | convolution fusion | flops 453894144 | bytes 6488448 | tf_op jit(solution)/shard_map/dot_general | solution.py:184
  300.1 13.8 %all-to-all-done.2.plain_ref = bf16[16,96,576]{2,1,0:T(8,128)(2,1)} async-done(((bf16[16,96,576]{2,1,0:T(8,128)(2,1)}), bf16[16,96,576]{2,1,0:T(8,128)(2,1)}, u32[]{:S(2)}, u32[]{:S(2)}) %all-to-all-start.2) | async-done | bytes 1769504 | tf_op jit(solution)/shard_map/all_to_all | solution.py:185
  313.9 1.5 copy-done.2
  315.4 5.7 %shard_map.95 = (bf16[96,8192]{1,0:T(8,128)(2,1)}, bf16[96,1024]{1,0:T(8,128)(2,1)}) custom-call(bf16[16,96,576]{2,1,0:T(8,128)(2,1)} %all-to-all-done.2.plain_ref, bf16[96,9216]{1,0:T(8,128)(2,1)S(1)} %copy-done.2, bf16[96,9216]{1,0:T(8,128)(2,1)S(1)} %copy-done.2), custom_call_target="tpu_custom_call" | custom-call | flops 884736 | bytes 5308416 | tf_op jit(solution)/shard_map/pallas_call | solution.py:75
  (75 shorter events, 5.0 us)
Async XLA Ops:
  0.6 118.1 %copy-start = (bf16[2,64,8192]{2,1,0:T(8,128)(2,1)S(1)}, bf16[2,64,8192]{2,1,0:T(8,128)(2,1)}, u32[]{:S(2)}) copy-start(bf16[2,64,8192]{2,1,0:T(8,128)(2,1)} %param.14) | copy-start | bytes 6291460
  0.6 10.7 %copy-start.14 = (s32[96,1]{0,1:T(1,128)S(1)}, s32[96,1]{0,1:T(1,128)}, u32[]{:S(2)}) copy-start(s32[96,1]{0,1:T(1,128)} %param.9) | copy-start | bytes 1156
  0.7 10.8 %copy-start.13 = (s32[96,1]{0,1:T(1,128)S(1)}, s32[96,1]{0,1:T(1,128)}, u32[]{:S(2)}) copy-start(s32[96,1]{0,1:T(1,128)} %param.10) | copy-start | bytes 1156
  4.0 20.8 %collective-permute-start.5 = (bf16[96,4096]{1,0:T(8,128)(2,1)}, bf16[96,4096]{1,0:T(8,128)(2,1)S(1)}, u32[]{:S(2)}, u32[]{:S(2)}) collective-permute-start(bf16[96,4096]{1,0:T(8,128)(2,1)} %get-tuple-element.42), channel_id=1, source_target_pairs={{0,4},{1,5},{2,6},{3,7},{4,8},{5,9},{6,10},{7,11},{8,12},{9,13},{1... | collective-permute-start | bytes 2359304 | tf_op jit(solution)/shard_map/ppermute | solution.py:20
  5.6 19.6 %collective-permute-start.4 = (bf16[96,4096]{1,0:T(8,128)(2,1)}, bf16[96,4096]{1,0:T(8,128)(2,1)}, u32[]{:S(2)}, u32[]{:S(2)}) collective-permute-start(bf16[96,4096]{1,0:T(8,128)(2,1)} %get-tuple-element.42), channel_id=1, source_target_pairs={{0,12},{1,13},{2,14},{3,15},{4,0},{5,1},{6,2},{7,3},{8,4},{9,5},{1... | collective-permute-start | bytes 2359304 | tf_op jit(solution)/shard_map/ppermute | solution.py:20
  7.3 25.8 %collective-permute-start = (bf16[96,4096]{1,0:T(8,128)(2,1)}, bf16[96,4096]{1,0:T(8,128)(2,1)}, u32[]{:S(2)}, u32[]{:S(2)}) collective-permute-start(bf16[96,4096]{1,0:T(8,128)(2,1)} %get-tuple-element.45), channel_id=1, source_target_pairs={{0,3},{1,0},{2,1},{3,2},{4,7},{5,4},{6,5},{7,6},{8,11},{9,8},{10,9... | collective-permute-start | bytes 2359304 | tf_op jit(solution)/shard_map/ppermute | solution.py:20
  11.3 20.0 %collective-permute-start.1 = (bf16[96,4096]{1,0:T(8,128)(2,1)}, bf16[96,4096]{1,0:T(8,128)(2,1)}, u32[]{:S(2)}, u32[]{:S(2)}) collective-permute-start(bf16[96,4096]{1,0:T(8,128)(2,1)} %get-tuple-element.45), channel_id=1, source_target_pairs={{0,1},{1,2},{2,3},{3,0},{4,5},{5,6},{6,7},{7,4},{8,9},{9,10},{10,1... | collective-permute-start | bytes 2359304 | tf_op jit(solution)/shard_map/ppermute | solution.py:20
  24.8 17.5 %collective-permute-start.6 = (bf16[48,4096]{1,0:T(8,128)(2,1)S(1)}, bf16[48,4096]{1,0:T(8,128)(2,1)S(1)}, u32[]{:S(2)}, u32[]{:S(2)}) collective-permute-start(bf16[48,4096]{1,0:T(8,128)(2,1)S(1)} %slice.118), channel_id=1, source_target_pairs={{0,4},{1,5},{2,6},{3,7},{4,8},{5,9},{6,10},{7,11},{8,12},{9,13},{1... | collective-permute-start | bytes 1179656 | tf_op jit(solution)/shard_map/ppermute | solution.py:20
  26.2 16.1 %collective-permute-start.7 = (bf16[48,4096]{1,0:T(8,128)(2,1)S(1)}, bf16[48,4096]{1,0:T(8,128)(2,1)}, u32[]{:S(2)}, u32[]{:S(2)}) collective-permute-start(bf16[48,4096]{1,0:T(8,128)(2,1)S(1)} %slice.119), channel_id=1, source_target_pairs={{0,12},{1,13},{2,14},{3,15},{4,0},{5,1},{6,2},{7,3},{8,4},{9,5},{1... | collective-permute-start | bytes 1179656 | tf_op jit(solution)/shard_map/ppermute | solution.py:20
  33.1 17.9 %collective-permute-start.2 = (bf16[48,4096]{1,0:T(8,128)(2,1)}, bf16[48,4096]{1,0:T(8,128)(2,1)}, u32[]{:S(2)}, u32[]{:S(2)}) collective-permute-start(bf16[48,4096]{1,0:T(8,128)(2,1)} %slice.116), channel_id=1, source_target_pairs={{0,1},{1,2},{2,3},{3,0},{4,5},{5,6},{6,7},{7,4},{8,9},{9,10},{10,1... | collective-permute-start | bytes 1179656 | tf_op jit(solution)/shard_map/ppermute | solution.py:20
  34.9 17.9 %collective-permute-start.3 = (bf16[48,4096]{1,0:T(8,128)(2,1)}, bf16[48,4096]{1,0:T(8,128)(2,1)}, u32[]{:S(2)}, u32[]{:S(2)}) collective-permute-start(bf16[48,4096]{1,0:T(8,128)(2,1)} %slice.117), channel_id=1, source_target_pairs={{0,3},{1,0},{2,1},{3,2},{4,7},{5,4},{6,5},{7,6},{8,11},{9,8},{10,9... | collective-permute-start | bytes 1179656 | tf_op jit(solution)/shard_map/ppermute | solution.py:20
  42.3 60.1 %all-to-all-start = ((bf16[128,2,8320]{2,1,0:T(2,128)(2,1)}), bf16[128,2,8320]{2,1,0:T(2,128)(2,1)}, u32[]{:S(2)}, u32[]{:S(2)}) async-start(bf16[128,2,8320]{2,1,0:T(2,128)(2,1)} %reshape.35), calls=%async_computation | async-start | bytes 8519680 | tf_op jit(solution)/shard_map/all_to_all | solution.py:140
  57.6 106.0 %collective-permute-start.10 = (bf16[384,4096]{1,0:T(8,128)(2,1)}, bf16[384,4096]{1,0:T(8,128)(2,1)}, u32[]{:S(2)}, u32[]{:S(2)}) collective-permute-start(bf16[384,4096]{1,0:T(8,128)(2,1)} %constant_dynamic-update-slice_fusion.5), channel_id=1, source_target_pairs={{0,3},{1,0},{2,1},{3,2},{4,7},{5,4},{6,5},{7,6},{8,11},{9,8},{10,9... | collective-permute-start | bytes 9437192 | tf_op jit(solution)/shard_map/ppermute | solution.py:20
  61.0 103.9 %collective-permute-start.11 = (bf16[384,4096]{1,0:T(8,128)(2,1)}, bf16[384,4096]{1,0:T(8,128)(2,1)}, u32[]{:S(2)}, u32[]{:S(2)}) collective-permute-start(bf16[384,4096]{1,0:T(8,128)(2,1)} %constant_dynamic-update-slice_fusion.5), channel_id=1, source_target_pairs={{0,1},{1,2},{2,3},{3,0},{4,5},{5,6},{6,7},{7,4},{8,9},{9,10},{10,1... | collective-permute-start | bytes 9437192 | tf_op jit(solution)/shard_map/ppermute | solution.py:20
  61.0 104.6 %collective-permute-start.8 = (bf16[384,4096]{1,0:T(8,128)(2,1)}, bf16[384,4096]{1,0:T(8,128)(2,1)}, u32[]{:S(2)}, u32[]{:S(2)}) collective-permute-start(bf16[384,4096]{1,0:T(8,128)(2,1)} %constant_dynamic-update-slice_fusion), channel_id=1, source_target_pairs={{0,12},{1,13},{2,14},{3,15},{4,0},{5,1},{6,2},{7,3},{8,4},{9,5},{1... | collective-permute-start | bytes 9437192 | tf_op jit(solution)/shard_map/ppermute | solution.py:20
  63.9 101.7 %collective-permute-start.9 = (bf16[384,4096]{1,0:T(8,128)(2,1)}, bf16[384,4096]{1,0:T(8,128)(2,1)}, u32[]{:S(2)}, u32[]{:S(2)}) collective-permute-start(bf16[384,4096]{1,0:T(8,128)(2,1)} %constant_dynamic-update-slice_fusion), channel_id=1, source_target_pairs={{0,4},{1,5},{2,6},{3,7},{4,8},{5,9},{6,10},{7,11},{8,12},{9,13},{1... | collective-permute-start | bytes 9437192 | tf_op jit(solution)/shard_map/ppermute | solution.py:20
  66.6 5.0 %copy-start.12 = (bf16[384,4096]{1,0:T(8,128)(2,1)S(1)}, bf16[384,4096]{1,0:T(8,128)(2,1)}, u32[]{:S(2)}) copy-start(bf16[384,4096]{1,0:T(8,128)(2,1)} %constant_dynamic-update-slice_fusion.5) | copy-start | bytes 9437188
  71.6 3.6 %copy-start.4 = (bf16[4096,576]{1,0:T(8,128)(2,1)}, bf16[4096,576]{1,0:T(8,128)(2,1)S(1)}, u32[]{:S(2)}) copy-start(bf16[4096,576]{1,0:T(8,128)(2,1)S(1)} %get-tuple-element.36) | copy-start | bytes 14155780
  71.6 4.8 %copy-start.3 = (bf16[4096,576]{1,0:T(8,128)(2,1)}, bf16[4096,576]{1,0:T(8,128)(2,1)S(1)}, u32[]{:S(2)}) copy-start(bf16[4096,576]{1,0:T(8,128)(2,1)S(1)} %get-tuple-element.37) | copy-start | bytes 14155780
  71.6 4.8 %copy-start.11 = (bf16[384,4096]{1,0:T(8,128)(2,1)S(1)}, bf16[384,4096]{1,0:T(8,128)(2,1)}, u32[]{:S(2)}) copy-start(bf16[384,4096]{1,0:T(8,128)(2,1)} %constant_dynamic-update-slice_fusion) | copy-start | bytes 9437188
  110.6 4.5 %copy-start.5 = (bf16[256,8320]{1,0:T(8,128)(2,1)S(1)}, bf16[256,8320]{1,0:T(8,128)(2,1)}, u32[]{:S(2)}) copy-start(bf16[256,8320]{1,0:T(8,128)(2,1)} %reshape.36) | copy-start | bytes 12779524
  115.2 3.2 %copy-start.10 = (bf16[2,64,1024]{2,1,0:T(8,128)(2,1)S(1)}, bf16[2,64,1024]{2,1,0:T(8,128)(2,1)}, u32[]{:S(2)}) copy-start(bf16[2,64,1024]{2,1,0:T(8,128)(2,1)} %param.15) | copy-start | bytes 786436
  122.4 58.0 %slice-start.2 = ((s8[5242880]{0:T(1024)(128)(4,1)}), s8[1048576]{0:T(1024)(128)(4,1)S(1)}, s32[]{:S(2)}) async-start(s8[5242880]{0:T(1024)(128)(4,1)} %bitcast.68), calls=%async_computation.5 | async-start | bytes 2097152
  130.1 50.4 %slice-start.3 = ((s8[5242880]{0:T(1024)(128)(4,1)}), s8[4194304]{0:T(1024)(128)(4,1)S(1)}, s32[]{:S(2)}) async-start(s8[5242880]{0:T(1024)(128)(4,1)} %bitcast.68), calls=%async_computation.6 | async-start | bytes 8388608
  176.8 70.9 %collective-permute-start.14 = (bf16[192,4096]{1,0:T(8,128)(2,1)}, bf16[192,4096]{1,0:T(8,128)(2,1)}, u32[]{:S(2)}, u32[]{:S(2)}) collective-permute-start(bf16[192,4096]{1,0:T(8,128)(2,1)} %slice.106), channel_id=1, source_target_pairs={{0,1},{1,2},{2,3},{3,0},{4,5},{5,6},{6,7},{7,4},{8,9},{9,10},{10,1... | collective-permute-start | bytes 4718600 | tf_op jit(solution)/shard_map/ppermute | solution.py:20
  178.0 75.8 %collective-permute-start.15 = (bf16[192,4096]{1,0:T(8,128)(2,1)S(1)}, bf16[192,4096]{1,0:T(8,128)(2,1)}, u32[]{:S(2)}, u32[]{:S(2)}) collective-permute-start(bf16[192,4096]{1,0:T(8,128)(2,1)S(1)} %slice.107), channel_id=1, source_target_pairs={{0,3},{1,0},{2,1},{3,2},{4,7},{5,4},{6,5},{7,6},{8,11},{9,8},{10,9... | collective-permute-start | bytes 4718600 | tf_op jit(solution)/shard_map/ppermute | solution.py:20
  188.7 77.9 %collective-permute-start.12 = (bf16[192,4096]{1,0:T(8,128)(2,1)}, bf16[192,4096]{1,0:T(8,128)(2,1)}, u32[]{:S(2)}, u32[]{:S(2)}) collective-permute-start(bf16[192,4096]{1,0:T(8,128)(2,1)} %slice.103), channel_id=1, source_target_pairs={{0,4},{1,5},{2,6},{3,7},{4,8},{5,9},{6,10},{7,11},{8,12},{9,13},{1... | collective-permute-start | bytes 4718600 | tf_op jit(solution)/shard_map/ppermute | solution.py:20
  191.9 79.8 %collective-permute-start.13 = (bf16[192,4096]{1,0:T(8,128)(2,1)}, bf16[192,4096]{1,0:T(8,128)(2,1)}, u32[]{:S(2)}, u32[]{:S(2)}) collective-permute-start(bf16[192,4096]{1,0:T(8,128)(2,1)} %slice.104), channel_id=1, source_target_pairs={{0,12},{1,13},{2,14},{3,15},{4,0},{5,1},{6,2},{7,3},{8,4},{9,5},{1... | collective-permute-start | bytes 4718600 | tf_op jit(solution)/shard_map/ppermute | solution.py:20
  194.6 12.5 %slice-start = ((s8[5242880]{0:T(1024)(128)(4,1)}), s8[1048576]{0:T(1024)(128)(4,1)S(1)}, s32[]{:S(2)}) async-start(s8[5242880]{0:T(1024)(128)(4,1)} %bitcast.66), calls=%async_computation.3 | async-start | bytes 2097152
  194.6 86.3 %all-to-all-start.1 = ((bf16[128,2,9216]{2,1,0:T(2,128)(2,1)}), bf16[128,2,9216]{2,1,0:T(2,128)(2,1)}, u32[]{:S(2)}, u32[]{:S(2)}) async-start(bf16[128,2,9216]{2,1,0:T(2,128)(2,1)} %reshape.39), calls=%async_computation.1 | async-start | bytes 9437184 | tf_op jit(solution)/shard_map/all_to_all | solution.py:153
  201.0 6.2 %slice-start.1 = ((s8[5242880]{0:T(1024)(128)(4,1)}), s8[4194304]{0:T(1024)(128)(4,1)S(1)}, s32[]{:S(2)}) async-start(s8[5242880]{0:T(1024)(128)(4,1)} %bitcast.66), calls=%async_computation.4 | async-start | bytes 8388608
  201.0 52.8 %slice-start.4 = ((s8[5242880]{0:T(1024)(128)(4,1)}), s8[4194304]{0:T(1024)(128)(4,1)S(1)}, s32[]{:S(2)}) async-start(s8[5242880]{0:T(1024)(128)(4,1)} %bitcast.70), calls=%async_computation.7 | async-start | bytes 8388608
  207.2 46.6 %slice-start.5 = ((s8[5242880]{0:T(1024)(128)(4,1)}), s8[1048576]{0:T(1024)(128)(4,1)S(1)}, s32[]{:S(2)}) async-start(s8[5242880]{0:T(1024)(128)(4,1)} %bitcast.70), calls=%async_computation.8 | async-start | bytes 2097152
  258.3 17.8 %copy-start.6 = (f32[384,576]{1,0:T(8,128)S(1)}, f32[384,576]{1,0:T(8,128)}, u32[]{:S(2)}) copy-start(f32[384,576]{1,0:T(8,128)} %fusion.67) | copy-start | bytes 2654212
  258.3 17.8 %copy-start.7 = (f32[384,576]{1,0:T(8,128)S(1)}, f32[384,576]{1,0:T(8,128)}, u32[]{:S(2)}) copy-start(f32[384,576]{1,0:T(8,128)} %fusion.64) | copy-start | bytes 2654212
  258.3 17.8 %copy-start.8 = (f32[384,576]{1,0:T(8,128)S(1)}, f32[384,576]{1,0:T(8,128)}, u32[]{:S(2)}) copy-start(f32[384,576]{1,0:T(8,128)} %fusion.68) | copy-start | bytes 2654212
  258.3 17.8 %copy-start.9 = (f32[384,576]{1,0:T(8,128)S(1)}, f32[384,576]{1,0:T(8,128)}, u32[]{:S(2)}) copy-start(f32[384,576]{1,0:T(8,128)} %fusion.69) | copy-start | bytes 2654212
  280.9 32.9 %all-to-all-start.2 = ((bf16[16,96,576]{2,1,0:T(8,128)(2,1)}), bf16[16,96,576]{2,1,0:T(8,128)(2,1)}, u32[]{:S(2)}, u32[]{:S(2)}) async-start(bf16[16,96,576]{2,1,0:T(8,128)(2,1)} %bitcast.65), calls=%async_computation.2 | async-start | bytes 3932160 | tf_op jit(solution)/shard_map/all_to_all | solution.py:185
  295.5 25.6 %copy-start.1 = (bf16[2,64,8192]{2,1,0:T(8,128)(2,1)S(1)}, bf16[2,64,8192]{2,1,0:T(8,128)(2,1)}, u32[]{:S(2)}) copy-start(bf16[2,64,8192]{2,1,0:T(8,128)(2,1)} %param.14) | copy-start | bytes 6291460
  313.9 1.5 copy-start.2

commit v3 on v2

--- a/solution.py
+++ b/solution.py
@@ -159,9 +159,13 @@
     weights = jnp.concatenate([query_base_output, value_base_output], axis=1)
     gathered = [[line, *line_sides(line, two)] for line, two in zip(lines, (along_y, along_z))]
     sides = [blocks[1:] for blocks in gathered]
-    sides, slot_index = lax.optimization_barrier((sides, slot_index))
-    for blocks, (after, before), two in zip(gathered, sides, (along_y, along_z)):
-        far = jnp.concatenate(line_far(after, before, two), axis=0)
+    sides = [list(x) for x in sides]
+    fars = [
+        jnp.concatenate(line_far(after, before, two), axis=0)
+        for (after, before), two in zip(sides, (along_y, along_z))
+    ]
+    sides[1][1], back = lax.optimization_barrier((sides[1][1], back))
+    for blocks, (after, before), far in zip(gathered, sides, fars):
         blocks[1:] = [after, far, before]
     partial = []
     for part in range(2):

time: 323 us -> 320 us (level)
  waiting for transfers between devices: 130 us -> 125 us
  other arithmetic: 12.6 us -> 16.9 us
  local copies, waits for them, and re-layouts: 67 us -> 63.3 us
    ppermute x16, waiting for transfers between devices: 94.1 us -> 85.8 us  [shift(): return lax.ppermute(x, 'tp', pairs)]
    concatenate x1, other arithmetic: 5 us -> 9.12 us  [on_device(): weights = jnp.concatenate([query_base_output, value_base_output], axis=1)]
    all_to_all x1, waiting for transfers between devices: 13.8 us -> 17.2 us  [on_device(): lax.all_to_all(projected.reshape(members, row_count, both), 'tp', split_a...]
    unnamed x48 -> x46, local copies, waits for them, and re-layouts: 13.1 us -> 12.8 us
  transfers between devices with their start and end apart: 19 -> 19, of which waited for: 11 -> 5; matrix products, arithmetic and copies ran while one was open for 37% -> 39% of each run, Pallas kernels for 0% -> 0%
where the time goes in v3:
time: 320 us; the launch traced here: 319 us
  waiting for transfers between devices  125 us (39%)
  local copies, waits for them, and re-layouts  63.3 us (20%)
  matrix products  59.5 us (19%)
  starting transfers between devices  46.6 us (15%)
  other arithmetic  16.9 us (5%)
  Pallas kernels  5.73 us (2%)
    ppermute x16, waiting for transfers between devices, shift(): return lax.ppermute(x, 'tp', pairs)  85.8 us
    dot_general x8, matrix products, on_device(): jnp.dot(x, w, preferred_element_type=F32).reshape(side, row_count, both)  40.9 us
    ppermute x16, starting transfers between devices, shift(): return lax.ppermute(x, 'tp', pairs)  29.6 us
    all_to_all x1, waiting for transfers between devices, on_device(): lax.all_to_all(send_rows, ('grp', 'tp'), split_axis=0, concat_axis=0, til...  22.5 us
    all_to_all x1, waiting for transfers between devices, on_device(): lax.all_to_all(projected.reshape(members, row_count, both), 'tp', split_a...  17.2 us
    unnamed x46, local copies, waits for them, and re-layouts  12.8 us
    concatenate x1, other arithmetic, on_device(): weights = jnp.concatenate([query_base_output, value_base_output], axis=1)  9.12 us
    dot_general x2, matrix products, apply_lowrank_adapters(): reduced = jnp.dot(rows, adapter_down_weight[i], preferred_element_type=F32)  7.7 us
  transfers between devices with their start and end apart: 19, of which 5 were waited for; matrix products, arithmetic and copies ran while one was open for 39% of the time, Pallas kernels for 0%

profile of v3, /device:TPU:6, one launch (start us, length us, event | category | flops | bytes accessed | tf_op | source)
XLA Modules:
  0.0 318.7 jit_solution(16017247956841034484)
XLA Ops:
  0.7 3.1 fusion.61
  3.8 1.6 collective-permute-start.5
  5.3 1.7 collective-permute-start.4
  7.0 4.0 %collective-permute-start = (bf16[96,4096]{1,0:T(8,128)(2,1)}, bf16[96,4096]{1,0:T(8,128)(2,1)}, u32[]{:S(2)}, u32[]{:S(2)}) collective-permute-start(bf16[96,4096]{1,0:T(8,128)(2,1)} %get-tuple-element.39), channel_id=1, source_target_pairs={{0,3},{1,0},{2,1},{3,2},{4,7},{5,4},{6,5},{7,6},{8,11},{9,8},{10,9... | collective-permute-start | bytes 2359304 | tf_op jit(solution)/shard_map/ppermute | solution.py:20
  11.2 13.1 %collective-permute-done.5 = bf16[96,4096]{1,0:T(8,128)(2,1)S(1)} collective-permute-done((bf16[96,4096]{1,0:T(8,128)(2,1)S(1)}, bf16[96,4096]{1,0:T(8,128)(2,1)S(1)}, u32[]{:S(2)}, u32[]{:S(2)}) %collective-permute-start.5) | collective-permute-done | bytes 786464 | tf_op jit(solution)/shard_map/ppermute | solution.py:20
  24.3 0.8 slice.118
  25.4 0.9 copy-done.11
  26.3 0.8 slice.119
  27.1 2.9 collective-permute-start.7
  30.2 4.7 %convolution_convert_fusion = bf16[256,8320]{1,0:T(8,128)(2,1)} fusion(bf16[96,128]{1,0:T(8,128)(2,1)S(1)} %broadcast_in_dim.36, bf16[96,8192]{1,0:T(8,128)(2,1)} %param.8, s32[96]{0:T(128)S(1)} %multiply_add_fusion), kind=kOutput, calls=%fused_computation | convolution fusion | flops 414294016 | bytes 5857664 | tf_op jit(solution)/shard_map/dot_general | solution.py:127
  34.8 7.2 %reshape.35 = bf16[128,2,8320]{2,1,0:T(2,128)(2,1)} reshape(bf16[256,8320]{1,0:T(8,128)(2,1)} %convolution_convert_fusion) | data formatting | bytes 8519680 | tf_op jit(solution)/shard_map/reshape | solution.py:128
  42.1 1.8 slice.116
  43.9 1.9 collective-permute-start.2
  45.8 1.8 slice.117
  47.5 2.1 collective-permute-start.3
  49.7 6.4 %all-to-all-start = ((bf16[128,2,8320]{2,1,0:T(2,128)(2,1)}), bf16[128,2,8320]{2,1,0:T(2,128)(2,1)}, u32[]{:S(2)}, u32[]{:S(2)}) async-start(bf16[128,2,8320]{2,1,0:T(2,128)(2,1)} %reshape.35), calls=%async_computation | async-start | bytes 8519680 | tf_op jit(solution)/shard_map/all_to_all | solution.py:140
  56.1 2.1 constant_dynamic-update-slice_fusion.8
  58.2 2.1 constant_dynamic-update-slice_fusion.3
  60.3 0.8 constant_dynamic-update-slice_fusion.7
  61.0 1.8 constant_dynamic-update-slice_fusion.6
  62.8 1.8 constant_dynamic-update-slice_fusion.2
  64.6 1.8 constant_dynamic-update-slice_fusion.1
  66.4 0.9 constant_dynamic-update-slice_fusion.5
  67.3 2.1 constant_dynamic-update-slice_fusion
  69.4 3.4 %collective-permute-start.12 = (bf16[384,4096]{1,0:T(8,128)(2,1)}, bf16[384,4096]{1,0:T(8,128)(2,1)}, u32[]{:S(2)}, u32[]{:S(2)}) collective-permute-start(bf16[384,4096]{1,0:T(8,128)(2,1)} %constant_dynamic-update-slice_fusion.5), channel_id=1, source_target_pairs={{0,3},{1,0},{2,1},{3,2},{4,7},{5,4},{6,5},{7,6},{8,11},{9,8},{10,9... | collective-permute-start | bytes 9437192 | tf_op jit(solution)/shard_map/ppermute | solution.py:20
  72.8 2.9 collective-permute-start.8
  75.7 2.7 copy.46
  78.4 9.1 %pad_maximum_fusion = (bf16[4096,576]{1,0:T(8,128)(2,1)}, bf16[4096,576]{1,0:T(8,128)(2,1)}) fusion(bf16[8192,64]{1,0:T(8,128)(2,1)} %copy.46, bf16[8192,512]{1,0:T(8,128)(2,1)} %param.11), kind=kLoop, calls=%fused_computation.7 | loop fusion | flops 18874368 | bytes 18874368 | tf_op jit(solution)/shard_map/concatenate | solution.py:159
  87.5 22.5 %all-to-all-done = bf16[128,2,8320]{2,1,0:T(2,128)(2,1)} async-done(((bf16[128,2,8320]{2,1,0:T(2,128)(2,1)}), bf16[128,2,8320]{2,1,0:T(2,128)(2,1)}, u32[]{:S(2)}, u32[]{:S(2)}) %all-to-all-start) | async-done | bytes 4259872 | tf_op jit(solution)/shard_map/all_to_all | solution.py:140
  110.0 7.2 %reshape.36 = bf16[256,8320]{1,0:T(8,128)(2,1)} reshape(bf16[128,2,8320]{2,1,0:T(2,128)(2,1)} %all-to-all-done) | data formatting | bytes 8519680 | tf_op jit(solution)/shard_map/reshape | solution.py:142
  117.3 1.0 compare_reduce_fusion.1
  118.3 4.5 %fusion.30 = bf16[256,128]{0,1:T(8,128)(2,1)S(1)} fusion(bf16[2,8192,128]{2,1,0:T(8,128)(2,1)} %param.13, bf16[256,8320]{1,0:T(8,128)(2,1)} %reshape.36, pred[256]{0:T(512)(128)(4,1)S(1)} %get-tuple-element.28), kind=kOutput, calls=%fused_computation.40 | convolution fusion | flops 536936448 | bytes 6357248 | tf_op jit(solution)/shard_map/dot_general | solution.py:49
  122.8 3.2 fusion.40
  126.4 1.3 fusion
  127.6 2.5 pad_maximum_fusion.1
  130.1 7.6 %reshape.39 = bf16[128,2,9216]{2,1,0:T(2,128)(2,1)} reshape(bf16[256,9216]{1,0:T(8,128)(2,1)} %pad_maximum_fusion.1) | data formatting | bytes 9437184 | tf_op jit(solution)/shard_map/reshape | solution.py:151
  137.7 5.2 %all-to-all-start.1 = ((bf16[128,2,9216]{2,1,0:T(2,128)(2,1)}), bf16[128,2,9216]{2,1,0:T(2,128)(2,1)}, u32[]{:S(2)}, u32[]{:S(2)}) async-start(bf16[128,2,9216]{2,1,0:T(2,128)(2,1)} %reshape.39), calls=%async_computation.1 | async-start | bytes 9437184 | tf_op jit(solution)/shard_map/all_to_all | solution.py:153
  143.0 7.1 %fusion.67 = f32[384,576]{1,0:T(8,128)} fusion(bf16[384,4096]{1,0:T(8,128)(2,1)} %constant_dynamic-update-slice_fusion.5, bf16[4096,576]{1,0:T(8,128)(2,1)} %get-tuple-element.30), kind=kOutput, calls=%fused_computation.83 | convolution fusion | flops 1811939328 | bytes 8749056 | tf_op jit(solution)/shard_map/dot_general | solution.py:176
  150.1 3.6 %fusion.64 = f32[384,576]{1,0:T(8,128)} fusion(bf16[384,4096]{1,0:T(8,128)(2,1)S(1)} %copy-done.13, bf16[4096,576]{1,0:T(8,128)(2,1)S(1)} %bitcast.69), kind=kOutput, calls=%fused_computation.80 | convolution fusion | flops 1811939328 | bytes 8749056 | tf_op jit(solution)/shard_map/dot_general | solution.py:176
  153.8 56.8 %collective-permute-done.13 = bf16[384,4096]{1,0:T(8,128)(2,1)} collective-permute-done((bf16[384,4096]{1,0:T(8,128)(2,1)}, bf16[384,4096]{1,0:T(8,128)(2,1)}, u32[]{:S(2)}, u32[]{:S(2)}) %collective-permute-start.13) | collective-permute-done | bytes 3145760 | tf_op jit(solution)/shard_map/ppermute | solution.py:20
  210.5 1.5 slice.124
  212.3 1.5 slice.125
  213.8 5.0 %collective-permute-start.15 = (bf16[192,4096]{1,0:T(8,128)(2,1)S(1)}, bf16[192,4096]{1,0:T(8,128)(2,1)S(1)}, u32[]{:S(2)}, u32[]{:S(2)}) collective-permute-start(bf16[192,4096]{1,0:T(8,128)(2,1)S(1)} %slice.125), channel_id=1, source_target_pairs={{0,3},{1,0},{2,1},{3,2},{4,7},{5,4},{6,5},{7,6},{8,11},{9,8},{10,9... | collective-permute-start | bytes 4718600 | tf_op jit(solution)/shard_map/ppermute | solution.py:20
  218.8 1.5 slice.122
  220.5 1.6 slice.123
  222.0 3.5 %collective-permute-start.11 = (bf16[192,4096]{1,0:T(8,128)(2,1)S(1)}, bf16[192,4096]{1,0:T(8,128)(2,1)S(1)}, u32[]{:S(2)}, u32[]{:S(2)}) collective-permute-start(bf16[192,4096]{1,0:T(8,128)(2,1)S(1)} %slice.123), channel_id=1, source_target_pairs={{0,12},{1,13},{2,14},{3,15},{4,0},{5,1},{6,2},{7,3},{8,4},{9,5},{1... | collective-permute-start | bytes 4718600 | tf_op jit(solution)/shard_map/ppermute | solution.py:20
  225.6 5.5 %fusion.68 = f32[384,576]{1,0:T(8,128)} fusion(bf16[384,4096]{1,0:T(8,128)(2,1)} %collective-permute-done.12, bf16[4096,576]{1,0:T(8,128)(2,1)S(1)} %bitcast.67), kind=kOutput, calls=%fused_computation.84 | convolution fusion | flops 1811939328 | bytes 8749056 | tf_op jit(solution)/shard_map/dot_general | solution.py:176
  231.0 5.5 %fusion.65 = f32[384,576]{1,0:T(8,128)} fusion(bf16[384,4096]{1,0:T(8,128)(2,1)} %collective-permute-done.8, bf16[4096,576]{1,0:T(8,128)(2,1)S(1)} %bitcast.69), kind=kOutput, calls=%fused_computation.81 | convolution fusion | flops 1811939328 | bytes 8749056 | tf_op jit(solution)/shard_map/dot_general | solution.py:176
  236.6 5.4 %fusion.66 = f32[384,576]{1,0:T(8,128)} fusion(bf16[384,4096]{1,0:T(8,128)(2,1)} %collective-permute-done.9, bf16[4096,576]{1,0:T(8,128)(2,1)S(1)} %bitcast.69), kind=kOutput, calls=%fused_computation.82 | convolution fusion | flops 1811939328 | bytes 8749056 | tf_op jit(solution)/shard_map/dot_general | solution.py:176
  242.0 15.9 %collective-permute-done.14 = bf16[192,4096]{1,0:T(8,128)(2,1)S(1)} collective-permute-done((bf16[192,4096]{1,0:T(8,128)(2,1)S(1)}, bf16[192,4096]{1,0:T(8,128)(2,1)S(1)}, u32[]{:S(2)}, u32[]{:S(2)}) %collective-permute-start.14) | collective-permute-done | bytes 1572896 | tf_op jit(solution)/shard_map/ppermute | solution.py:20
  257.9 3.6 %fusion.11 = f32[384,576]{1,0:T(8,128)} fusion(bf16[4096,576]{1,0:T(8,128)(2,1)S(1)} %bitcast.67, bf16[192,4096]{1,0:T(8,128)(2,1)S(1)} %collective-permute-done.15, bf16[192,4096]{1,0:T(8,128)(2,1)S(1)} %collective-permute-done.14), kind=kOutput, calls=%fused_computation.20 | convolution fusion | flops 1818230784 | bytes 8749056 | tf_op jit(solution)/shard_map/dot_general | solution.py:176
  261.5 3.7 %fusion.7 = f32[384,576]{1,0:T(8,128)} fusion(bf16[4096,576]{1,0:T(8,128)(2,1)S(1)} %bitcast.69, bf16[192,4096]{1,0:T(8,128)(2,1)S(1)} %collective-permute-done.11, bf16[192,4096]{1,0:T(8,128)(2,1)S(1)} %collective-permute-done.10), kind=kOutput, calls=%fused_computation.16 | convolution fusion | flops 1818230784 | bytes 8749056 | tf_op jit(solution)/shard_map/dot_general | solution.py:176
  265.3 6.4 %fusion.69 = f32[384,576]{1,0:T(8,128)S(1)} fusion(bf16[384,4096]{1,0:T(8,128)(2,1)} %collective-permute-done.13, bf16[4096,576]{1,0:T(8,128)(2,1)} %get-tuple-element.30), kind=kOutput, calls=%fused_computation.85 | convolution fusion | flops 1811939328 | bytes 8749056 | tf_op jit(solution)/shard_map/dot_general | solution.py:176
  271.8 0.7 fusion.2
  272.7 1.1 maximum_select_fusion
  274.0 0.3 fusion.19
  274.5 0.3 maximum_select_fusion.2
  275.0 1.7 fusion.20
  276.7 5.4 %all-to-all-start.2 = ((bf16[16,96,576]{2,1,0:T(8,128)(2,1)}), bf16[16,96,576]{2,1,0:T(8,128)(2,1)}, u32[]{:S(2)}, u32[]{:S(2)}) async-start(bf16[16,96,576]{2,1,0:T(8,128)(2,1)} %bitcast.65), calls=%async_computation.2 | async-start | bytes 3932160 | tf_op jit(solution)/shard_map/all_to_all | solution.py:189
  282.1 7.5 %reshape.41 = bf16[256,9216]{1,0:T(8,128)(2,1)} reshape(bf16[128,2,9216]{2,1,0:T(2,128)(2,1)} %all-to-all-done.1) | data formatting | bytes 9437184 | tf_op jit(solution)/shard_map/reshape | solution.py:186
  289.6 4.7 %convolution_convert_fusion.1.query_term_ref.value_term_ref = bf16[96,9216]{1,0:T(8,128)(2,1)} fusion(bf16[256,9216]{1,0:T(8,128)(2,1)} %reshape.41, s32[96]{0:T(128)S(1)} %multiply_add_fusion), kind=kOutput, calls=%fused_computation.2 | convolution fusion | flops 453894144 | bytes 6488448 | tf_op jit(solution)/shard_map/dot_general | solution.py:188
  294.3 17.2 %all-to-all-done.2.plain_ref = bf16[16,96,576]{2,1,0:T(8,128)(2,1)} async-done(((bf16[16,96,576]{2,1,0:T(8,128)(2,1)}), bf16[16,96,576]{2,1,0:T(8,128)(2,1)}, u32[]{:S(2)}, u32[]{:S(2)}) %all-to-all-start.2) | async-done | bytes 1769504 | tf_op jit(solution)/shard_map/all_to_all | solution.py:189
  311.5 1.5 copy-done.2
  312.9 5.7 %shard_map.95 = (bf16[96,8192]{1,0:T(8,128)(2,1)}, bf16[96,1024]{1,0:T(8,128)(2,1)}) custom-call(bf16[16,96,576]{2,1,0:T(8,128)(2,1)} %all-to-all-done.2.plain_ref, bf16[96,9216]{1,0:T(8,128)(2,1)S(1)} %copy-done.2, bf16[96,9216]{1,0:T(8,128)(2,1)S(1)} %copy-done.2), custom_call_target="tpu_custom_call" | custom-call | flops 884736 | bytes 5308416 | tf_op jit(solution)/shard_map/pallas_call | solution.py:75
  (72 shorter events, 2.0 us)
Async XLA Ops:
  0.6 125.7 %copy-start = (bf16[2,64,8192]{2,1,0:T(8,128)(2,1)S(1)}, bf16[2,64,8192]{2,1,0:T(8,128)(2,1)}, u32[]{:S(2)}) copy-start(bf16[2,64,8192]{2,1,0:T(8,128)(2,1)} %param.14) | copy-start | bytes 6291460
  0.6 10.4 %copy-start.14 = (s32[96,1]{0,1:T(1,128)S(1)}, s32[96,1]{0,1:T(1,128)}, u32[]{:S(2)}) copy-start(s32[96,1]{0,1:T(1,128)} %param.9) | copy-start | bytes 1156
  0.7 29.4 %copy-start.15 = (s32[96,1]{0,1:T(1,128)S(1)}, s32[96,1]{0,1:T(1,128)}, u32[]{:S(2)}) copy-start(s32[96,1]{0,1:T(1,128)} %param.10) | copy-start | bytes 1156
  3.8 20.6 %collective-permute-start.5 = (bf16[96,4096]{1,0:T(8,128)(2,1)S(1)}, bf16[96,4096]{1,0:T(8,128)(2,1)S(1)}, u32[]{:S(2)}, u32[]{:S(2)}) collective-permute-start(bf16[96,4096]{1,0:T(8,128)(2,1)S(1)} %get-tuple-element.36), channel_id=1, source_target_pairs={{0,4},{1,5},{2,6},{3,7},{4,8},{5,9},{6,10},{7,11},{8,12},{9,13},{1... | collective-permute-start | bytes 2359304 | tf_op jit(solution)/shard_map/ppermute | solution.py:20
  5.3 20.1 %collective-permute-start.4 = (bf16[96,4096]{1,0:T(8,128)(2,1)S(1)}, bf16[96,4096]{1,0:T(8,128)(2,1)S(1)}, u32[]{:S(2)}, u32[]{:S(2)}) collective-permute-start(bf16[96,4096]{1,0:T(8,128)(2,1)S(1)} %get-tuple-element.36), channel_id=1, source_target_pairs={{0,12},{1,13},{2,14},{3,15},{4,0},{5,1},{6,2},{7,3},{8,4},{9,5},{1... | collective-permute-start | bytes 2359304 | tf_op jit(solution)/shard_map/ppermute | solution.py:20
  7.0 38.8 %collective-permute-start = (bf16[96,4096]{1,0:T(8,128)(2,1)}, bf16[96,4096]{1,0:T(8,128)(2,1)}, u32[]{:S(2)}, u32[]{:S(2)}) collective-permute-start(bf16[96,4096]{1,0:T(8,128)(2,1)} %get-tuple-element.39), channel_id=1, source_target_pairs={{0,3},{1,0},{2,1},{3,2},{4,7},{5,4},{6,5},{7,6},{8,11},{9,8},{10,9... | collective-permute-start | bytes 2359304 | tf_op jit(solution)/shard_map/ppermute | solution.py:20
  11.0 31.0 %collective-permute-start.1 = (bf16[96,4096]{1,0:T(8,128)(2,1)}, bf16[96,4096]{1,0:T(8,128)(2,1)}, u32[]{:S(2)}, u32[]{:S(2)}) collective-permute-start(bf16[96,4096]{1,0:T(8,128)(2,1)} %get-tuple-element.39), channel_id=1, source_target_pairs={{0,1},{1,2},{2,3},{3,0},{4,5},{5,6},{6,7},{7,4},{8,9},{9,10},{10,1... | collective-permute-start | bytes 2359304 | tf_op jit(solution)/shard_map/ppermute | solution.py:20
  25.1 24.5 %collective-permute-start.6 = (bf16[48,4096]{1,0:T(8,128)(2,1)}, bf16[48,4096]{1,0:T(8,128)(2,1)S(1)}, u32[]{:S(2)}, u32[]{:S(2)}) collective-permute-start(bf16[48,4096]{1,0:T(8,128)(2,1)} %slice.118), channel_id=1, source_target_pairs={{0,4},{1,5},{2,6},{3,7},{4,8},{5,9},{6,10},{7,11},{8,12},{9,13},{1... | collective-permute-start | bytes 1179656 | tf_op jit(solution)/shard_map/ppermute | solution.py:20
  25.4 0.9 copy-start.11
  27.1 22.5 %collective-permute-start.7 = (bf16[48,4096]{1,0:T(8,128)(2,1)}, bf16[48,4096]{1,0:T(8,128)(2,1)}, u32[]{:S(2)}, u32[]{:S(2)}) collective-permute-start(bf16[48,4096]{1,0:T(8,128)(2,1)} %slice.119), channel_id=1, source_target_pairs={{0,12},{1,13},{2,14},{3,15},{4,0},{5,1},{6,2},{7,3},{8,4},{9,5},{1... | collective-permute-start | bytes 1179656 | tf_op jit(solution)/shard_map/ppermute | solution.py:20
  43.9 19.0 %collective-permute-start.2 = (bf16[48,4096]{1,0:T(8,128)(2,1)}, bf16[48,4096]{1,0:T(8,128)(2,1)}, u32[]{:S(2)}, u32[]{:S(2)}) collective-permute-start(bf16[48,4096]{1,0:T(8,128)(2,1)} %slice.116), channel_id=1, source_target_pairs={{0,1},{1,2},{2,3},{3,0},{4,5},{5,6},{6,7},{7,4},{8,9},{9,10},{10,1... | collective-permute-start | bytes 1179656 | tf_op jit(solution)/shard_map/ppermute | solution.py:20
  47.5 17.1 %collective-permute-start.3 = (bf16[48,4096]{1,0:T(8,128)(2,1)}, bf16[48,4096]{1,0:T(8,128)(2,1)}, u32[]{:S(2)}, u32[]{:S(2)}) collective-permute-start(bf16[48,4096]{1,0:T(8,128)(2,1)} %slice.117), channel_id=1, source_target_pairs={{0,3},{1,0},{2,1},{3,2},{4,7},{5,4},{6,5},{7,6},{8,11},{9,8},{10,9... | collective-permute-start | bytes 1179656 | tf_op jit(solution)/shard_map/ppermute | solution.py:20
  49.7 60.3 %all-to-all-start = ((bf16[128,2,8320]{2,1,0:T(2,128)(2,1)}), bf16[128,2,8320]{2,1,0:T(2,128)(2,1)}, u32[]{:S(2)}, u32[]{:S(2)}) async-start(bf16[128,2,8320]{2,1,0:T(2,128)(2,1)} %reshape.35), calls=%async_computation | async-start | bytes 8519680 | tf_op jit(solution)/shard_map/all_to_all | solution.py:140
  69.4 142.9 %collective-permute-start.12 = (bf16[384,4096]{1,0:T(8,128)(2,1)}, bf16[384,4096]{1,0:T(8,128)(2,1)}, u32[]{:S(2)}, u32[]{:S(2)}) collective-permute-start(bf16[384,4096]{1,0:T(8,128)(2,1)} %constant_dynamic-update-slice_fusion.5), channel_id=1, source_target_pairs={{0,3},{1,0},{2,1},{3,2},{4,7},{5,4},{6,5},{7,6},{8,11},{9,8},{10,9... | collective-permute-start | bytes 9437192 | tf_op jit(solution)/shard_map/ppermute | solution.py:20
  72.8 137.8 %collective-permute-start.13 = (bf16[384,4096]{1,0:T(8,128)(2,1)}, bf16[384,4096]{1,0:T(8,128)(2,1)}, u32[]{:S(2)}, u32[]{:S(2)}) collective-permute-start(bf16[384,4096]{1,0:T(8,128)(2,1)} %constant_dynamic-update-slice_fusion.5), channel_id=1, source_target_pairs={{0,1},{1,2},{2,3},{3,0},{4,5},{5,6},{6,7},{7,4},{8,9},{9,10},{10,1... | collective-permute-start | bytes 9437192 | tf_op jit(solution)/shard_map/ppermute | solution.py:20
  72.8 147.7 %collective-permute-start.8 = (bf16[384,4096]{1,0:T(8,128)(2,1)}, bf16[384,4096]{1,0:T(8,128)(2,1)}, u32[]{:S(2)}, u32[]{:S(2)}) collective-permute-start(bf16[384,4096]{1,0:T(8,128)(2,1)} %constant_dynamic-update-slice_fusion), channel_id=1, source_target_pairs={{0,12},{1,13},{2,14},{3,15},{4,0},{5,1},{6,2},{7,3},{8,4},{9,5},{1... | collective-permute-start | bytes 9437192 | tf_op jit(solution)/shard_map/ppermute | solution.py:20
  75.7 143.2 %collective-permute-start.9 = (bf16[384,4096]{1,0:T(8,128)(2,1)}, bf16[384,4096]{1,0:T(8,128)(2,1)}, u32[]{:S(2)}, u32[]{:S(2)}) collective-permute-start(bf16[384,4096]{1,0:T(8,128)(2,1)} %constant_dynamic-update-slice_fusion), channel_id=1, source_target_pairs={{0,4},{1,5},{2,6},{3,7},{4,8},{5,9},{6,10},{7,11},{8,12},{9,13},{1... | collective-permute-start | bytes 9437192 | tf_op jit(solution)/shard_map/ppermute | solution.py:20
  118.3 4.5 %copy-start.3 = (bf16[256,8320]{1,0:T(8,128)(2,1)S(1)}, bf16[256,8320]{1,0:T(8,128)(2,1)}, u32[]{:S(2)}) copy-start(bf16[256,8320]{1,0:T(8,128)(2,1)} %reshape.36) | copy-start | bytes 12779524
  122.8 3.2 %copy-start.12 = (bf16[2,64,1024]{2,1,0:T(8,128)(2,1)S(1)}, bf16[2,64,1024]{2,1,0:T(8,128)(2,1)}, u32[]{:S(2)}) copy-start(bf16[2,64,1024]{2,1,0:T(8,128)(2,1)} %param.15) | copy-start | bytes 786436
  137.7 12.4 %slice-start.2 = ((s8[5242880]{0:T(1024)(128)(4,1)}), s8[1048576]{0:T(1024)(128)(4,1)S(1)}, s32[]{:S(2)}) async-start(s8[5242880]{0:T(1024)(128)(4,1)} %bitcast.68), calls=%async_computation.5 | async-start | bytes 2097152
  137.7 127.5 %all-to-all-start.1 = ((bf16[128,2,9216]{2,1,0:T(2,128)(2,1)}), bf16[128,2,9216]{2,1,0:T(2,128)(2,1)}, u32[]{:S(2)}, u32[]{:S(2)}) async-start(bf16[128,2,9216]{2,1,0:T(2,128)(2,1)} %reshape.39), calls=%async_computation.1 | async-start | bytes 9437184 | tf_op jit(solution)/shard_map/all_to_all | solution.py:153
  142.9 7.2 %slice-start.3 = ((s8[5242880]{0:T(1024)(128)(4,1)}), s8[4194304]{0:T(1024)(128)(4,1)S(1)}, s32[]{:S(2)}) async-start(s8[5242880]{0:T(1024)(128)(4,1)} %bitcast.68), calls=%async_computation.6 | async-start | bytes 8388608
  142.9 7.2 %copy-start.13 = (bf16[384,4096]{1,0:T(8,128)(2,1)S(1)}, bf16[384,4096]{1,0:T(8,128)(2,1)}, u32[]{:S(2)}) copy-start(bf16[384,4096]{1,0:T(8,128)(2,1)} %constant_dynamic-update-slice_fusion) | copy-start | bytes 9437188
  142.9 82.6 %slice-start = ((s8[5242880]{0:T(1024)(128)(4,1)}), s8[4194304]{0:T(1024)(128)(4,1)S(1)}, s32[]{:S(2)}) async-start(s8[5242880]{0:T(1024)(128)(4,1)} %bitcast.66), calls=%async_computation.3 | async-start | bytes 8388608
  150.1 75.4 %slice-start.1 = ((s8[5242880]{0:T(1024)(128)(4,1)}), s8[1048576]{0:T(1024)(128)(4,1)S(1)}, s32[]{:S(2)}) async-start(s8[5242880]{0:T(1024)(128)(4,1)} %bitcast.66), calls=%async_computation.4 | async-start | bytes 2097152
  212.1 45.8 %collective-permute-start.14 = (bf16[192,4096]{1,0:T(8,128)(2,1)S(1)}, bf16[192,4096]{1,0:T(8,128)(2,1)S(1)}, u32[]{:S(2)}, u32[]{:S(2)}) collective-permute-start(bf16[192,4096]{1,0:T(8,128)(2,1)S(1)} %slice.124), channel_id=1, source_target_pairs={{0,1},{1,2},{2,3},{3,0},{4,5},{5,6},{6,7},{7,4},{8,9},{9,10},{10,1... | collective-permute-start | bytes 4718600 | tf_op jit(solution)/shard_map/ppermute | solution.py:20
  213.8 44.1 %collective-permute-start.15 = (bf16[192,4096]{1,0:T(8,128)(2,1)S(1)}, bf16[192,4096]{1,0:T(8,128)(2,1)S(1)}, u32[]{:S(2)}, u32[]{:S(2)}) collective-permute-start(bf16[192,4096]{1,0:T(8,128)(2,1)S(1)} %slice.125), channel_id=1, source_target_pairs={{0,3},{1,0},{2,1},{3,2},{4,7},{5,4},{6,5},{7,6},{8,11},{9,8},{10,9... | collective-permute-start | bytes 4718600 | tf_op jit(solution)/shard_map/ppermute | solution.py:20
  220.4 41.1 %collective-permute-start.10 = (bf16[192,4096]{1,0:T(8,128)(2,1)S(1)}, bf16[192,4096]{1,0:T(8,128)(2,1)S(1)}, u32[]{:S(2)}, u32[]{:S(2)}) collective-permute-start(bf16[192,4096]{1,0:T(8,128)(2,1)S(1)} %slice.122), channel_id=1, source_target_pairs={{0,4},{1,5},{2,6},{3,7},{4,8},{5,9},{6,10},{7,11},{8,12},{9,13},{1... | collective-permute-start | bytes 4718600 | tf_op jit(solution)/shard_map/ppermute | solution.py:20
  222.0 39.5 %collective-permute-start.11 = (bf16[192,4096]{1,0:T(8,128)(2,1)S(1)}, bf16[192,4096]{1,0:T(8,128)(2,1)S(1)}, u32[]{:S(2)}, u32[]{:S(2)}) collective-permute-start(bf16[192,4096]{1,0:T(8,128)(2,1)S(1)} %slice.123), channel_id=1, source_target_pairs={{0,12},{1,13},{2,14},{3,15},{4,0},{5,1},{6,2},{7,3},{8,4},{9,5},{1... | collective-permute-start | bytes 4718600 | tf_op jit(solution)/shard_map/ppermute | solution.py:20
  265.2 6.5 %copy-start.4 = (f32[384,576]{1,0:T(8,128)S(1)}, f32[384,576]{1,0:T(8,128)}, u32[]{:S(2)}) copy-start(f32[384,576]{1,0:T(8,128)} %fusion.67) | copy-start | bytes 2654212
  265.2 6.5 %copy-start.5 = (f32[384,576]{1,0:T(8,128)S(1)}, f32[384,576]{1,0:T(8,128)}, u32[]{:S(2)}) copy-start(f32[384,576]{1,0:T(8,128)} %fusion.64) | copy-start | bytes 2654212
  265.2 6.5 %copy-start.6 = (f32[384,576]{1,0:T(8,128)S(1)}, f32[384,576]{1,0:T(8,128)}, u32[]{:S(2)}) copy-start(f32[384,576]{1,0:T(8,128)} %fusion.68) | copy-start | bytes 2654212
  265.2 6.5 %copy-start.7 = (f32[384,576]{1,0:T(8,128)S(1)}, f32[384,576]{1,0:T(8,128)}, u32[]{:S(2)}) copy-start(f32[384,576]{1,0:T(8,128)} %fusion.65) | copy-start | bytes 2654212
  265.2 6.5 %copy-start.8 = (f32[384,576]{1,0:T(8,128)S(1)}, f32[384,576]{1,0:T(8,128)}, u32[]{:S(2)}) copy-start(f32[384,576]{1,0:T(8,128)} %fusion.66) | copy-start | bytes 2654212
  265.2 6.5 %copy-start.9 = (f32[384,576]{1,0:T(8,128)S(1)}, f32[384,576]{1,0:T(8,128)}, u32[]{:S(2)}) copy-start(f32[384,576]{1,0:T(8,128)} %fusion.11) | copy-start | bytes 2654212
  265.3 6.5 %copy-start.10 = (f32[384,576]{1,0:T(8,128)S(1)}, f32[384,576]{1,0:T(8,128)}, u32[]{:S(2)}) copy-start(f32[384,576]{1,0:T(8,128)} %fusion.7) | copy-start | bytes 2654212
  276.7 34.8 %all-to-all-start.2 = ((bf16[16,96,576]{2,1,0:T(8,128)(2,1)}), bf16[16,96,576]{2,1,0:T(8,128)(2,1)}, u32[]{:S(2)}, u32[]{:S(2)}) async-start(bf16[16,96,576]{2,1,0:T(8,128)(2,1)} %bitcast.65), calls=%async_computation.2 | async-start | bytes 3932160 | tf_op jit(solution)/shard_map/all_to_all | solution.py:189
  289.6 29.0 %copy-start.1 = (bf16[2,64,8192]{2,1,0:T(8,128)(2,1)S(1)}, bf16[2,64,8192]{2,1,0:T(8,128)(2,1)}, u32[]{:S(2)}) copy-start(bf16[2,64,8192]{2,1,0:T(8,128)(2,1)} %param.14) | copy-start | bytes 6291460
  311.5 1.5 copy-start.2

commit v4 on v1

--- a/solution.py
+++ b/solution.py
@@ -60,29 +60,34 @@
 
 
 def finish_kernel(plain_ref, query_term_ref, value_term_ref, queries_ref, values_ref):
-    query_cols = queries_ref.shape[1] // 2
-    for i in range(2):
+    count, _, both = plain_ref.shape
+    query_cols = queries_ref.shape[1] // count
+    value_cols = both - query_cols
+    for i in range(count):
         cols = slice(i * query_cols, (i + 1) * query_cols)
         base = plain_ref[i, :, :query_cols].astype(F32)
         queries_ref[:, cols] = (base + query_term_ref[:, cols].astype(F32)).astype(BF)
-    base = jnp.concatenate([plain_ref[0, :, query_cols:], plain_ref[1, :, query_cols:]], axis=1)
-    values_ref[...] = (base.astype(F32) + value_term_ref[...].astype(F32)).astype(BF)
+    for i in range(0, count, 2):
+        cols = slice(i * value_cols, (i + 2) * value_cols)
+        base = jnp.concatenate([plain_ref[i, :, query_cols:], plain_ref[i + 1, :, query_cols:]], axis=1)
+        values_ref[:, cols] = (base.astype(F32) + value_term_ref[:, cols].astype(F32)).astype(BF)
 
 
 def finish(plain, terms, query_cols, value_cols):
     members, rows, both = plain.shape
-    value_at = members * query_cols // (2 * value_cols)
+    count = 4
+    value_at = members * query_cols // (count * value_cols)
     return pl.pallas_call(
         finish_kernel,
-        grid=(members // 2,),
+        grid=(members // count,),
         in_specs=[
-            pl.BlockSpec((2, rows, both), lambda i: (i, 0, 0)),
-            pl.BlockSpec((rows, 2 * query_cols), lambda i: (0, i)),
-            pl.BlockSpec((rows, 2 * value_cols), lambda i: (0, value_at + i)),
+            pl.BlockSpec((count, rows, both), lambda i: (i, 0, 0)),
+            pl.BlockSpec((rows, count * query_cols), lambda i: (0, i)),
+            pl.BlockSpec((rows, count * value_cols), lambda i: (0, value_at + i)),
         ],
         out_specs=[
-            pl.BlockSpec((rows, 2 * query_cols), lambda i: (0, i)),
-            pl.BlockSpec((rows, 2 * value_cols), lambda i: (0, i)),
+            pl.BlockSpec((rows, count * query_cols), lambda i: (0, i)),
+            pl.BlockSpec((rows, count * value_cols), lambda i: (0, i)),
         ],
         out_shape=[
             jax.ShapeDtypeStruct((rows, members * query_cols), BF),

time: 302 us -> 300 us (level)
  no operation moved by 1% of the time
where the time goes in v4:
time: 300 us; the launch traced here: 298 us
  waiting for transfers between devices  121 us (40%)
  local copies, waits for them, and re-layouts  58.4 us (19%)
  matrix products  51.6 us (17%)
  starting transfers between devices  49.9 us (17%)
  other arithmetic  12.5 us (4%)
  Pallas kernels  3.87 us (1%)
    ppermute x16, waiting for transfers between devices, shift(): return lax.ppermute(x, 'tp', pairs)  107 us
    dot_general x8, matrix products, on_device(): jnp.dot(x, w, preferred_element_type=F32).reshape(side, row_count, both)  34.4 us
    ppermute x16, starting transfers between devices, shift(): return lax.ppermute(x, 'tp', pairs)  28.8 us
    all_to_all x1, waiting for transfers between devices, on_device(): lax.all_to_all(projected.reshape(members, row_count, both), 'tp', split_a...  13.5 us
    all_to_all x1, starting transfers between devices, on_device(): lax.all_to_all(send_rows, ('grp', 'tp'), split_axis=0, concat_axis=0, til...  10.1 us
    unnamed x38, local copies, waits for them, and re-layouts  8.82 us
    dot_general x2, matrix products, apply_lowrank_adapters(): reduced = jnp.dot(rows, adapter_down_weight[i], preferred_element_type=F32)  7.7 us
    reshape x1, local copies, waits for them, and re-layouts, on_device(): back = back.reshape(slot_total, back.shape[2])  7.54 us
  transfers between devices with their start and end apart: 19, of which 7 were waited for; matrix products, arithmetic and copies ran while one was open for 39% of the time, Pallas kernels for 0%

profile of v4, /device:TPU:6, one launch (start us, length us, event | category | flops | bytes accessed | tf_op | source)
XLA Modules:
  0.0 298.4 jit_solution(14079870381132564991)
XLA Ops:
  0.7 3.4 %fusion.61 = (bf16[96,4096]{1,0:T(8,128)(2,1)}, bf16[384,4096]{1,0:T(8,128)(2,1)}, bf16[384,4096]{1,0:T(8,128)(2,1)}, bf16[96,4096]{1,0:T(8,128)(2,1)}) fusion(bf16[96,8192]{1,0:T(8,128)(2,1)} %param.8), kind=kLoop, calls=%fused_computation.76 | loop fusion | bytes 4718592 | tf_op jit(solution)/shard_map/slice | solution.py:158
  4.1 4.0 %collective-permute-start = (bf16[96,4096]{1,0:T(8,128)(2,1)}, bf16[96,4096]{1,0:T(8,128)(2,1)}, u32[]{:S(2)}, u32[]{:S(2)}) collective-permute-start(bf16[96,4096]{1,0:T(8,128)(2,1)} %get-tuple-element.21), channel_id=1, source_target_pairs={{0,3},{1,0},{2,1},{3,2},{4,7},{5,4},{6,5},{7,6},{8,11},{9,8},{10,9... | collective-permute-start | bytes 2359304 | tf_op jit(solution)/shard_map/ppermute | solution.py:20
  8.1 3.0 %collective-permute-start.8 = (bf16[96,4096]{1,0:T(8,128)(2,1)}, bf16[96,4096]{1,0:T(8,128)(2,1)}, u32[]{:S(2)}, u32[]{:S(2)}) collective-permute-start(bf16[96,4096]{1,0:T(8,128)(2,1)} %get-tuple-element.18), channel_id=1, source_target_pairs={{0,12},{1,13},{2,14},{3,15},{4,0},{5,1},{6,2},{7,3},{8,4},{9,5},{1... | collective-permute-start | bytes 2359304 | tf_op jit(solution)/shard_map/ppermute | solution.py:20
  11.4 3.3 %convolution_convert_fusion = bf16[256,8320]{1,0:T(8,128)(2,1)} fusion(bf16[96,128]{1,0:T(8,128)(2,1)S(1)} %broadcast_in_dim.34, bf16[96,8192]{1,0:T(8,128)(2,1)S(1)} %copy-done.3, s32[96]{0:T(128)S(1)} %multiply_add_fusion), kind=kOutput, calls=%fused_computation | convolution fusion | flops 414294016 | bytes 5857664 | tf_op jit(solution)/shard_map/dot_general | solution.py:132
  14.7 7.3 %reshape.34 = bf16[128,2,8320]{2,1,0:T(2,128)(2,1)} reshape(bf16[256,8320]{1,0:T(8,128)(2,1)} %convolution_convert_fusion) | data formatting | bytes 8519680 | tf_op jit(solution)/shard_map/reshape | solution.py:133
  21.9 10.1 %all-to-all-start = ((bf16[128,2,8320]{2,1,0:T(2,128)(2,1)}), bf16[128,2,8320]{2,1,0:T(2,128)(2,1)}, u32[]{:S(2)}, u32[]{:S(2)}) async-start(bf16[128,2,8320]{2,1,0:T(2,128)(2,1)} %reshape.34), calls=%async_computation | async-start | bytes 8519680 | tf_op jit(solution)/shard_map/all_to_all | solution.py:135
  32.1 2.7 copy.46
  34.8 4.9 %pad_maximum_fusion = (bf16[4096,576]{1,0:T(8,128)(2,1)S(1)}, bf16[4096,576]{1,0:T(8,128)(2,1)S(1)}) fusion(bf16[8192,64]{1,0:T(8,128)(2,1)} %copy.46, bf16[8192,512]{1,0:T(8,128)(2,1)} %param.11), kind=kLoop, calls=%fused_computation.7 | loop fusion | flops 18874368 | bytes 18874368 | tf_op jit(solution)/shard_map/concatenate | solution.py:166
  39.7 1.3 slice.117
  41.0 1.7 collective-permute-start.2
  42.7 1.3 slice.118
  44.0 1.9 collective-permute-start.3
  45.9 1.6 collective-permute-start.10
  47.5 1.0 slice.124
  48.5 1.8 collective-permute-start.11
  50.3 2.1 constant_dynamic-update-slice_fusion.3
  52.4 2.1 constant_dynamic-update-slice_fusion.8
  54.5 34.9 %collective-permute-done.2 = bf16[48,4096]{1,0:T(8,128)(2,1)S(1)} collective-permute-done((bf16[48,4096]{1,0:T(8,128)(2,1)S(1)}, bf16[48,4096]{1,0:T(8,128)(2,1)S(1)}, u32[]{:S(2)}, u32[]{:S(2)}) %collective-permute-start.2) | collective-permute-done | bytes 393248 | tf_op jit(solution)/shard_map/ppermute | solution.py:20
  89.4 0.8 constant_dynamic-update-slice_fusion.2
  90.2 0.8 constant_dynamic-update-slice_fusion.1
  90.9 2.1 constant_dynamic-update-slice_fusion
  93.0 1.5 collective-permute-start.5
  94.5 1.7 collective-permute-start.4
  96.2 0.8 constant_dynamic-update-slice_fusion.7
  97.0 0.8 constant_dynamic-update-slice_fusion.6
  97.8 1.0 constant_dynamic-update-slice_fusion.5
  99.0 3.0 collective-permute-start.12
  102.0 5.4 %fusion.64 = f32[384,576]{1,0:T(8,128)} fusion(bf16[384,4096]{1,0:T(8,128)(2,1)} %constant_dynamic-update-slice_fusion, bf16[4096,576]{1,0:T(8,128)(2,1)S(1)} %get-tuple-element.13), kind=kOutput, calls=%fused_computation.79 | convolution fusion | flops 1811939328 | bytes 8749056 | tf_op jit(solution)/shard_map/dot_general | solution.py:175
  107.4 5.5 %fusion.67 = f32[384,576]{1,0:T(8,128)} fusion(bf16[384,4096]{1,0:T(8,128)(2,1)} %constant_dynamic-update-slice_fusion.5, bf16[4096,576]{1,0:T(8,128)(2,1)S(1)} %get-tuple-element.12), kind=kOutput, calls=%fused_computation.82 | convolution fusion | flops 1811939328 | bytes 8749056 | tf_op jit(solution)/shard_map/dot_general | solution.py:175
  112.9 7.3 %reshape.35 = bf16[256,8320]{1,0:T(8,128)(2,1)} reshape(bf16[128,2,8320]{2,1,0:T(2,128)(2,1)} %all-to-all-done) | data formatting | bytes 8519680 | tf_op jit(solution)/shard_map/reshape | solution.py:137
  120.1 1.0 compare_reduce_fusion.1
  121.1 4.5 %fusion.30 = bf16[256,128]{0,1:T(8,128)(2,1)S(1)} fusion(bf16[2,8192,128]{2,1,0:T(8,128)(2,1)} %param.13, bf16[256,8320]{1,0:T(8,128)(2,1)} %reshape.35, pred[256]{0:T(512)(128)(4,1)S(1)} %get-tuple-element.10), kind=kOutput, calls=%fused_computation.40 | convolution fusion | flops 536936448 | bytes 6357248 | tf_op jit(solution)/shard_map/dot_general | solution.py:49
  125.7 3.2 %fusion.40 = bf16[256,128]{0,1:T(8,128)(2,1)S(1)} fusion(bf16[2,8192,128]{2,1,0:T(8,128)(2,1)} %param.13, bf16[256,8320]{1,0:T(8,128)(2,1)S(1)} %copy-done.6, pred[256]{0:T(512)(128)(4,1)S(1)} %get-tuple-element.11), kind=kOutput, calls=%fused_computation.42 | convolution fusion | flops 536936448 | bytes 6357504 | tf_op jit(solution)/shard_map/dot_general | solution.py:49
  129.2 1.3 fusion
  130.5 2.5 pad_maximum_fusion.1
  133.0 7.5 %reshape.38 = bf16[128,2,9216]{2,1,0:T(2,128)(2,1)} reshape(bf16[256,9216]{1,0:T(8,128)(2,1)} %pad_maximum_fusion.1) | data formatting | bytes 9437184 | tf_op jit(solution)/shard_map/reshape | solution.py:147
  140.5 6.3 %all-to-all-start.1 = ((bf16[128,2,9216]{2,1,0:T(2,128)(2,1)}), bf16[128,2,9216]{2,1,0:T(2,128)(2,1)}, u32[]{:S(2)}, u32[]{:S(2)}) async-start(bf16[128,2,9216]{2,1,0:T(2,128)(2,1)} %reshape.38), calls=%async_computation.1 | async-start | bytes 9437184 | tf_op jit(solution)/shard_map/all_to_all | solution.py:146
  146.9 58.3 %collective-permute-done.4 = bf16[384,4096]{1,0:T(8,128)(2,1)} collective-permute-done((bf16[384,4096]{1,0:T(8,128)(2,1)}, bf16[384,4096]{1,0:T(8,128)(2,1)}, u32[]{:S(2)}, u32[]{:S(2)}) %collective-permute-start.4) | collective-permute-done | bytes 3145760 | tf_op jit(solution)/shard_map/ppermute | solution.py:20
  205.2 1.5 slice.122
  206.8 4.1 %collective-permute-start.7 = (bf16[192,4096]{1,0:T(8,128)(2,1)S(1)}, bf16[192,4096]{1,0:T(8,128)(2,1)S(1)}, u32[]{:S(2)}, u32[]{:S(2)}) collective-permute-start(bf16[192,4096]{1,0:T(8,128)(2,1)S(1)} %slice.122), channel_id=1, source_target_pairs={{0,12},{1,13},{2,14},{3,15},{4,0},{5,1},{6,2},{7,3},{8,4},{9,5},{1... | collective-permute-start | bytes 4718600 | tf_op jit(solution)/shard_map/ppermute | solution.py:20
  210.9 1.5 slice.121
  212.5 7.2 %collective-permute-done.12 = bf16[384,4096]{1,0:T(8,128)(2,1)} collective-permute-done((bf16[384,4096]{1,0:T(8,128)(2,1)}, bf16[384,4096]{1,0:T(8,128)(2,1)}, u32[]{:S(2)}, u32[]{:S(2)}) %collective-permute-start.12) | collective-permute-done | bytes 3145760 | tf_op jit(solution)/shard_map/ppermute | solution.py:20
  219.7 1.5 slice.126
  221.2 3.9 %collective-permute-start.15 = (bf16[192,4096]{1,0:T(8,128)(2,1)S(1)}, bf16[192,4096]{1,0:T(8,128)(2,1)S(1)}, u32[]{:S(2)}, u32[]{:S(2)}) collective-permute-start(bf16[192,4096]{1,0:T(8,128)(2,1)S(1)} %slice.126), channel_id=1, source_target_pairs={{0,3},{1,0},{2,1},{3,2},{4,7},{5,4},{6,5},{7,6},{8,11},{9,8},{10,9... | collective-permute-start | bytes 4718600 | tf_op jit(solution)/shard_map/ppermute | solution.py:20
  225.1 1.7 slice.125
  227.2 4.5 %fusion.66 = f32[384,576]{1,0:T(8,128)S(1)} fusion(bf16[384,4096]{1,0:T(8,128)(2,1)} %collective-permute-done.5, bf16[4096,576]{1,0:T(8,128)(2,1)S(1)} %bitcast.69), kind=kOutput, calls=%fused_computation.81 | convolution fusion | flops 1811939328 | bytes 8749056 | tf_op jit(solution)/shard_map/dot_general | solution.py:175
  231.7 4.5 %fusion.65 = f32[384,576]{1,0:T(8,128)S(1)} fusion(bf16[384,4096]{1,0:T(8,128)(2,1)} %collective-permute-done.4, bf16[4096,576]{1,0:T(8,128)(2,1)S(1)} %bitcast.69), kind=kOutput, calls=%fused_computation.80 | convolution fusion | flops 1811939328 | bytes 8749056 | tf_op jit(solution)/shard_map/dot_general | solution.py:175
  236.2 4.5 %fusion.69 = f32[384,576]{1,0:T(8,128)S(1)} fusion(bf16[384,4096]{1,0:T(8,128)(2,1)} %collective-permute-done.13, bf16[4096,576]{1,0:T(8,128)(2,1)S(1)} %bitcast.67), kind=kOutput, calls=%fused_computation.84 | convolution fusion | flops 1811939328 | bytes 8749056 | tf_op jit(solution)/shard_map/dot_general | solution.py:175
  240.7 4.5 %fusion.68 = f32[384,576]{1,0:T(8,128)S(1)} fusion(bf16[384,4096]{1,0:T(8,128)(2,1)} %collective-permute-done.12, bf16[4096,576]{1,0:T(8,128)(2,1)S(1)} %bitcast.67), kind=kOutput, calls=%fused_computation.83 | convolution fusion | flops 1811939328 | bytes 8749056 | tf_op jit(solution)/shard_map/dot_general | solution.py:175
  245.3 3.4 %collective-permute-done.7 = bf16[192,4096]{1,0:T(8,128)(2,1)S(1)} collective-permute-done((bf16[192,4096]{1,0:T(8,128)(2,1)S(1)}, bf16[192,4096]{1,0:T(8,128)(2,1)S(1)}, u32[]{:S(2)}, u32[]{:S(2)}) %collective-permute-start.7) | collective-permute-done | bytes 1572896 | tf_op jit(solution)/shard_map/ppermute | solution.py:20
  248.7 2.7 fusion.7
  251.4 1.7 collective-permute-done.15
  253.1 1.8 collective-permute-done.14
  254.9 2.9 fusion.11
  257.8 0.6 fusion.2
  258.6 1.0 maximum_select_fusion
  259.9 0.3 fusion.19
  260.9 1.7 fusion.20
  262.6 4.7 %all-to-all-start.2 = ((bf16[16,96,576]{2,1,0:T(8,128)(2,1)}), bf16[16,96,576]{2,1,0:T(8,128)(2,1)}, u32[]{:S(2)}, u32[]{:S(2)}) async-start(bf16[16,96,576]{2,1,0:T(8,128)(2,1)} %bitcast.65), calls=%async_computation.2 | async-start | bytes 3932160 | tf_op jit(solution)/shard_map/all_to_all | solution.py:187
  267.3 7.5 %reshape.40 = bf16[256,9216]{1,0:T(8,128)(2,1)} reshape(bf16[128,2,9216]{2,1,0:T(2,128)(2,1)} %all-to-all-done.1) | data formatting | bytes 9437184 | tf_op jit(solution)/shard_map/reshape | solution.py:185
  274.8 4.7 %convolution_convert_fusion.1.query_term_ref.value_term_ref = bf16[96,9216]{1,0:T(8,128)(2,1)} fusion(bf16[256,9216]{1,0:T(8,128)(2,1)} %reshape.40, s32[96]{0:T(128)S(1)} %multiply_add_fusion), kind=kOutput, calls=%fused_computation.2 | convolution fusion | flops 453894144 | bytes 6488448 | tf_op jit(solution)/shard_map/dot_general | solution.py:186
  279.5 13.5 %all-to-all-done.2.plain_ref = bf16[16,96,576]{2,1,0:T(8,128)(2,1)} async-done(((bf16[16,96,576]{2,1,0:T(8,128)(2,1)}), bf16[16,96,576]{2,1,0:T(8,128)(2,1)}, u32[]{:S(2)}, u32[]{:S(2)}) %all-to-all-start.2) | async-done | bytes 1769504 | tf_op jit(solution)/shard_map/all_to_all | solution.py:187
  293.0 1.5 copy-done.2
  294.5 3.9 %shard_map.95 = (bf16[96,8192]{1,0:T(8,128)(2,1)}, bf16[96,1024]{1,0:T(8,128)(2,1)}) custom-call(bf16[16,96,576]{2,1,0:T(8,128)(2,1)} %all-to-all-done.2.plain_ref, bf16[96,9216]{1,0:T(8,128)(2,1)S(1)} %copy-done.2, bf16[96,9216]{1,0:T(8,128)(2,1)S(1)} %copy-done.2), custom_call_target="tpu_custom_call" | custom-call | flops 884736 | bytes 5308416 | tf_op jit(solution)/shard_map/pallas_call | solution.py:80
  (64 shorter events, 2.4 us)
Async XLA Ops:
  0.6 128.6 %copy-start = (bf16[2,64,8192]{2,1,0:T(8,128)(2,1)S(1)}, bf16[2,64,8192]{2,1,0:T(8,128)(2,1)}, u32[]{:S(2)}) copy-start(bf16[2,64,8192]{2,1,0:T(8,128)(2,1)} %param.14) | copy-start | bytes 6291460
  0.6 10.8 %copy-start.3 = (bf16[96,8192]{1,0:T(8,128)(2,1)S(1)}, bf16[96,8192]{1,0:T(8,128)(2,1)}, u32[]{:S(2)}) copy-start(bf16[96,8192]{1,0:T(8,128)(2,1)} %param.8) | copy-start | bytes 4718596
  0.7 10.5 %copy-start.10 = (s32[96,1]{0,1:T(1,128)S(1)}, s32[96,1]{0,1:T(1,128)}, u32[]{:S(2)}) copy-start(s32[96,1]{0,1:T(1,128)} %param.10) | copy-start | bytes 1156
  0.7 10.5 %copy-start.11 = (s32[96,1]{0,1:T(1,128)S(1)}, s32[96,1]{0,1:T(1,128)}, u32[]{:S(2)}) copy-start(s32[96,1]{0,1:T(1,128)} %param.9) | copy-start | bytes 1156
  4.1 38.7 %collective-permute-start = (bf16[96,4096]{1,0:T(8,128)(2,1)}, bf16[96,4096]{1,0:T(8,128)(2,1)}, u32[]{:S(2)}, u32[]{:S(2)}) collective-permute-start(bf16[96,4096]{1,0:T(8,128)(2,1)} %get-tuple-element.21), channel_id=1, source_target_pairs={{0,3},{1,0},{2,1},{3,2},{4,7},{5,4},{6,5},{7,6},{8,11},{9,8},{10,9... | collective-permute-start | bytes 2359304 | tf_op jit(solution)/shard_map/ppermute | solution.py:20
  8.1 31.6 %collective-permute-start.1 = (bf16[96,4096]{1,0:T(8,128)(2,1)}, bf16[96,4096]{1,0:T(8,128)(2,1)}, u32[]{:S(2)}, u32[]{:S(2)}) collective-permute-start(bf16[96,4096]{1,0:T(8,128)(2,1)} %get-tuple-element.21), channel_id=1, source_target_pairs={{0,1},{1,2},{2,3},{3,0},{4,5},{5,6},{6,7},{7,4},{8,9},{9,10},{10,1... | collective-permute-start | bytes 2359304 | tf_op jit(solution)/shard_map/ppermute | solution.py:20
  8.1 39.4 %collective-permute-start.8 = (bf16[96,4096]{1,0:T(8,128)(2,1)}, bf16[96,4096]{1,0:T(8,128)(2,1)}, u32[]{:S(2)}, u32[]{:S(2)}) collective-permute-start(bf16[96,4096]{1,0:T(8,128)(2,1)} %get-tuple-element.18), channel_id=1, source_target_pairs={{0,12},{1,13},{2,14},{3,15},{4,0},{5,1},{6,2},{7,3},{8,4},{9,5},{1... | collective-permute-start | bytes 2359304 | tf_op jit(solution)/shard_map/ppermute | solution.py:20
  11.1 34.8 %collective-permute-start.9 = (bf16[96,4096]{1,0:T(8,128)(2,1)}, bf16[96,4096]{1,0:T(8,128)(2,1)S(1)}, u32[]{:S(2)}, u32[]{:S(2)}) collective-permute-start(bf16[96,4096]{1,0:T(8,128)(2,1)} %get-tuple-element.18), channel_id=1, source_target_pairs={{0,4},{1,5},{2,6},{3,7},{4,8},{5,9},{6,10},{7,11},{8,12},{9,13},{1... | collective-permute-start | bytes 2359304 | tf_op jit(solution)/shard_map/ppermute | solution.py:20
  21.9 90.9 %all-to-all-start = ((bf16[128,2,8320]{2,1,0:T(2,128)(2,1)}), bf16[128,2,8320]{2,1,0:T(2,128)(2,1)}, u32[]{:S(2)}, u32[]{:S(2)}) async-start(bf16[128,2,8320]{2,1,0:T(2,128)(2,1)} %reshape.34), calls=%async_computation | async-start | bytes 8519680 | tf_op jit(solution)/shard_map/all_to_all | solution.py:135
  39.7 62.3 %copy-start.5 = (bf16[4096,576]{1,0:T(8,128)(2,1)}, bf16[4096,576]{1,0:T(8,128)(2,1)S(1)}, u32[]{:S(2)}) copy-start(bf16[4096,576]{1,0:T(8,128)(2,1)S(1)} %get-tuple-element.13) | copy-start | bytes 14155780
  39.7 67.7 %copy-start.4 = (bf16[4096,576]{1,0:T(8,128)(2,1)}, bf16[4096,576]{1,0:T(8,128)(2,1)S(1)}, u32[]{:S(2)}) copy-start(bf16[4096,576]{1,0:T(8,128)(2,1)S(1)} %get-tuple-element.12) | copy-start | bytes 14155780
  41.0 48.4 %collective-permute-start.2 = (bf16[48,4096]{1,0:T(8,128)(2,1)S(1)}, bf16[48,4096]{1,0:T(8,128)(2,1)S(1)}, u32[]{:S(2)}, u32[]{:S(2)}) collective-permute-start(bf16[48,4096]{1,0:T(8,128)(2,1)S(1)} %slice.117), channel_id=1, source_target_pairs={{0,1},{1,2},{2,3},{3,0},{4,5},{5,6},{6,7},{7,4},{8,9},{9,10},{10,1... | collective-permute-start | bytes 1179656 | tf_op jit(solution)/shard_map/ppermute | solution.py:20
  44.0 46.1 %collective-permute-start.3 = (bf16[48,4096]{1,0:T(8,128)(2,1)S(1)}, bf16[48,4096]{1,0:T(8,128)(2,1)S(1)}, u32[]{:S(2)}, u32[]{:S(2)}) collective-permute-start(bf16[48,4096]{1,0:T(8,128)(2,1)S(1)} %slice.118), channel_id=1, source_target_pairs={{0,3},{1,0},{2,1},{3,2},{4,7},{5,4},{6,5},{7,6},{8,11},{9,8},{10,9... | collective-permute-start | bytes 1179656 | tf_op jit(solution)/shard_map/ppermute | solution.py:20
  45.9 50.3 %collective-permute-start.10 = (bf16[48,4096]{1,0:T(8,128)(2,1)S(1)}, bf16[48,4096]{1,0:T(8,128)(2,1)S(1)}, u32[]{:S(2)}, u32[]{:S(2)}) collective-permute-start(bf16[48,4096]{1,0:T(8,128)(2,1)S(1)} %slice.123), channel_id=1, source_target_pairs={{0,4},{1,5},{2,6},{3,7},{4,8},{5,9},{6,10},{7,11},{8,12},{9,13},{1... | collective-permute-start | bytes 1179656 | tf_op jit(solution)/shard_map/ppermute | solution.py:20
  48.5 48.5 %collective-permute-start.11 = (bf16[48,4096]{1,0:T(8,128)(2,1)S(1)}, bf16[48,4096]{1,0:T(8,128)(2,1)S(1)}, u32[]{:S(2)}, u32[]{:S(2)}) collective-permute-start(bf16[48,4096]{1,0:T(8,128)(2,1)S(1)} %slice.124), channel_id=1, source_target_pairs={{0,12},{1,13},{2,14},{3,15},{4,0},{5,1},{6,2},{7,3},{8,4},{9,5},{1... | collective-permute-start | bytes 1179656 | tf_op jit(solution)/shard_map/ppermute | solution.py:20
  93.0 117.9 %collective-permute-start.5 = (bf16[384,4096]{1,0:T(8,128)(2,1)}, bf16[384,4096]{1,0:T(8,128)(2,1)}, u32[]{:S(2)}, u32[]{:S(2)}) collective-permute-start(bf16[384,4096]{1,0:T(8,128)(2,1)} %constant_dynamic-update-slice_fusion), channel_id=1, source_target_pairs={{0,4},{1,5},{2,6},{3,7},{4,8},{5,9},{6,10},{7,11},{8,12},{9,13},{1... | collective-permute-start | bytes 9437192 | tf_op jit(solution)/shard_map/ppermute | solution.py:20
  94.5 110.7 %collective-permute-start.4 = (bf16[384,4096]{1,0:T(8,128)(2,1)}, bf16[384,4096]{1,0:T(8,128)(2,1)}, u32[]{:S(2)}, u32[]{:S(2)}) collective-permute-start(bf16[384,4096]{1,0:T(8,128)(2,1)} %constant_dynamic-update-slice_fusion), channel_id=1, source_target_pairs={{0,12},{1,13},{2,14},{3,15},{4,0},{5,1},{6,2},{7,3},{8,4},{9,5},{1... | collective-permute-start | bytes 9437192 | tf_op jit(solution)/shard_map/ppermute | solution.py:20
  98.7 126.4 %collective-permute-start.13 = (bf16[384,4096]{1,0:T(8,128)(2,1)}, bf16[384,4096]{1,0:T(8,128)(2,1)}, u32[]{:S(2)}, u32[]{:S(2)}) collective-permute-start(bf16[384,4096]{1,0:T(8,128)(2,1)} %constant_dynamic-update-slice_fusion.5), channel_id=1, source_target_pairs={{0,1},{1,2},{2,3},{3,0},{4,5},{5,6},{6,7},{7,4},{8,9},{9,10},{10,1... | collective-permute-start | bytes 9437192 | tf_op jit(solution)/shard_map/ppermute | solution.py:20
  99.0 120.7 %collective-permute-start.12 = (bf16[384,4096]{1,0:T(8,128)(2,1)}, bf16[384,4096]{1,0:T(8,128)(2,1)}, u32[]{:S(2)}, u32[]{:S(2)}) collective-permute-start(bf16[384,4096]{1,0:T(8,128)(2,1)} %constant_dynamic-update-slice_fusion.5), channel_id=1, source_target_pairs={{0,3},{1,0},{2,1},{3,2},{4,7},{5,4},{6,5},{7,6},{8,11},{9,8},{10,9... | collective-permute-start | bytes 9437192 | tf_op jit(solution)/shard_map/ppermute | solution.py:20
  121.1 4.5 %copy-start.6 = (bf16[256,8320]{1,0:T(8,128)(2,1)S(1)}, bf16[256,8320]{1,0:T(8,128)(2,1)}, u32[]{:S(2)}) copy-start(bf16[256,8320]{1,0:T(8,128)(2,1)} %reshape.35) | copy-start | bytes 12779524
  125.7 3.2 %copy-start.9 = (bf16[2,64,1024]{2,1,0:T(8,128)(2,1)S(1)}, bf16[2,64,1024]{2,1,0:T(8,128)(2,1)}, u32[]{:S(2)}) copy-start(bf16[2,64,1024]{2,1,0:T(8,128)(2,1)} %param.15) | copy-start | bytes 786436
  140.5 86.6 %slice-start.2 = ((s8[5242880]{0:T(1024)(128)(4,1)}), s8[1048576]{0:T(1024)(128)(4,1)S(1)}, s32[]{:S(2)}) async-start(s8[5242880]{0:T(1024)(128)(4,1)} %bitcast.68), calls=%async_computation.5 | async-start | bytes 2097152
  140.5 122.1 %all-to-all-start.1 = ((bf16[128,2,9216]{2,1,0:T(2,128)(2,1)}), bf16[128,2,9216]{2,1,0:T(2,128)(2,1)}, u32[]{:S(2)}, u32[]{:S(2)}) async-start(bf16[128,2,9216]{2,1,0:T(2,128)(2,1)} %reshape.38), calls=%async_computation.1 | async-start | bytes 9437184 | tf_op jit(solution)/shard_map/all_to_all | solution.py:146
  146.9 80.3 %slice-start.3 = ((s8[5242880]{0:T(1024)(128)(4,1)}), s8[4194304]{0:T(1024)(128)(4,1)S(1)}, s32[]{:S(2)}) async-start(s8[5242880]{0:T(1024)(128)(4,1)} %bitcast.68), calls=%async_computation.6 | async-start | bytes 8388608
  206.8 41.9 %collective-permute-start.7 = (bf16[192,4096]{1,0:T(8,128)(2,1)S(1)}, bf16[192,4096]{1,0:T(8,128)(2,1)S(1)}, u32[]{:S(2)}, u32[]{:S(2)}) collective-permute-start(bf16[192,4096]{1,0:T(8,128)(2,1)S(1)} %slice.122), channel_id=1, source_target_pairs={{0,12},{1,13},{2,14},{3,15},{4,0},{5,1},{6,2},{7,3},{8,4},{9,5},{1... | collective-permute-start | bytes 4718600 | tf_op jit(solution)/shard_map/ppermute | solution.py:20
  212.4 36.3 %collective-permute-start.6 = (bf16[192,4096]{1,0:T(8,128)(2,1)S(1)}, bf16[192,4096]{1,0:T(8,128)(2,1)S(1)}, u32[]{:S(2)}, u32[]{:S(2)}) collective-permute-start(bf16[192,4096]{1,0:T(8,128)(2,1)S(1)} %slice.121), channel_id=1, source_target_pairs={{0,4},{1,5},{2,6},{3,7},{4,8},{5,9},{6,10},{7,11},{8,12},{9,13},{1... | collective-permute-start | bytes 4718600 | tf_op jit(solution)/shard_map/ppermute | solution.py:20
  221.2 31.9 %collective-permute-start.15 = (bf16[192,4096]{1,0:T(8,128)(2,1)S(1)}, bf16[192,4096]{1,0:T(8,128)(2,1)S(1)}, u32[]{:S(2)}, u32[]{:S(2)}) collective-permute-start(bf16[192,4096]{1,0:T(8,128)(2,1)S(1)} %slice.126), channel_id=1, source_target_pairs={{0,3},{1,0},{2,1},{3,2},{4,7},{5,4},{6,5},{7,6},{8,11},{9,8},{10,9... | collective-permute-start | bytes 4718600 | tf_op jit(solution)/shard_map/ppermute | solution.py:20
  225.1 11.0 %slice-start = ((s8[5242880]{0:T(1024)(128)(4,1)}), s8[4194304]{0:T(1024)(128)(4,1)S(1)}, s32[]{:S(2)}) async-start(s8[5242880]{0:T(1024)(128)(4,1)} %bitcast.66), calls=%async_computation.3 | async-start | bytes 8388608
  226.9 9.3 %slice-start.1 = ((s8[5242880]{0:T(1024)(128)(4,1)}), s8[1048576]{0:T(1024)(128)(4,1)S(1)}, s32[]{:S(2)}) async-start(s8[5242880]{0:T(1024)(128)(4,1)} %bitcast.66), calls=%async_computation.4 | async-start | bytes 2097152
  226.9 28.1 %collective-permute-start.14 = (bf16[192,4096]{1,0:T(8,128)(2,1)S(1)}, bf16[192,4096]{1,0:T(8,128)(2,1)S(1)}, u32[]{:S(2)}, u32[]{:S(2)}) collective-permute-start(bf16[192,4096]{1,0:T(8,128)(2,1)S(1)} %slice.125), channel_id=1, source_target_pairs={{0,1},{1,2},{2,3},{3,0},{4,5},{5,6},{6,7},{7,4},{8,9},{9,10},{10,1... | collective-permute-start | bytes 4718600 | tf_op jit(solution)/shard_map/ppermute | solution.py:20
  251.4 6.4 %copy-start.7 = (f32[384,576]{1,0:T(8,128)S(1)}, f32[384,576]{1,0:T(8,128)}, u32[]{:S(2)}) copy-start(f32[384,576]{1,0:T(8,128)} %fusion.64) | copy-start | bytes 2654212
  251.4 6.4 %copy-start.8 = (f32[384,576]{1,0:T(8,128)S(1)}, f32[384,576]{1,0:T(8,128)}, u32[]{:S(2)}) copy-start(f32[384,576]{1,0:T(8,128)} %fusion.67) | copy-start | bytes 2654212
  262.6 30.4 %all-to-all-start.2 = ((bf16[16,96,576]{2,1,0:T(8,128)(2,1)}), bf16[16,96,576]{2,1,0:T(8,128)(2,1)}, u32[]{:S(2)}, u32[]{:S(2)}) async-start(bf16[16,96,576]{2,1,0:T(8,128)(2,1)} %bitcast.65), calls=%async_computation.2 | async-start | bytes 3932160 | tf_op jit(solution)/shard_map/all_to_all | solution.py:187
  274.8 23.5 %copy-start.1 = (bf16[2,64,8192]{2,1,0:T(8,128)(2,1)S(1)}, bf16[2,64,8192]{2,1,0:T(8,128)(2,1)}, u32[]{:S(2)}) copy-start(bf16[2,64,8192]{2,1,0:T(8,128)(2,1)} %param.14) | copy-start | bytes 6291460
  293.0 1.5 copy-start.2
